TPU v7x, 32 devices: a whole 2x2x4 slice. The times are simulated.
32 devices in a mesh: ctx: 4 (over y, x), fsdp: 8 (over z, core).
Axes of the slice: x: 2, y: 2, z: 4, core: 2. Of those that a mesh axis runs over, the one named last changes fastest.
Arguments:
- activations: bfloat16 [8, 1536, 768], P('fsdp', 'ctx'), may hold values from -6 to 6
- cotangent: bfloat16 [8, 1536, 768], P('fsdp', 'ctx'), may hold values from -6 to 6
- doc_start: int32 [8, 1536], P('fsdp', 'ctx'), may hold values from 0 to 1535, as said below
- deal: int32 [4], replicated, may hold values from 0 to 3, as said below
- attend_in: bfloat16 [2, 768, 2304], P(None, 'fsdp'), may hold values from -0.21875 to 0.21875
- query_bias: bfloat16 [2, 768], P(None, 'fsdp'), may hold values from -3 to 3
- value_bias: bfloat16 [2, 768], P(None, 'fsdp'), may hold values from -3 to 3
- attend_out: bfloat16 [2, 768, 768], P(None, 'fsdp'), may hold values from -1.25 to 1.25
- attend_bias: bfloat16 [2, 768], P(None, 'fsdp'), may hold values from -3 to 3
- first_gain: bfloat16 [2, 768], P(None, 'fsdp'), may hold values from 0.099609375 to 1.8984375
- first_shift: bfloat16 [2, 768], P(None, 'fsdp'), may hold values from -3 to 3
- expand_proj: bfloat16 [2, 768, 3072], P(None, 'fsdp'), may hold values from -0.21875 to 0.21875
- expand_bias: bfloat16 [2, 3072], P(None, 'fsdp'), may hold values from -3 to 3
- reduce_proj: bfloat16 [2, 3072, 768], P(None, 'fsdp'), may hold values from -0.109375 to 0.109375
- reduce_bias: bfloat16 [2, 768], P(None, 'fsdp'), may hold values from -3 to 3
- second_gain: bfloat16 [2, 768], P(None, 'fsdp'), may hold values from 0.099609375 to 1.8984375
- second_shift: bfloat16 [2, 768], P(None, 'fsdp'), may hold values from -3 to 3
Outputs:
- out_act: bfloat16 [8, 1536, 768], P('fsdp', 'ctx')
- in_grad: float32 [8, 1536, 768], P('fsdp', 'ctx')
- attend_in_grad: float32 [2, 768, 2304], P(None, 'fsdp')
- query_bias_grad: float32 [2, 768], P(None, 'fsdp')
- value_bias_grad: float32 [2, 768], P(None, 'fsdp')
- attend_out_grad: float32 [2, 768, 768], P(None, 'fsdp')
- attend_bias_grad: float32 [2, 768], P(None, 'fsdp')
- first_gain_grad: float32 [2, 768], P(None, 'fsdp')
- first_shift_grad: float32 [2, 768], P(None, 'fsdp')
- expand_proj_grad: float32 [2, 768, 3072], P(None, 'fsdp')
- expand_bias_grad: float32 [2, 3072], P(None, 'fsdp')
- reduce_proj_grad: float32 [2, 3072, 768], P(None, 'fsdp')
- reduce_bias_grad: float32 [2, 768], P(None, 'fsdp')
- second_gain_grad: float32 [2, 768], P(None, 'fsdp')
- second_shift_grad: float32 [2, 768], P(None, 'fsdp')
Inputs may be any that keep to these rules, and one draw needn't show every extreme that they name: `doc_start`: rows of one document share the position where it begins; each sequence's first document begins at 0 and covers its first half or more; the last position of a sequence is a document of its own. A permutation of 0 to 3; index c of ctx holds blocks deal[c] and 7 - deal[c].
All inputs are finite; a program needn't handle non-finite values.
Results may differ from a plain program's by a relative error of at most 0.022.
Values may be sent and summed in bfloat16 or wider, within the bound.
No kernel may reach another device: no remote copies, remote signals or barrier semaphores. Data moves between devices by JAX's collectives and lax.ppermute only.
A program may use at most 192 MiB of HBM per device.

v0:
```python
import jax
import jax.numpy as jnp
from jax import lax
from jax.sharding import PartitionSpec as P

HEADS = 12
HEAD_DIM = 64
LAYERS = 2
BLK = 192


norm_eps = 1e-05


def for_sending(x):
    return jax.tree.map(lambda a: a.astype(jnp.bfloat16) if a.dtype == jnp.float32 else a, x)


def layer_norm(values, gain, shift):
    centre = values - jnp.mean(values, axis=-1, keepdims=True)
    spread = jnp.mean(centre * centre, axis=-1, keepdims=True)
    return centre * lax.rsqrt(spread + norm_eps) * gain + shift


def gelu_exact(inputs):
    return 0.5 * inputs * (1.0 + jax.scipy.special.erf(inputs * 0.7071067811865476))


def key_positions(deal):
    pairs = deal.shape[0]
    offsets = jnp.arange(BLK, dtype=jnp.int32)
    first = deal[:, None] * BLK + offsets[None, :]
    second = (2 * pairs - 1 - deal)[:, None] * BLK + offsets[None, :]
    return jnp.concatenate([first, second], axis=1).reshape(-1)


def split_heads(matrix):
    return matrix.reshape(matrix.shape[0], HEADS, HEAD_DIM).transpose(1, 0, 2)


def join_heads(stacked):
    return stacked.transpose(1, 0, 2).reshape(stacked.shape[1], HEADS * HEAD_DIM)


def attend_forward(queries, keys_full, values_full, allowed):

    def one_head(items):
        head_q, head_k, head_v = items
        scores = jnp.einsum(
            "qd,kd->qk", head_q, head_k, preferred_element_type=jnp.float32
        ) * HEAD_DIM ** (-0.5)
        scores = jnp.where(allowed, scores, -1e30)
        top = jnp.max(scores, axis=-1, keepdims=True)
        weights = jnp.exp(scores - top)
        total = jnp.sum(weights, axis=-1, keepdims=True)
        probs = (weights / total).astype(jnp.bfloat16)
        output = jnp.einsum("qk,kd->qd", probs, head_v, preferred_element_type=jnp.float32)
        return (output, top[:, 0] + jnp.log(total[:, 0]))

    outputs, log_totals = lax.map(
        one_head, (split_heads(queries), split_heads(keys_full), split_heads(values_full))
    )
    return (join_heads(outputs), log_totals)


def attend_backward(queries, keys_full, values_full, log_totals, grad_context, allowed):

    def one_head(items):
        head_q, head_k, head_v, head_lse, head_grad = items
        scores = jnp.einsum(
            "qd,kd->qk", head_q, head_k, preferred_element_type=jnp.float32
        ) * HEAD_DIM ** (-0.5)
        scores = jnp.where(allowed, scores, -1e30)
        probs = jnp.exp(scores - head_lse[:, None])
        grad_probs = jnp.einsum("qd,kd->qk", head_grad, head_v, preferred_element_type=jnp.float32)
        inner_sum = jnp.sum(probs * grad_probs, axis=-1, keepdims=True)
        grad_scores = (probs * (grad_probs - inner_sum)).astype(jnp.bfloat16)
        grad_q = jnp.einsum(
            "qk,kd->qd", grad_scores, head_k, preferred_element_type=jnp.float32
        ) * HEAD_DIM ** (-0.5)
        grad_k = jnp.einsum(
            "qk,qd->kd", grad_scores, head_q, preferred_element_type=jnp.float32
        ) * HEAD_DIM ** (-0.5)
        grad_v = jnp.einsum(
            "qk,qd->kd", probs.astype(jnp.bfloat16), head_grad, preferred_element_type=jnp.float32
        )
        return (grad_q, grad_k, grad_v)

    grads = lax.map(
        one_head,
        (
            split_heads(queries),
            split_heads(keys_full),
            split_heads(values_full),
            log_totals,
            split_heads(grad_context),
        ),
    )
    return (join_heads(grads[0]), join_heads(grads[1]), join_heads(grads[2]))


def forward_layer(hidden, weights, allowed):
    (
        attend_in,
        query_bias,
        value_bias,
        attend_out,
        attend_bias,
        first_gain,
        first_shift,
        expand_proj,
        expand_bias,
        reduce_proj,
        reduce_bias,
        second_gain,
        second_shift,
    ) = weights
    width = hidden.shape[1]
    low_hidden = hidden.astype(jnp.bfloat16)
    projected = jnp.dot(low_hidden, attend_in, preferred_element_type=jnp.float32)
    queries = (projected[:, :width] + query_bias.astype(jnp.float32)).astype(jnp.bfloat16)
    keys_own = projected[:, width : 2 * width].astype(jnp.bfloat16)
    values_own = (projected[:, 2 * width :] + value_bias.astype(jnp.float32)).astype(jnp.bfloat16)
    keys_full, values_full = (
        lax.all_gather(keys_own, "ctx", axis=0, tiled=True),
        lax.all_gather(values_own, "ctx", axis=0, tiled=True),
    )
    context, log_totals = attend_forward(queries, keys_full, values_full, allowed)
    low_context = context.astype(jnp.bfloat16)
    branch = jnp.dot(
        low_context, attend_out, preferred_element_type=jnp.float32
    ) + attend_bias.astype(jnp.float32)
    first_sum = hidden + branch
    normed = layer_norm(first_sum, first_gain.astype(jnp.float32), first_shift.astype(jnp.float32))
    low_normed = normed.astype(jnp.bfloat16)
    inner_pre = jnp.dot(
        low_normed, expand_proj, preferred_element_type=jnp.float32
    ) + expand_bias.astype(jnp.float32)
    active = gelu_exact(inner_pre).astype(jnp.bfloat16)
    output_branch = jnp.dot(
        active, reduce_proj, preferred_element_type=jnp.float32
    ) + reduce_bias.astype(jnp.float32)
    second_sum = normed + output_branch
    output = layer_norm(
        second_sum, second_gain.astype(jnp.float32), second_shift.astype(jnp.float32)
    )
    saved = (
        low_hidden,
        queries,
        keys_full,
        values_full,
        log_totals,
        low_context,
        first_sum,
        low_normed,
        inner_pre,
        active,
        second_sum,
    )
    return (output, saved)


def column_sum(matrix):
    return jnp.sum(matrix.astype(jnp.float32), axis=0)


def backward_layer(grad_hidden, weights, saved, allowed):
    (
        attend_in,
        query_bias,
        value_bias,
        attend_out,
        attend_bias,
        first_gain,
        first_shift,
        expand_proj,
        expand_bias,
        reduce_proj,
        reduce_bias,
        second_gain,
        second_shift,
    ) = weights
    (
        low_hidden,
        queries,
        keys_full,
        values_full,
        log_totals,
        low_context,
        first_sum,
        low_normed,
        inner_pre,
        active,
        second_sum,
    ) = saved
    width = low_hidden.shape[1]
    second_pull = jax.vjp(
        layer_norm, second_sum, second_gain.astype(jnp.float32), second_shift.astype(jnp.float32)
    )[1]
    grad_second_sum, grad_second_gain, grad_second_shift = second_pull(grad_hidden)
    grad_branch = grad_second_sum.astype(jnp.bfloat16)
    grad_reduce_bias = column_sum(grad_branch)
    grad_reduce = jnp.einsum("tf,td->fd", active, grad_branch, preferred_element_type=jnp.float32)
    grad_active = jnp.einsum(
        "td,fd->tf", grad_branch, reduce_proj, preferred_element_type=jnp.float32
    )
    gelu_pull = jax.vjp(gelu_exact, inner_pre)[1]
    grad_inner = gelu_pull(grad_active)[0].astype(jnp.bfloat16)
    grad_expand_bias = column_sum(grad_inner)
    grad_expand = jnp.einsum(
        "td,tf->df", low_normed, grad_inner, preferred_element_type=jnp.float32
    )
    grad_normed = grad_second_sum + jnp.einsum(
        "tf,df->td", grad_inner, expand_proj, preferred_element_type=jnp.float32
    )
    first_pull = jax.vjp(
        layer_norm, first_sum, first_gain.astype(jnp.float32), first_shift.astype(jnp.float32)
    )[1]
    grad_first_sum, grad_first_gain, grad_first_shift = first_pull(grad_normed)
    grad_attn = grad_first_sum.astype(jnp.bfloat16)
    grad_attend_bias = column_sum(grad_attn)
    grad_attend_out = jnp.einsum(
        "td,te->de", low_context, grad_attn, preferred_element_type=jnp.float32
    )
    grad_context = jnp.einsum(
        "te,de->td", grad_attn, attend_out, preferred_element_type=jnp.float32
    ).astype(jnp.bfloat16)
    grad_queries, grad_keys_full, grad_values_full = attend_backward(
        queries, keys_full, values_full, log_totals, grad_context, allowed
    )
    grad_keys, grad_values = (
        lax.psum_scatter(
            grad_keys_full.astype(jnp.bfloat16), "ctx", scatter_dimension=0, tiled=True
        ).astype(jnp.float32),
        lax.psum_scatter(
            grad_values_full.astype(jnp.bfloat16), "ctx", scatter_dimension=0, tiled=True
        ).astype(jnp.float32),
    )
    grad_proj = jnp.concatenate(
        [
            grad_queries.astype(jnp.bfloat16),
            grad_keys.astype(jnp.bfloat16),
            grad_values.astype(jnp.bfloat16),
        ],
        axis=1,
    )
    grad_query_bias = column_sum(grad_proj[:, :width])
    grad_value_bias = column_sum(grad_proj[:, 2 * width :])
    grad_attend_in = jnp.einsum(
        "td,te->de", low_hidden, grad_proj, preferred_element_type=jnp.float32
    )
    grad_input = grad_first_sum + jnp.einsum(
        "te,de->td", grad_proj, attend_in, preferred_element_type=jnp.float32
    )
    grads = (
        grad_attend_in,
        grad_query_bias,
        grad_value_bias,
        grad_attend_out,
        grad_attend_bias,
        grad_first_gain,
        grad_first_shift,
        grad_expand,
        grad_expand_bias,
        grad_reduce,
        grad_reduce_bias,
        grad_second_gain,
        grad_second_shift,
    )
    return (grad_input, grads)


def reduce_grads(grads):
    shards = (
        lax.psum_scatter(
            grads[0].astype(jnp.bfloat16), "fsdp", scatter_dimension=0, tiled=True
        ).astype(jnp.float32),
        lax.psum_scatter(
            grads[1].astype(jnp.bfloat16), "fsdp", scatter_dimension=0, tiled=True
        ).astype(jnp.float32),
        lax.psum_scatter(
            grads[2].astype(jnp.bfloat16), "fsdp", scatter_dimension=0, tiled=True
        ).astype(jnp.float32),
        lax.psum_scatter(
            grads[3].astype(jnp.bfloat16), "fsdp", scatter_dimension=0, tiled=True
        ).astype(jnp.float32),
        lax.psum_scatter(
            grads[4].astype(jnp.bfloat16), "fsdp", scatter_dimension=0, tiled=True
        ).astype(jnp.float32),
        lax.psum_scatter(
            grads[5].astype(jnp.bfloat16), "fsdp", scatter_dimension=0, tiled=True
        ).astype(jnp.float32),
        lax.psum_scatter(
            grads[6].astype(jnp.bfloat16), "fsdp", scatter_dimension=0, tiled=True
        ).astype(jnp.float32),
        lax.psum_scatter(
            grads[7].astype(jnp.bfloat16), "fsdp", scatter_dimension=0, tiled=True
        ).astype(jnp.float32),
        lax.psum_scatter(
            grads[8].astype(jnp.bfloat16), "fsdp", scatter_dimension=0, tiled=True
        ).astype(jnp.float32),
        lax.psum_scatter(
            grads[9].astype(jnp.bfloat16), "fsdp", scatter_dimension=0, tiled=True
        ).astype(jnp.float32),
        lax.psum_scatter(
            grads[10].astype(jnp.bfloat16), "fsdp", scatter_dimension=0, tiled=True
        ).astype(jnp.float32),
        lax.psum_scatter(
            grads[11].astype(jnp.bfloat16), "fsdp", scatter_dimension=0, tiled=True
        ).astype(jnp.float32),
        lax.psum_scatter(
            grads[12].astype(jnp.bfloat16), "fsdp", scatter_dimension=0, tiled=True
        ).astype(jnp.float32),
    )
    return (
        lax.psum(shards[0].astype(jnp.bfloat16), "ctx").astype(jnp.float32),
        lax.psum(shards[1].astype(jnp.bfloat16), "ctx").astype(jnp.float32),
        lax.psum(shards[2].astype(jnp.bfloat16), "ctx").astype(jnp.float32),
        lax.psum(shards[3].astype(jnp.bfloat16), "ctx").astype(jnp.float32),
        lax.psum(shards[4].astype(jnp.bfloat16), "ctx").astype(jnp.float32),
        lax.psum(shards[5].astype(jnp.bfloat16), "ctx").astype(jnp.float32),
        lax.psum(shards[6].astype(jnp.bfloat16), "ctx").astype(jnp.float32),
        lax.psum(shards[7].astype(jnp.bfloat16), "ctx").astype(jnp.float32),
        lax.psum(shards[8].astype(jnp.bfloat16), "ctx").astype(jnp.float32),
        lax.psum(shards[9].astype(jnp.bfloat16), "ctx").astype(jnp.float32),
        lax.psum(shards[10].astype(jnp.bfloat16), "ctx").astype(jnp.float32),
        lax.psum(shards[11].astype(jnp.bfloat16), "ctx").astype(jnp.float32),
        lax.psum(shards[12].astype(jnp.bfloat16), "ctx").astype(jnp.float32),
    )


def layer_slices(sharded, layer_index):
    return tuple((tensor[layer_index] for tensor in sharded))


def on_device(
    activations,
    cotangent,
    doc_start,
    deal,
    attend_in,
    query_bias,
    value_bias,
    attend_out,
    attend_bias,
    first_gain,
    first_shift,
    expand_proj,
    expand_bias,
    reduce_proj,
    reduce_bias,
    second_gain,
    second_shift,
):
    sharded = (
        attend_in,
        query_bias,
        value_bias,
        attend_out,
        attend_bias,
        first_gain,
        first_shift,
        expand_proj,
        expand_bias,
        reduce_proj,
        reduce_bias,
        second_gain,
        second_shift,
    )
    row_count = activations.shape[1]
    positions = key_positions(deal)
    own_rank = lax.axis_index("ctx")
    own_positions = lax.dynamic_slice_in_dim(positions, own_rank * row_count, row_count)
    own_starts = doc_start[0]
    key_starts = lax.all_gather(own_starts, "ctx", axis=0, tiled=True)
    allowed = (positions[None, :] <= own_positions[:, None]) & (
        key_starts[None, :] == own_starts[:, None]
    )
    hidden = activations[0].astype(jnp.float32)
    kept_weights = []
    kept_saved = []
    for layer_index in range(LAYERS):
        weights = lax.all_gather(
            for_sending(layer_slices(sharded, layer_index)), "fsdp", axis=0, tiled=True
        )
        hidden, saved = forward_layer(hidden, weights, allowed)
        kept_weights.append(weights)
        kept_saved.append(saved)
    out_act = hidden.astype(jnp.bfloat16)[None]
    grad_hidden = cotangent[0].astype(jnp.float32)
    reduced = [None] * LAYERS
    for layer_index in reversed(range(LAYERS)):
        weights = lax.all_gather(
            for_sending(layer_slices(sharded, layer_index)), "fsdp", axis=0, tiled=True
        )
        grad_hidden, grads = backward_layer(grad_hidden, weights, kept_saved[layer_index], allowed)
        reduced[layer_index] = reduce_grads(grads)
    stacked = [
        jnp.stack([reduced[layer_index][member] for layer_index in range(LAYERS)])
        for member in range(13)
    ]
    return (
        out_act,
        grad_hidden[None],
        stacked[0],
        stacked[1],
        stacked[2],
        stacked[3],
        stacked[4],
        stacked[5],
        stacked[6],
        stacked[7],
        stacked[8],
        stacked[9],
        stacked[10],
        stacked[11],
        stacked[12],
    )


def solution(mesh):
    placed = (
        P("fsdp", "ctx", None),
        P("fsdp", "ctx", None),
        P("fsdp", "ctx"),
        P(),
        P(None, "fsdp", None),
        P(None, "fsdp"),
        P(None, "fsdp"),
        P(None, "fsdp", None),
        P(None, "fsdp"),
        P(None, "fsdp"),
        P(None, "fsdp"),
        P(None, "fsdp", None),
        P(None, "fsdp"),
        P(None, "fsdp", None),
        P(None, "fsdp"),
        P(None, "fsdp"),
        P(None, "fsdp"),
    )
    return jax.shard_map(
        on_device,
        mesh=mesh,
        in_specs=placed,
        out_specs=(
            P("fsdp", "ctx", None),
            P("fsdp", "ctx", None),
            P(None, "fsdp", None),
            P(None, "fsdp"),
            P(None, "fsdp"),
            P(None, "fsdp", None),
            P(None, "fsdp"),
            P(None, "fsdp"),
            P(None, "fsdp"),
            P(None, "fsdp", None),
            P(None, "fsdp"),
            P(None, "fsdp", None),
            P(None, "fsdp"),
            P(None, "fsdp"),
            P(None, "fsdp"),
        ),
        check_vma=False,
    )
```

profile of v0, /device:TPU:1, one launch (start us, length us, event | category | flops | bytes accessed | tf_op | source)
XLA Modules:
  0.0 1474.6 jit_solution(12362441199929390381)
XLA Ops:
  26.6 28.4 %all-reduce.35 = (bf16[768]{0:T(1024)(128)(2,1)S(1)}, bf16[768]{0:T(1024)(128)(2,1)S(1)}, bf16[768]{0:T(1024)(128)(2,1)S(1)}, bf16[768]{0:T(1024)(128)(2,1)S(1)}...) all-reduce(bf16[768]{0:T(1024)(128)(2,1)} %dynamic-update-slice, ...), channel_id=3, replica_groups=mesh['ctx'=4,'fsdp'=8] {'fsdp'}, use_global_device_ids=true, to_apply=%add | all-reduce | flops 11520 | bytes 46080
  76.7 18.9 %all-gather.9 = bf16[1,3072]{1,0:T(2,128)(2,1)S(1)} all-gather(bf16[1,384]{1,0:T(2,128)(2,1)S(1)} %get-tuple-element.661), channel_id=11, replica_groups=mesh['ctx'=4,'fsdp'=8] {'fsdp'}, dimensions={1}, use_global_device_ids=true | all-gather | bytes 6912 | tf_op jit(solution)/shard_map/all_gather | solution.py:383
  107.9 31.9 %all-gather.40.cloned.1.call-done = bf16[1536,768]{1,0:T(8,128)(2,1)} async-done(((bf16[384,768]{1,0:T(8,128)(2,1)}), bf16[1536,768]{1,0:T(8,128)(2,1)}) %all-gather.40.cloned.1.call-update) | async-done | bytes 2359312 | tf_op jit(solution)/shard_map/all_gather | solution.py:125
  148.1 70.6 %while.56 = (s32[]{:T(128)}, bf16[12,384,64]{1,2,0:T(8,128)(2,1)}, f32[12,384]{1,0:T(8,128)}, bf16[12,384,64]{2,1,0:T(8,128)(2,1)S(1)}, bf16[12,1536,64]{2,1,0:T...) while((s32[]{:T(128)}, bf16[12,384,64]{1,2,0:T(8,128)(2,1)}, ...), condition=%wide.region_3.4_spmd.clone, body=%wide.region_0.3_spmd.clone.sunk | while | flops 157482624 | bytes 8114353 | solution.py:60
  223.3 6.8 multiply_convert_fusion.3
  230.1 41.0 %all-gather.54.cloned.1.call-done = bf16[1,3072,768]{2,1,0:T(8,128)(2,1)} async-done(((bf16[1,384,768]{2,1,0:T(8,128)(2,1)}), bf16[1,3072,768]{2,1,0:T(8,128)(2,1)}) %all-gather.54.cloned.1.call-update) | async-done | bytes 4718608 | tf_op jit(solution)/shard_map/all_gather | solution.py:383
  276.7 36.5 %all-gather.56.cloned.1.call-done = bf16[1,768,2304]{2,1,0:T(8,128)(2,1)} async-done(((bf16[1,96,2304]{2,1,0:T(8,128)(2,1)}), bf16[1,768,2304]{2,1,0:T(8,128)(2,1)}) %all-gather.56.cloned.1.call-update) | async-done | bytes 3538960 | tf_op jit(solution)/shard_map/all_gather | solution.py:383
  324.9 13.3 all-gather.22
  341.1 14.0 all-gather.46.cloned.1.call-done
  361.9 33.1 %all-gather.44.cloned.1.call-done = bf16[1536,768]{1,0:T(8,128)(2,1)} async-done(((bf16[384,768]{1,0:T(8,128)(2,1)}), bf16[1536,768]{1,0:T(8,128)(2,1)}) %all-gather.44.cloned.1.call-update) | async-done | bytes 2359312 | tf_op jit(solution)/shard_map/all_gather | solution.py:125
  403.3 71.0 %while.57 = (s32[]{:T(128)}, bf16[12,384,64]{1,2,0:T(8,128)(2,1)}, f32[12,384]{1,0:T(8,128)}, bf16[12,384,64]{2,1,0:T(8,128)(2,1)}, bf16[12,1536,64]{2,1,0:T(8,1...) while((s32[]{:T(128)}, bf16[12,384,64]{1,2,0:T(8,128)(2,1)}, ...), condition=%wide.region_11.12_spmd.clone, body=%wide.region_8.11_spmd.clone.sunk | while | flops 157482624 | bytes 8113841 | solution.py:60
  477.0 6.9 multiply_convert_fusion.2
  483.9 41.5 %all-gather.62.cloned.1.call-done = bf16[1,3072,768]{2,1,0:T(8,128)(2,1)} async-done(((bf16[1,384,768]{2,1,0:T(8,128)(2,1)}), bf16[1,3072,768]{2,1,0:T(8,128)(2,1)}) %all-gather.62.cloned.1.call-update) | async-done | bytes 4718608 | tf_op jit(solution)/shard_map/all_gather | solution.py:383
  549.8 119.0 %while.58 = (s32[]{:T(128)}, bf16[12,384,64]{1,2,0:T(8,128)(2,1)}, bf16[12,1536,64]{1,2,0:T(8,128)(2,1)S(1)}, bf16[12,1536,64]{1,2,0:T(8,128)(2,1)}, bf16[12,384...) while((s32[]{:T(128)}, bf16[12,384,64]{1,2,0:T(8,128)(2,1)}, ...), condition=%wide.region_22.23_spmd.clone, body=%wide.region_20.22_spmd.clone.sunk | while | flops 384687744 | bytes 20093092 | solution.py:89
  675.6 31.7 %reduce-scatter.37.cloned.1.call-done = bf16[384,768]{1,0:T(8,128)(2,1)} async-done(((bf16[1536,768]{1,0:T(8,128)(2,1)}), bf16[384,768]{1,0:T(8,128)(2,1)}) %reduce-scatter.37.cloned.1.call-update) | async-done | bytes 589840
  709.4 38.2 %reduce-scatter.39.cloned.1.call-done = bf16[384,768]{1,0:T(8,128)(2,1)} async-done(((bf16[1536,768]{1,0:T(8,128)(2,1)}), bf16[384,768]{1,0:T(8,128)(2,1)}) %reduce-scatter.39.cloned.1.call-update) | async-done | bytes 589840
  756.3 7.3 fusion.211
  774.3 119.0 %while.59 = (s32[]{:T(128)}, bf16[12,384,64]{1,2,0:T(8,128)(2,1)}, bf16[12,1536,64]{1,2,0:T(8,128)(2,1)S(1)}, bf16[12,1536,64]{1,2,0:T(8,128)(2,1)}, bf16[12,384...) while((s32[]{:T(128)}, bf16[12,384,64]{1,2,0:T(8,128)(2,1)}, ...), condition=%wide.region_31.32_spmd.clone, body=%wide.region_29.31_spmd.clone.sunk | while | flops 384687744 | bytes 20093092 | solution.py:89
  907.1 26.2 %reduce-scatter.41.cloned.1.call-done = bf16[384,768]{1,0:T(8,128)(2,1)} async-done(((bf16[1536,768]{1,0:T(8,128)(2,1)}), bf16[384,768]{1,0:T(8,128)(2,1)}) %reduce-scatter.41.cloned.1.call-update) | async-done | bytes 589840
  934.7 39.0 %reduce-scatter.43.cloned.1.call-done = bf16[384,768]{1,0:T(8,128)(2,1)} async-done(((bf16[1536,768]{1,0:T(8,128)(2,1)}), bf16[384,768]{1,0:T(8,128)(2,1)}) %reduce-scatter.43.cloned.1.call-update) | async-done | bytes 589840
  991.0 6.5 convolution_convert_fusion
  1013.7 6.4 convolution_convert_fusion.1
  1025.9 27.6 %all-reduce.34 = (bf16[768]{0:T(1024)(128)(2,1)}, bf16[768]{0:T(1024)(128)(2,1)}, bf16[768]{0:T(1024)(128)(2,1)}, bf16[768]{0:T(1024)(128)(2,1)}, bf16[768]{0:T(...) all-reduce(bf16[768]{0:T(1024)(128)(2,1)S(1)} %dynamic-update-slice, ...), channel_id=28, replica_groups=mesh['ctx'=4,'fsdp'=8] {'fsdp'}, use_global_device_ids=true, to_apply=%add.15 | all-reduce | flops 19200 | bytes 76800
  1055.6 7.7 reduce-scatter.45.cloned.1.call-done
  1065.4 31.0 %reduce-scatter.27.cloned.1.call-done = bf16[96,768]{1,0:T(8,128)(2,1)} async-done(((bf16[768,768]{1,0:T(8,128)(2,1)}), bf16[96,768]{1,0:T(8,128)(2,1)}) %reduce-scatter.27.cloned.1.call-update) | async-done | bytes 147472 | tf_op jit(solution)/shard_map/reduce_scatter | solution.py:284
  1096.4 33.1 %reduce-scatter.25.cloned.1.call-done = bf16[96,768]{1,0:T(8,128)(2,1)} async-done(((bf16[768,768]{1,0:T(8,128)(2,1)}), bf16[96,768]{1,0:T(8,128)(2,1)}) %reduce-scatter.25.cloned.1.call-update) | async-done | bytes 147472 | tf_op jit(solution)/shard_map/reduce_scatter | solution.py:284
  1129.6 56.7 %reduce-scatter.35.cloned.1.call-done = bf16[384,768]{1,0:T(8,128)(2,1)} async-done(((bf16[3072,768]{1,0:T(8,128)(2,1)}), bf16[384,768]{1,0:T(8,128)(2,1)}) %reduce-scatter.35.cloned.1.call-update) | async-done | bytes 589840 | tf_op jit(solution)/shard_map/reduce_scatter | solution.py:302
  1186.3 55.6 %reduce-scatter.31.cloned.1.call-done = bf16[96,3072]{1,0:T(8,128)(2,1)} async-done(((bf16[768,3072]{1,0:T(8,128)(2,1)}), bf16[96,3072]{1,0:T(8,128)(2,1)}) %reduce-scatter.31.cloned.1.call-update) | async-done | bytes 589840 | tf_op jit(solution)/shard_map/reduce_scatter | solution.py:296
  1241.9 55.7 %reduce-scatter.29.cloned.1.call-done = bf16[96,3072]{1,0:T(8,128)(2,1)} async-done(((bf16[768,3072]{1,0:T(8,128)(2,1)}), bf16[96,3072]{1,0:T(8,128)(2,1)}) %reduce-scatter.29.cloned.1.call-update) | async-done | bytes 589840 | tf_op jit(solution)/shard_map/reduce_scatter | solution.py:296
  1297.6 55.5 %reduce-scatter.33.cloned.1.call-done = bf16[384,768]{1,0:T(8,128)(2,1)} async-done(((bf16[3072,768]{1,0:T(8,128)(2,1)}), bf16[384,768]{1,0:T(8,128)(2,1)}) %reduce-scatter.33.cloned.1.call-update) | async-done | bytes 589840 | tf_op jit(solution)/shard_map/reduce_scatter | solution.py:302
  1376.2 14.1 all-reduce.36
  1407.4 51.7 %all-reduce.40.cloned.1.call-done = (bf16[1,96,2304]{1,2,0:T(8,128)(2,1)}, bf16[1,96,2304]{1,2,0:T(8,128)(2,1)}, bf16[1,96,768]{2,1,0:T(8,128)(2,1)}, bf16[1,96,...) async-done(((bf16[1,96,2304]{1,2,0:T(8,128)(2,1)}, ...) | async-done | bytes 3538960 | tf_op jit(solution)/shard_map/psum | solution.py:316
  (978 shorter events, 639.5 us)
Async XLA Ops:
  7.3 47.7 %all-gather.48.cloned.1.call-start = ((), (), s32[]{:S(2)}) async-start(), calls=%async_computation.22 | async-start | bytes 3981312 | tf_op jit(solution)/shard_map/all_gather | solution.py:383
  9.6 91.5 %all-gather.42.cloned.1.call-start = ((), (), s32[]{:S(2)}) async-start(), calls=%async_computation.13 | async-start | bytes 2949120 | tf_op jit(solution)/shard_map/all_gather | solution.py:126
  60.6 79.2 %all-gather.40.cloned.1.call-start = ((), (), s32[]{:S(2)}) async-start(), calls=%async_computation.12 | async-start | bytes 2949120 | tf_op jit(solution)/shard_map/all_gather | solution.py:125
  62.9 155.9 %all-gather.50.cloned.1.call-start = ((), (), s32[]{:S(2)}) async-start(), calls=%async_computation.23 | async-start | bytes 1327104 | tf_op jit(solution)/shard_map/all_gather | solution.py:383
  63.7 159.5 %all-gather.52.cloned.1.call-start = ((), (), s32[]{:S(2)}) async-start(), calls=%async_computation.24 | async-start | bytes 5308416 | tf_op jit(solution)/shard_map/all_gather | solution.py:383
  64.9 206.3 %all-gather.54.cloned.1.call-start = ((), (), s32[]{:S(2)}) async-start(), calls=%async_computation.25 | async-start | bytes 5308416 | tf_op jit(solution)/shard_map/all_gather | solution.py:383
  66.1 247.1 %all-gather.56.cloned.1.call-start = ((), (), s32[]{:S(2)}) async-start(), calls=%async_computation.26 | async-start | bytes 3981312 | tf_op jit(solution)/shard_map/all_gather | solution.py:383
  66.8 288.2 %all-gather.46.cloned.1.call-start = ((), (), s32[]{:S(2)}) async-start(), calls=%async_computation.15 | async-start | bytes 2949120 | tf_op jit(solution)/shard_map/all_gather | solution.py:126
  319.0 76.0 %all-gather.44.cloned.1.call-start = ((), (), s32[]{:S(2)}) async-start(), calls=%async_computation.14 | async-start | bytes 2949120 | tf_op jit(solution)/shard_map/all_gather | solution.py:125
  321.2 153.1 %all-gather.58.cloned.1.call-start = ((), (), s32[]{:S(2)}) async-start(), calls=%async_computation.27 | async-start | bytes 1327104 | tf_op jit(solution)/shard_map/all_gather | solution.py:383
  321.8 155.2 %all-gather.60.cloned.1.call-start = ((), (), s32[]{:S(2)}) async-start(), calls=%async_computation.28 | async-start | bytes 5308416 | tf_op jit(solution)/shard_map/all_gather | solution.py:383
  322.5 202.9 %all-gather.62.cloned.1.call-start = ((), (), s32[]{:S(2)}) async-start(), calls=%async_computation.29 | async-start | bytes 5308416 | tf_op jit(solution)/shard_map/all_gather | solution.py:383
  323.1 384.1 %reduce-scatter.37.cloned.1.call-start = ((), (), s32[]{:S(2)}) async-start(), calls=%async_computation.30 | async-start | bytes 2949120
  403.3 71.0 %copy-start.8 = (f32[384,768]{1,0:T(8,128)S(1)}, f32[384,768]{1,0:T(8,128)}, u32[]{:S(2)}) copy-start(f32[384,768]{1,0:T(8,128)} %copy-done.7) | copy-start | bytes 3538948
  476.6 65.6 %copy-start.13 = (f32[384,768]{1,0:T(8,128)}, f32[384,768]{1,0:T(8,128)S(1)}, u32[]{:S(2)}) copy-start(f32[384,768]{1,0:T(8,128)S(1)} %get-tuple-element.690) | copy-start | bytes 3538948
  476.6 65.6 %copy-start.53 = (f32[384]{0:T(512)}, f32[384]{0:T(512)S(1)}, u32[]{:S(2)}) copy-start(f32[384]{0:T(512)S(1)} %broadcast_multiply_fusion.1) | copy-start | bytes 4612
  671.3 76.3 %reduce-scatter.39.cloned.1.call-start = ((), (), s32[]{:S(2)}) async-start(), calls=%async_computation.31 | async-start | bytes 2949120
  675.5 74.2 %copy-start.9 = (f32[384,768]{1,0:T(8,128)S(1)}, f32[384,768]{1,0:T(8,128)}, u32[]{:S(2)}) copy-start(f32[384,768]{1,0:T(8,128)} %copy-done.7) | copy-start | bytes 3538948
  675.5 74.2 %copy-start.16 = (f32[384,768]{1,0:T(8,128)S(1)}, f32[384,768]{1,0:T(8,128)}, u32[]{:S(2)}) copy-start(f32[384,768]{1,0:T(8,128)} %copy-done.15) | copy-start | bytes 3538948
  675.5 74.2 %copy-start.51 = (f32[384]{0:T(512)S(1)}, f32[384]{0:T(512)}, u32[]{:S(2)}) copy-start(f32[384]{0:T(512)} %copy-done.50) | copy-start | bytes 4612
  675.5 257.8 %reduce-scatter.41.cloned.1.call-start = ((), (), s32[]{:S(2)}) async-start(), calls=%async_computation.32 | async-start | bytes 2949120
  895.8 77.9 %reduce-scatter.43.cloned.1.call-start = ((), (), s32[]{:S(2)}) async-start(), calls=%async_computation.33 | async-start | bytes 2949120
  900.0 153.6 %reduce-scatter.47.cloned.1.call-start = ((), (), s32[]{:S(2)}) async-start(), calls=%async_computation.35 | async-start | bytes 3981312
  906.7 68.4 %copy-start.128 = (bf16[1,384,768]{2,1,0:T(8,128)(2,1)S(1)}, bf16[1,384,768]{2,1,0:T(8,128)(2,1)}, u32[]{:S(2)}) copy-start(bf16[1,384,768]{2,1,0:T(8,128)(2,1)} %param.25) | copy-start | bytes 1769476
  906.7 156.7 %reduce-scatter.45.cloned.1.call-start = ((), (), s32[]{:S(2)}) async-start(), calls=%async_computation.34 | async-start | bytes 3981312
  986.0 110.4 %reduce-scatter.27.cloned.1.call-start = ((), (), s32[]{:S(2)}) async-start(), calls=%async_computation.17 | async-start | bytes 1327104 | tf_op jit(solution)/shard_map/reduce_scatter | solution.py:284
  989.0 140.5 %reduce-scatter.25.cloned.1.call-start = ((), (), s32[]{:S(2)}) async-start(), calls=%async_computation.16 | async-start | bytes 1327104 | tf_op jit(solution)/shard_map/reduce_scatter | solution.py:284
  990.9 195.4 %reduce-scatter.35.cloned.1.call-start = ((), (), s32[]{:S(2)}) async-start(), calls=%async_computation.21 | async-start | bytes 5308416 | tf_op jit(solution)/shard_map/reduce_scatter | solution.py:302
  997.6 244.4 %reduce-scatter.31.cloned.1.call-start = ((), (), s32[]{:S(2)}) async-start(), calls=%async_computation.19 | async-start | bytes 5308416 | tf_op jit(solution)/shard_map/reduce_scatter | solution.py:296
  1005.2 292.4 %reduce-scatter.29.cloned.1.call-start = ((), (), s32[]{:S(2)}) async-start(), calls=%async_computation.18 | async-start | bytes 5308416 | tf_op jit(solution)/shard_map/reduce_scatter | solution.py:296
  1012.7 340.5 %reduce-scatter.33.cloned.1.call-start = ((), (), s32[]{:S(2)}) async-start(), calls=%async_computation.20 | async-start | bytes 5308416 | tf_op jit(solution)/shard_map/reduce_scatter | solution.py:302
  1020.3 438.8 %all-reduce.40.cloned.1.call-start = ((), (), s32[]{:S(2)}) async-start(), calls=%async_computation.36 | async-start | bytes 7667712 | tf_op jit(solution)/shard_map/psum | solution.py:316
  (196 other events, 1493.1 us)
Sparse Core Ops, SparseCore 0:
  10.3 44.5 all-gather.47
  60.7 39.1 all-gather.41
  102.3 37.4 all-gather.39
  141.9 23.0 all-gather.49
  167.0 51.4 all-gather.51
  220.6 50.5 all-gather.53
  272.8 40.3 all-gather.55
  319.1 35.9 all-gather.45
  357.5 37.4 all-gather.43
  396.5 23.0 all-gather.57
  421.8 51.4 all-gather.59
  474.8 50.5 all-gather.61
  671.4 35.7 reduce-scatter.36
  710.1 37.3 reduce-scatter.38
  895.9 37.3 reduce-scatter.40
  936.3 37.3 reduce-scatter.42
  975.9 41.6 reduce-scatter.46
  1019.9 43.4 reduce-scatter.44
  1066.2 30.1 reduce-scatter.26
  1098.6 30.9 reduce-scatter.24
  1131.9 54.3 reduce-scatter.34
  1188.6 53.2 reduce-scatter.30
  1244.2 53.3 reduce-scatter.28
  1299.8 53.3 reduce-scatter.32
  1358.2 100.8 all-reduce.39
where the time goes:
time: 1490 us; the launch traced here: 1470 us
  waiting for transfers between devices  683 us (46%)
  matrix products  415 us (28%)
  local copies, waits for them, and re-layouts  189 us (13%)
  blocking collectives  108 us (7%)
  other arithmetic  58.8 us (4%)
  between operations  17.7 us (1%)
    unnamed x31, waiting for transfers between devices  146 us
    all_gather x8, waiting for transfers between devices, on_device(): lax.all_gather(for_sending(layer_slices(sharded, layer_index)), 'fsdp', a...  119 us
    reduce_scatter x2, waiting for transfers between devices, reduce_grads(): lax.psum_scatter(grads[9].astype(jnp.bfloat16), 'fsdp', scatter_dimension...  112 us
    reduce_scatter x2, waiting for transfers between devices, reduce_grads(): lax.psum_scatter(grads[7].astype(jnp.bfloat16), 'fsdp', scatter_dimension...  111 us
    dot_general x48, matrix products, one_head(): jnp.einsum('qd,kd->qk', head_q, head_k, preferred_element_type=jnp.float32)  94.2 us
    unnamed x323, local copies, waits for them, and re-layouts  83.4 us
    all_gather x2, waiting for transfers between devices, forward_layer(): lax.all_gather(keys_own, 'ctx', axis=0, tiled=True)  65 us
    reduce_scatter x2, waiting for transfers between devices, reduce_grads(): lax.psum_scatter(grads[3].astype(jnp.bfloat16), 'fsdp', scatter_dimension...  64.1 us
  transfers between devices with their start and end apart: 25, of which 18 were waited for; matrix products, arithmetic and copies ran while one was open for 23% of the time, Pallas kernels for 0%

commit v1 on v0

--- a/solution.py
+++ b/solution.py
@@ -1,6 +1,10 @@
+import functools
+
 import jax
 import jax.numpy as jnp
 from jax import lax
+from jax.experimental import pallas as pl
+from jax.experimental.pallas import tpu as pltpu
 from jax.sharding import PartitionSpec as P
 
 HEADS = 12
@@ -333,7 +337,7 @@
     return tuple((tensor[layer_index] for tensor in sharded))
 
 
-def on_device(
+def on_device_plain(
     activations,
     cotangent,
     doc_start,
@@ -418,6 +422,606 @@
     )
 
 
+F32 = jnp.float32
+BF = jnp.bfloat16
+WIDTH = HEADS * HEAD_DIM
+QB = 256
+SCORE_SCALE = HEAD_DIM ** (-0.5) * 1.4426950408889634
+NEG = -1e30
+VMEM_LIMIT = 60 * 1024 * 1024
+
+
+def mm_nn(a, b):
+    return lax.dot_general(a, b, (((1,), (0,)), ((), ())), preferred_element_type=F32)
+
+
+def mm_nt(a, b):
+    return lax.dot_general(a, b, (((1,), (1,)), ((), ())), preferred_element_type=F32)
+
+
+def mm_tn(a, b):
+    return lax.dot_general(a, b, (((0,), (0,)), ((), ())), preferred_element_type=F32)
+
+
+def call(kernel, outs, args, specs, scratch, name, flops, nbytes):
+    return pl.pallas_call(
+        kernel,
+        out_shape=[jax.ShapeDtypeStruct(shape, dtype) for shape, dtype in outs],
+        in_specs=[pl.BlockSpec(memory_space=space) for space in specs],
+        out_specs=[pl.BlockSpec(memory_space=pltpu.VMEM) for _ in outs],
+        scratch_shapes=scratch,
+        compiler_params=pltpu.CompilerParams(vmem_limit_bytes=VMEM_LIMIT),
+        cost_estimate=pl.CostEstimate(flops=flops, bytes_accessed=nbytes, transcendentals=0),
+        name=name,
+    )(*args)
+
+
+def block_of(block, blocks):
+    half = 0 if 2 * block < blocks else 1
+    return (block if half == 0 else blocks - 1 - block), half
+
+
+def attn_fwd_kernel(
+    jmap, inv, jmin, h0, h1, h2, h3, w, bias, qrow, kcol, qkv, ctx, lse, q_s, k_s, vt_s, o_s, *, heads, tokens
+):
+    blocks = tokens // BLK
+    hw = heads * HEAD_DIM
+    for j, piece in enumerate((h0, h1, h2, h3)):
+        qkv[j] = (mm_nn(piece[...], w[...]) + bias[...]).astype(BF)
+    for pair in range(blocks // 2):
+        rows = []
+        for block in (2 * pair, 2 * pair + 1):
+            at, half = block_of(block, blocks)
+            rows.append(qkv[jmap[at], half * BLK : (half + 1) * BLK, :])
+        both = jnp.concatenate(rows, axis=0)
+        lo, hi = 2 * pair * BLK, 2 * (pair + 1) * BLK
+        for h in range(heads):
+            q_s[h, lo:hi, :] = both[:, h * HEAD_DIM : (h + 1) * HEAD_DIM]
+            k_s[h, lo:hi, :] = both[:, hw + h * HEAD_DIM : hw + (h + 1) * HEAD_DIM]
+        vt_s[:, lo:hi] = both[:, 2 * hw :].T
+    iota_k = lax.broadcasted_iota(jnp.int32, (QB, QB), 0)
+    iota_q = lax.broadcasted_iota(jnp.int32, (QB, QB), 1)
+    causal = iota_k <= iota_q
+    for h in range(heads):
+        for i in range(tokens // QB):
+            lo = i * QB
+            q = q_s[h, lo : lo + QB, :]
+            starts_q = qrow[0:1, lo : lo + QB]
+
+            def scores(at, diagonal):
+                s = mm_nt(k_s[h, pl.ds(at, QB), :], q) * SCORE_SCALE
+                col = kcol[pl.ds(at, QB), :]
+                allowed = jnp.concatenate([col, col], axis=1) == starts_q
+                if diagonal:
+                    allowed = allowed & causal
+                return jnp.where(allowed, s, NEG)
+
+            s = scores(lo, True)
+            top = jnp.max(s, axis=0, keepdims=True)
+            p = jnp.exp2(s - top)
+            total = jnp.sum(p, axis=0, keepdims=True)
+            out = mm_nn(vt_s[h * HEAD_DIM : (h + 1) * HEAD_DIM, lo : lo + QB], p.astype(BF))
+
+            def step(jb, carry):
+                top, total, out = carry
+                at = pl.multiple_of(jb * QB, QB)
+                s = scores(at, False)
+                new_top = jnp.maximum(top, jnp.max(s, axis=0, keepdims=True))
+                p = jnp.exp2(s - new_top)
+                alpha = jnp.exp2(top - new_top)
+                total = total * alpha + jnp.sum(p, axis=0, keepdims=True)
+                out = out * alpha + mm_nn(
+                    vt_s[h * HEAD_DIM : (h + 1) * HEAD_DIM, pl.ds(at, QB)], p.astype(BF)
+                )
+                return (new_top, total, out)
+
+            if i > 0:
+                top, total, out = lax.fori_loop(jmin[i], i, step, (top, total, out))
+            o_s[h * HEAD_DIM : (h + 1) * HEAD_DIM, lo : lo + QB] = out / total
+            lse[h : h + 1, lo : lo + QB] = top + jnp.log2(total)
+    for pair in range(blocks // 2):
+        lo, hi = 2 * pair * BLK, 2 * (pair + 1) * BLK
+        both = o_s[:, lo:hi].T.astype(BF)
+        for n, block in enumerate((2 * pair, 2 * pair + 1)):
+            at, half = block_of(block, blocks)
+            ctx[inv[at], :, half * hw : (half + 1) * hw] = both[n * BLK : (n + 1) * BLK, :]
+
+
+def attn_bwd_kernel(
+    jmap, inv, jmin, h0, h1, h2, h3, w, qrow, kcol, qkv, ctx, gctx, lse,
+    g_own, g_a, g_bd, dw,
+    q_s, k_s, v_s, do_s, kt_s, delta_s, dk_s, dv_s, dqt_s, g_s, *, heads, tokens
+):
+    blocks = tokens // BLK
+    hw = heads * HEAD_DIM
+    scale = HEAD_DIM ** (-0.5)
+    for pair in range(blocks // 2):
+        rows, grads, outs = [], [], []
+        for block in (2 * pair, 2 * pair + 1):
+            at, half = block_of(block, blocks)
+            rows.append(qkv[jmap[at], half * BLK : (half + 1) * BLK, :])
+            grads.append(gctx[inv[at], :, half * hw : (half + 1) * hw])
+            outs.append(ctx[inv[at], :, half * hw : (half + 1) * hw])
+        both = jnp.concatenate(rows, axis=0)
+        grad = jnp.concatenate(grads, axis=0)
+        out = jnp.concatenate(outs, axis=0)
+        lo, hi = 2 * pair * BLK, 2 * (pair + 1) * BLK
+        prod = (grad.astype(F32) * out.astype(F32)).T
+        kt_s[:, lo:hi] = both[:, hw : 2 * hw].T
+        for h in range(heads):
+            c0, c1 = h * HEAD_DIM, (h + 1) * HEAD_DIM
+            q_s[h, lo:hi, :] = both[:, c0:c1]
+            k_s[h, lo:hi, :] = both[:, hw + c0 : hw + c1]
+            v_s[h, lo:hi, :] = both[:, 2 * hw + c0 : 2 * hw + c1]
+            do_s[h, lo:hi, :] = grad[:, c0:c1]
+            delta_s[h : h + 1, lo:hi] = jnp.sum(prod[c0:c1, :], axis=0, keepdims=True)
+    dk_s[...] = jnp.zeros_like(dk_s)
+    dv_s[...] = jnp.zeros_like(dv_s)
+    iota_k = lax.broadcasted_iota(jnp.int32, (QB, QB), 0)
+    iota_q = lax.broadcasted_iota(jnp.int32, (QB, QB), 1)
+    causal = iota_k <= iota_q
+    for h in range(heads):
+        for i in range(tokens // QB):
+            lo = i * QB
+            q = q_s[h, lo : lo + QB, :]
+            do = do_s[h, lo : lo + QB, :]
+            starts_q = qrow[0:1, lo : lo + QB]
+            lse_q = lse[h : h + 1, lo : lo + QB]
+            delta_q = delta_s[h : h + 1, lo : lo + QB]
+
+            def block(at, diagonal):
+                s = mm_nt(k_s[h, pl.ds(at, QB), :], q) * SCORE_SCALE
+                col = kcol[pl.ds(at, QB), :]
+                allowed = jnp.concatenate([col, col], axis=1) == starts_q
+                if diagonal:
+                    allowed = allowed & causal
+                p = jnp.exp2(jnp.where(allowed, s, NEG) - lse_q)
+                dp = mm_nt(v_s[h, pl.ds(at, QB), :], do)
+                ds = (p * (dp - delta_q)).astype(BF)
+                dv_s[h, pl.ds(at, QB), :] += mm_nn(p.astype(BF), do)
+                dk_s[h, pl.ds(at, QB), :] += mm_nn(ds, q)
+                return mm_nn(kt_s[h * HEAD_DIM : (h + 1) * HEAD_DIM, pl.ds(at, QB)], ds)
+
+            dq = block(lo, True)
+            if i > 0:
+                dq = lax.fori_loop(
+                    jmin[i], i, lambda jb, acc: acc + block(pl.multiple_of(jb * QB, QB), False), dq
+                )
+            dqt_s[h * HEAD_DIM : (h + 1) * HEAD_DIM, lo : lo + QB] = dq * scale
+    for pair in range(blocks // 2):
+        lo, hi = 2 * pair * BLK, 2 * (pair + 1) * BLK
+        parts = [dqt_s[:, lo:hi].T.astype(BF)]
+        parts += [(dk_s[h, lo:hi, :] * scale).astype(BF) for h in range(heads)]
+        parts += [dv_s[h, lo:hi, :].astype(BF) for h in range(heads)]
+        both = jnp.concatenate(parts, axis=1)
+        for n, block_at in enumerate((2 * pair, 2 * pair + 1)):
+            at, half = block_of(block_at, blocks)
+            g_s[jmap[at], half * BLK : (half + 1) * BLK, :] = both[n * BLK : (n + 1) * BLK, :]
+    total = None
+    sums = None
+    for j, piece in enumerate((h0, h1, h2, h3)):
+        g = g_s[j]
+        back = mm_nt(g, w[...])
+        if j == 0:
+            g_own[...] = back
+        elif j == 1:
+            g_a[...] = back.astype(BF)
+        else:
+            g_bd[j - 2] = back.astype(BF)
+        part = mm_tn(piece[...], g)
+        col = jnp.sum(g.astype(F32), axis=0, keepdims=True)
+        total = part if total is None else total + part
+        sums = col if sums is None else sums + col
+    shards, rows_out, cols = dw.shape
+    rows = WIDTH // shards
+    dw[:, 0:rows, :] = total.reshape(shards, rows, cols).astype(BF)
+    dw[:, rows:rows_out, :] = jnp.broadcast_to(sums[None], (shards, rows_out - rows, cols)).astype(BF)
+
+
+def start_ffn_copies(core, own, other, e_s, r_s, sems):
+    copies = []
+    for p, (mine, theirs) in enumerate(zip(own, (other[0], other[2], other[1], other[3]))):
+        group = []
+        for n, (src, parity) in enumerate(((mine, core), (theirs, 1 - core))):
+            for k, dst in enumerate((e_s, r_s)):
+                copy = pltpu.make_async_copy(src.at[:, k], dst.at[p, :, parity], sems.at[p, 2 * n + k])
+                copy.start()
+                group.append(copy)
+        copies.append(group)
+    return copies
+
+
+def ffn_scratch():
+    return [
+        pltpu.VMEM((4, 4, 2, 96, WIDTH), BF),
+        pltpu.VMEM((4, 4, 2, 96, WIDTH), BF),
+        pltpu.SemaphoreType.DMA((4, 4)),
+    ]
+
+
+def norm_parts(values):
+    centre = values - jnp.mean(values, axis=-1, keepdims=True)
+    spread = jnp.mean(centre * centre, axis=-1, keepdims=True)
+    rstd = lax.rsqrt(spread + norm_eps)
+    return centre * rstd, rstd
+
+
+def mlp_fwd_kernel(
+    core_ref, rk, cx, hid, wo, vec, eb, t, a, b, d, ct, ca, cb, cd,
+    lowctx, xhat1, rstd1, lown, act, gp, xhat2, rstd2, hnext, hlow,
+    e_s, r_s, sems,
+):
+    core = core_ref[0]
+    copies = start_ffn_copies(core, (t, a, b, d), (ct, ca, cb, cd), e_s, r_s, sems)
+    ranks, _, cols = cx.shape
+    hw = cols // 2
+    for s in range(ranks):
+        for half in range(2):
+            lowctx[half * BLK : (half + 1) * BLK, s * hw : (s + 1) * hw] = cx[s, :, half * hw : (half + 1) * hw]
+    first_sum = hid[...] + (mm_nn(lowctx[...], wo[...].reshape(WIDTH, WIDTH)) + vec[0:1, :])
+    x1, r1 = norm_parts(first_sum)
+    xhat1[...] = x1
+    rstd1[...] = r1
+    normed = x1 * vec[1:2, :] + vec[2:3, :]
+    lown[...] = normed.astype(BF)
+    out = normed + vec[3:4, :]
+    for p in range(4):
+        for copy in copies[p]:
+            copy.wait()
+        bias = eb[pl.ds(rk[p], 1), :]
+        u = mm_nn(lown[...], e_s[p].reshape(WIDTH, WIDTH)) + bias
+        cdf = 0.5 * (1.0 + lax.erf(u * 0.7071067811865476))
+        pdf = jnp.exp(-0.5 * u * u) * 0.3989422804014327
+        low = (u * cdf).astype(BF)
+        act[:, p * WIDTH : (p + 1) * WIDTH] = low
+        gp[:, p * WIDTH : (p + 1) * WIDTH] = (cdf + u * pdf).astype(BF)
+        out = out + mm_nn(low, r_s[p].reshape(WIDTH, WIDTH))
+    x2, r2 = norm_parts(out)
+    xhat2[...] = x2
+    rstd2[...] = r2
+    nxt = x2 * vec[4:5, :] + vec[5:6, :]
+    hnext[...] = nxt
+    hlow[...] = nxt.astype(BF)
+
+
+def norm_back(gy, gain, xhat, rstd):
+    g = gy * gain
+    return rstd * (g - jnp.mean(g, axis=-1, keepdims=True) - xhat * jnp.mean(g * xhat, axis=-1, keepdims=True))
+
+
+def rows_sum(x):
+    return jnp.sum(x, axis=0, keepdims=True)
+
+
+def mlp_bwd_kernel(
+    core_ref, rk, gh, xhat1, rstd1, xhat2, rstd2, gp, vec, wo, t, a, b, d, ct, ca, cb, cd,
+    gfs, gb, gat, di, gctx, ext,
+    e_s, r_s, sems, eb_s,
+):
+    core = core_ref[0]
+    copies = start_ffn_copies(core, (t, a, b, d), (ct, ca, cb, cd), e_s, r_s, sems)
+    grad = gh[...]
+    x2 = xhat2[...]
+    gss = norm_back(grad, vec[4:5, :], x2, rstd2[...])
+    low = gss.astype(BF)
+    gb[...] = low
+    sums = [None] * 8
+    sums[4] = rows_sum(grad * x2)
+    sums[5] = rows_sum(grad)
+    sums[3] = rows_sum(low.astype(F32))
+    gn = gss
+    eb_s[...] = jnp.zeros_like(eb_s)
+    for p in range(4):
+        for copy in copies[p]:
+            copy.wait()
+        ga = mm_nt(low, r_s[p].reshape(WIDTH, WIDTH))
+        dip = (ga * gp[:, p * WIDTH : (p + 1) * WIDTH].astype(F32)).astype(BF)
+        di[:, p * WIDTH : (p + 1) * WIDTH] = dip
+        eb_s[pl.ds(rk[p], 1), :] = rows_sum(dip.astype(F32))
+        gn = gn + mm_nt(dip, e_s[p].reshape(WIDTH, WIDTH))
+    x1 = xhat1[...]
+    gf = norm_back(gn, vec[1:2, :], x1, rstd1[...])
+    sums[1] = rows_sum(gn * x1)
+    sums[2] = rows_sum(gn)
+    gfs[...] = gf
+    lowa = gf.astype(BF)
+    gat[...] = lowa
+    sums[0] = rows_sum(lowa.astype(F32))
+    sums[6] = jnp.zeros_like(sums[0])
+    sums[7] = sums[6]
+    gc = mm_nt(lowa, wo[...].reshape(WIDTH, WIDTH)).astype(BF)
+    ranks, _, cols = gctx.shape
+    hw = cols // 2
+    for s in range(ranks):
+        for half in range(2):
+            gctx[s, :, half * hw : (half + 1) * hw] = gc[half * BLK : (half + 1) * BLK, s * hw : (s + 1) * hw]
+    vecs = jnp.concatenate(sums + [eb_s[...]], axis=0)
+    ext[...] = jnp.zeros_like(ext)
+    shards = ext.shape[0]
+    cut = WIDTH // shards
+    for f in range(shards):
+        ext[f, :, 0:cut] = vecs[:, f * cut : (f + 1) * cut].astype(BF)
+
+
+def wgrad_kernel(
+    core_ref, lown, di, act, gb, lowctx, gat, ext, mine_ta, mine_bd, other_ta, other_bd, dwo
+):
+    core = core_ref[0]
+    shards, rows_out, _ = dwo.shape
+    rows = WIDTH // shards
+    dwo[:, 0:rows, :] = mm_tn(lowctx[...], gat[...]).reshape(shards, rows, WIDTH).astype(BF)
+    dwo[:, rows:rows_out, :] = ext[...]
+    mine = ((mine_ta, 0), (mine_ta, 1), (mine_bd, 0), (mine_bd, 1))
+    other = ((other_ta, 0), (other_bd, 0), (other_ta, 1), (other_bd, 1))
+    for p in (2, 3, 1, 0):
+        cut = slice(p * WIDTH, (p + 1) * WIDTH)
+        for k, (left, right) in enumerate(((lown[...], di[:, cut]), (act[:, cut], gb[...]))):
+            x = mm_tn(left, right).reshape(4, 2, 96, WIDTH).astype(BF)
+            for parity in range(2):
+
+                @pl.when(core == parity)
+                def _():
+                    ref, at = mine[p]
+                    ref[at, :, k] = x[:, parity]
+
+                @pl.when(core != parity)
+                def _():
+                    ref, at = other[p]
+                    ref[at, :, k] = x[:, parity]
+
+
+def place_kernel(rk, ffn0, ffn1, ffn2, ffn3, win0, win1, win2, win3, dwo, e_out, r_out, i_out, o_out, e_s, i_s):
+    for p, (ffn, win) in enumerate(((ffn0, win0), (ffn1, win1), (ffn2, win2), (ffn3, win3))):
+        r_out[pl.ds(pl.multiple_of(rk[p] * 96, 96), 96), :] = ffn[1].astype(F32)
+        e_s[rk[p]] = ffn[0].astype(F32)
+        i_s[rk[p]] = win[0:96, :].astype(F32)
+    for f in range(8):
+        e_out[:, f * 384 : (f + 1) * 384] = jnp.concatenate(
+            [e_s[c, :, f * 96 : (f + 1) * 96] for c in range(4)], axis=1
+        )
+    hw = WIDTH // 4
+    for k in range(3):
+        i_out[:, k * WIDTH : (k + 1) * WIDTH] = jnp.concatenate(
+            [i_s[c, :, k * hw : (k + 1) * hw] for c in range(4)], axis=1
+        )
+    o_out[...] = dwo[0:96, :].astype(F32)
+
+
+def permutations(ctx, fsdp):
+    first, second, cores = [], [], []
+    for c in range(ctx):
+        for f in range(fsdp):
+            m1, m2 = (1, 2) if f % 2 == 0 else (2, 1)
+            first.append((c * fsdp + f, (c ^ m1) * fsdp + f))
+            second.append((c * fsdp + f, (c ^ m2) * fsdp + f))
+            cores.append((c * fsdp + f, c * fsdp + (f ^ 1)))
+    return first, second, cores
+
+
+def on_device_fast(
+    activations, cotangent, doc_start, deal,
+    attend_in, query_bias, value_bias, attend_out, attend_bias, first_gain, first_shift,
+    expand_proj, expand_bias, reduce_proj, reduce_bias, second_gain, second_shift,
+    *, ctx, fsdp,
+):
+    S = pltpu.SMEM
+    V = pltpu.VMEM
+    A = pl.ANY
+    first, second, cores = permutations(ctx, fsdp)
+    both_axes = ("ctx", "fsdp")
+
+    def via_first(x):
+        return lax.ppermute(x, both_axes, first)
+
+    def via_second(x):
+        return lax.ppermute(x, both_axes, second)
+
+    def via_core(x):
+        return lax.ppermute(x, both_axes, cores)
+
+    def gather_ctx(x):
+        a, b = via_first(x), via_second(x)
+        return (x, a, b, via_second(a))
+
+    heads = HEADS // ctx
+    hw = heads * HEAD_DIM
+    rows = activations.shape[1]
+    tokens = rows * ctx
+    c = lax.axis_index("ctx").astype(jnp.int32)
+    core = (lax.axis_index("fsdp") % 2).astype(jnp.int32)
+    core1 = core.reshape(1)
+    m1 = 1 + core
+    rk = jnp.stack([c, c ^ m1, c ^ (3 - m1), c ^ 3])
+    inv = jnp.sum(
+        jnp.where(deal[None, :] == jnp.arange(ctx)[:, None], jnp.arange(ctx)[None, :], 0), axis=1
+    ).astype(jnp.int32)
+    mask = inv ^ c
+    jmap = jnp.where((core == 1) & (mask > 0) & (mask < 3), 3 - mask, mask).astype(jnp.int32)
+
+    zgroups = [[2 * z + k for z in range(fsdp // 2)] for k in range(2)]
+    hidden = activations[0].astype(F32)
+    hlow = activations[0]
+
+    small = [attend_bias, first_gain, first_shift, reduce_bias, second_gain, second_shift, query_bias, value_bias]
+    packed = jnp.concatenate([jnp.stack(small, axis=1).reshape(LAYERS, -1), expand_bias], axis=1)
+    packed = lax.all_gather(packed.reshape(1, -1), "fsdp", axis=0, tiled=True).reshape(fsdp, LAYERS, -1)
+    cut = WIDTH // fsdp
+    vec = packed[:, :, : 8 * cut].reshape(fsdp, LAYERS, 8, cut).transpose(1, 2, 0, 3).reshape(LAYERS, 8, WIDTH)
+    vec = vec.astype(F32)
+    ebias = packed[:, :, 8 * cut :].reshape(fsdp, LAYERS, ctx, cut).transpose(1, 2, 0, 3)
+    ebias = ebias.reshape(LAYERS, ctx, WIDTH).astype(F32)
+
+    starts = lax.all_gather(doc_start[0], "ctx", axis=0, tiled=True).reshape(ctx, 2, BLK)
+    chosen = inv[:, None, None, None] == jnp.arange(ctx, dtype=jnp.int32)[None, :, None, None]
+    starts = jnp.sum(jnp.where(chosen, starts[None], 0), axis=1)
+    logical = jnp.concatenate([starts[:, 0], starts[::-1, 1]], axis=0).reshape(-1)
+    qrow = jnp.broadcast_to(logical[None, :], (8, tokens))
+    kcol = jnp.broadcast_to(logical[:, None], (tokens, 128))
+    jmin = jnp.min(logical.reshape(tokens // QB, QB), axis=1) // QB
+
+    def ffn_piece(layer):
+        e = expand_proj[layer].reshape(cut, fsdp, ctx, cut)
+        e = lax.dynamic_index_in_dim(e, c, axis=2, keepdims=False).reshape(cut, WIDTH)
+        r = lax.dynamic_slice_in_dim(reduce_proj[layer], c * cut, cut, axis=0)
+        x = lax.all_gather(
+            jnp.concatenate([e, r], axis=0), "fsdp", axis=0, tiled=True, axis_index_groups=zgroups
+        ).reshape(fsdp // 2, 2, cut, WIDTH)
+        own = gather_ctx(x)
+        return own + tuple(via_core(piece) for piece in own)
+
+    win = attend_in.reshape(LAYERS, cut, 3, WIDTH)
+    win = lax.dynamic_slice_in_dim(win, c * hw, hw, axis=3).reshape(LAYERS * cut, 3 * hw)
+    win = lax.all_gather(win, "fsdp", axis=0, tiled=True).reshape(fsdp, LAYERS, cut, 3 * hw)
+    win = [win[:, layer].reshape(WIDTH, 3 * hw) for layer in range(LAYERS)]
+    wout = lax.all_gather(attend_out.reshape(LAYERS * cut, WIDTH), "fsdp", axis=0, tiled=True)
+    wout = wout.reshape(fsdp, LAYERS, cut, WIDTH)
+    wout = [wout[:, layer] for layer in range(LAYERS)]
+    pieces = [ffn_piece(layer) for layer in range(LAYERS)]
+    qkv_bias = []
+    for layer in range(LAYERS):
+        qb = lax.dynamic_slice_in_dim(vec[layer, 6], c * hw, hw)
+        vb = lax.dynamic_slice_in_dim(vec[layer, 7], c * hw, hw)
+        qkv_bias.append(jnp.concatenate([qb, jnp.zeros_like(qb), vb])[None, :])
+
+    mac = 2
+    kept = []
+    for layer in range(LAYERS):
+        gathered = gather_ctx(hlow)
+        qkv, ctx_own, lse = call(
+            functools.partial(attn_fwd_kernel, heads=heads, tokens=tokens),
+            [((ctx, rows, 3 * hw), BF), ((ctx, BLK, 2 * hw), BF), ((8, tokens), F32)],
+            (jmap, inv, jmin) + gathered + (win[layer], qkv_bias[layer], qrow, kcol),
+            [S] * 3 + [V] * 8,
+            [
+                pltpu.VMEM((heads, tokens, HEAD_DIM), BF),
+                pltpu.VMEM((heads, tokens, HEAD_DIM), BF),
+                pltpu.VMEM((hw, tokens), BF),
+                pltpu.VMEM((hw, tokens), F32),
+            ],
+            "attn_fwd",
+            mac * tokens * WIDTH * 3 * hw * 4,
+            10 * 1024 * 1024,
+        )
+        cx = lax.all_to_all(ctx_own, "ctx", 0, 0, tiled=True)
+        lowctx, xhat1, rstd1, lown, act, gp, xhat2, rstd2, hidden, hlow = call(
+            mlp_fwd_kernel,
+            [
+                ((rows, WIDTH), BF), ((rows, WIDTH), F32), ((rows, 1), F32), ((rows, WIDTH), BF),
+                ((rows, 4 * WIDTH), BF), ((rows, 4 * WIDTH), BF), ((rows, WIDTH), F32), ((rows, 1), F32),
+                ((rows, WIDTH), F32), ((rows, WIDTH), BF),
+            ],
+            (core1, rk, cx, hidden, wout[layer], vec[layer], ebias[layer]) + pieces[layer],
+            [S] * 2 + [V] * 5 + [A] * 8,
+            ffn_scratch(),
+            "mlp_fwd",
+            mac * rows * WIDTH * WIDTH * 9,
+            20 * 1024 * 1024,
+        )
+        kept.append((gathered, qkv, ctx_own, lse, lowctx, xhat1, rstd1, lown, act, gp, xhat2, rstd2))
+    out_act = hlow[None]
+
+    grad = cotangent[0].astype(F32)
+    results = [None] * LAYERS
+    for layer in reversed(range(LAYERS)):
+        gathered, qkv, ctx_own, lse, lowctx, xhat1, rstd1, lown, act, gp, xhat2, rstd2 = kept[layer]
+        gfs, gb, gat, di, gctx, ext = call(
+            mlp_bwd_kernel,
+            [
+                ((rows, WIDTH), F32), ((rows, WIDTH), BF), ((rows, WIDTH), BF), ((rows, 4 * WIDTH), BF),
+                ((ctx, BLK, 2 * hw), BF), ((fsdp, 16, WIDTH), BF),
+            ],
+            (core1, rk, grad, xhat1, rstd1, xhat2, rstd2, gp, vec[layer], wout[layer]) + pieces[layer],
+            [S] * 2 + [V] * 8 + [A] * 8,
+            ffn_scratch() + [pltpu.VMEM((8, WIDTH), F32)],
+            "mlp_bwd",
+            mac * rows * WIDTH * WIDTH * 9,
+            20 * 1024 * 1024,
+        )
+        gcx = lax.all_to_all(gctx, "ctx", 0, 0, tiled=True)
+        pair = ((2, 4, 2, cut, WIDTH), BF)
+        mine_ta, mine_bd, other_ta, other_bd, dwo = call(
+            wgrad_kernel,
+            [pair, pair, pair, pair, ((fsdp, cut + 16, WIDTH), BF)],
+            (core1, lown, di, act, gb, lowctx, gat, ext),
+            [S] + [V] * 7,
+            [],
+            "wgrad",
+            mac * rows * WIDTH * WIDTH * 9,
+            20 * 1024 * 1024,
+        )
+        g_own, g_a, g_bd, dw = call(
+            functools.partial(attn_bwd_kernel, heads=heads, tokens=tokens),
+            [
+                ((rows, WIDTH), F32), ((rows, WIDTH), BF), ((2, rows, WIDTH), BF),
+                ((fsdp, cut + 16, 3 * hw), BF),
+            ],
+            (jmap, inv, jmin) + gathered + (win[layer], qrow, kcol, qkv, ctx_own, gcx, lse),
+            [S] * 3 + [V] * 11,
+            [
+                pltpu.VMEM((heads, tokens, HEAD_DIM), BF),
+                pltpu.VMEM((heads, tokens, HEAD_DIM), BF),
+                pltpu.VMEM((heads, tokens, HEAD_DIM), BF),
+                pltpu.VMEM((heads, tokens, HEAD_DIM), BF),
+                pltpu.VMEM((hw, tokens), BF),
+                pltpu.VMEM((8, tokens), F32),
+                pltpu.VMEM((heads, tokens, HEAD_DIM), F32),
+                pltpu.VMEM((heads, tokens, HEAD_DIM), F32),
+                pltpu.VMEM((hw, tokens), F32),
+                pltpu.VMEM((ctx, rows, 3 * hw), BF),
+            ],
+            "attn_bwd",
+            mac * tokens * WIDTH * 3 * hw * 8,
+            10 * 1024 * 1024,
+        )
+        back = via_second(g_bd).astype(F32)
+        over = via_first((g_a.astype(F32) + back[1]).astype(BF)).astype(F32)
+        grad = gfs + (g_own + (back[0] + over))
+        sum_bd = (mine_bd.astype(F32) + via_core(other_bd).astype(F32)).astype(BF)
+        back = via_second(sum_bd).astype(F32)
+        sum_ta = mine_ta.astype(F32) + via_core(other_ta).astype(F32) + back
+        over = via_first(sum_ta[1].astype(BF)).astype(F32)
+        ffn = lax.psum_scatter(
+            (sum_ta[0] + over).astype(BF), "fsdp", scatter_dimension=0, tiled=True, axis_index_groups=zgroups
+        ).reshape(2, cut, WIDTH)
+        dw = lax.psum_scatter(dw, "fsdp", scatter_dimension=0, tiled=True).reshape(cut + 16, 3 * hw)
+        dwo = lax.psum_scatter(dwo, "fsdp", scatter_dimension=0, tiled=True).reshape(cut + 16, WIDTH)
+        dwo = (dwo.astype(F32) + via_first(dwo).astype(F32)).astype(BF)
+        dwo = dwo.astype(F32) + via_second(dwo).astype(F32)
+        ffn_all = gather_ctx(ffn)
+        dw_all = gather_ctx(dw)
+        e_out, r_out, i_out, o_out = call(
+            place_kernel,
+            [((cut, 4 * WIDTH), F32), ((4 * cut, WIDTH), F32), ((cut, 3 * WIDTH), F32), ((cut, WIDTH), F32)],
+            (rk,) + ffn_all + dw_all + (dwo,),
+            [S] + [V] * 9,
+            [pltpu.VMEM((ctx, cut, WIDTH), F32), pltpu.VMEM((ctx, cut, 3 * hw), F32)],
+            "place",
+            0,
+            10 * 1024 * 1024,
+        )
+        shard = lax.axis_index("fsdp").astype(jnp.int32)
+        bias_rows = jnp.stack([piece[cut : cut + 1] for piece in dw_all])
+        owner = (shard * cut) // hw
+        holder = owner ^ c
+        holder = jnp.where((core == 1) & (holder > 0) & (holder < 3), 3 - holder, holder)
+        row = lax.dynamic_index_in_dim(bias_rows, holder, axis=0, keepdims=False)[0]
+        offset = shard * cut - owner * hw
+        qb = lax.dynamic_slice_in_dim(row, offset, cut).astype(F32)
+        vb = lax.dynamic_slice_in_dim(row, 2 * hw + offset, cut).astype(F32)
+        v = dwo[cut:, :cut]
+        results[layer] = (
+            i_out, qb, vb, o_out, v[0], v[1], v[2], e_out, v[8 : 8 + ctx].reshape(-1), r_out, v[3], v[4], v[5]
+        )
+    stacked = [jnp.stack([results[layer][n] for layer in range(LAYERS)]) for n in range(13)]
+    return (out_act, grad[None]) + tuple(stacked)
+
+
+def on_device(*args, ctx, fsdp):
+    if ctx == 4 and fsdp == 8 and args[0].shape[1] == 2 * BLK:
+        return on_device_fast(*args, ctx=ctx, fsdp=fsdp)
+    return on_device_plain(*args)
+
+
 def solution(mesh):
     placed = (
         P("fsdp", "ctx", None),
@@ -439,7 +1043,7 @@
         P(None, "fsdp"),
     )
     return jax.shard_map(
-        on_device,
+        functools.partial(on_device, ctx=mesh.shape["ctx"], fsdp=mesh.shape["fsdp"]),
         mesh=mesh,
         in_specs=placed,
         out_specs=(

time: 1490 us -> 607 us (0.41)
  waiting for transfers between devices: 683 us -> 198 us
  matrix products: 415 us -> 0 us
  Pallas kernels: 0 us -> 193 us
  local copies, waits for them, and re-layouts: 189 us -> 35.8 us
  blocking collectives: 108 us -> 33.2 us
  starting transfers between devices: 1.6 us -> 72.6 us
    dot_general x192 -> x0, matrix products: 415 us -> none  [the longest x48 94.2 us: one_head(): jnp.einsum('qd,kd->qk', head_q, head_k, preferred_element_type=jnp.float32)]
    reduce_scatter x6, waiting for transfers between devices: 288 us -> 23.6 us  [the longest x2 23.6 us: on_device_fast(): lax.psum_scatter((sum_ta[0] + over).astype(BF), 'fsdp', scatter_dimension...]
    all_gather x12 -> x4, waiting for transfers between devices: 198 us -> 2.17 us  [the longest x2 2.16 us: ffn_piece(): lax.all_gather(jnp.concatenate([e, r], axis=0), 'fsdp', axis=0, tiled=Tru...]
    pallas_call x0 -> x12, Pallas kernels: none -> 193 us  [call(): pl.pallas_call(kernel, out_shape=[jax.ShapeDtypeStruct(shape, dtype) for...]
    ppermute x0 -> x48, waiting for transfers between devices: none -> 169 us  [the longest x22 87 us: via_second(): return lax.ppermute(x, both_axes, second)]
    unnamed x31 -> x10, waiting for transfers between devices: 146 us -> 0.16 us
    unnamed x323 -> x108, local copies, waits for them, and re-layouts: 83.4 us -> 7.67 us
    ppermute x0 -> x48, starting transfers between devices: none -> 60.2 us  [the longest x12 23.1 us: via_core(): return lax.ppermute(x, both_axes, cores)]
  transfers between devices with their start and end apart: 25 -> 61, of which waited for: 18 -> 26; matrix products, arithmetic and copies ran while one was open for 23% -> 11% of each run, Pallas kernels for 0% -> 23%
where the time goes in v1:
time: 607 us; the launch traced here: 597 us
  waiting for transfers between devices  198 us (33%)
  Pallas kernels  193 us (32%)
  starting transfers between devices  72.6 us (12%)
  other arithmetic  49 us (8%)
  local copies, waits for them, and re-layouts  35.8 us (6%)
  blocking collectives  33.2 us (5%)
  between operations  15.3 us (3%)
    pallas_call x12, Pallas kernels, call(): pl.pallas_call(kernel, out_shape=[jax.ShapeDtypeStruct(shape, dtype) for...  193 us
    ppermute x22, waiting for transfers between devices, via_second(): return lax.ppermute(x, both_axes, second)  87 us
    ppermute x14, waiting for transfers between devices, via_first(): return lax.ppermute(x, both_axes, first)  82 us
    reduce_scatter x2, waiting for transfers between devices, on_device_fast(): lax.psum_scatter((sum_ta[0] + over).astype(BF), 'fsdp', scatter_dimension...  23.6 us
    ppermute x12, starting transfers between devices, via_core(): return lax.ppermute(x, both_axes, cores)  23.1 us
    ppermute x22, starting transfers between devices, via_second(): return lax.ppermute(x, both_axes, second)  22.8 us
    all_gather x1, blocking collectives, on_device_fast(): lax.all_gather(packed.reshape(1, -1), 'fsdp', axis=0, tiled=True)  15.4 us
    ppermute x14, starting transfers between devices, via_first(): return lax.ppermute(x, both_axes, first)  14.4 us
  transfers between devices with their start and end apart: 61, of which 26 were waited for; matrix products, arithmetic and copies ran while one was open for 11% of the time, Pallas kernels for 23%

profile of v1, /device:TPU:1, one launch (start us, length us, event | category | flops | bytes accessed | tf_op | source)
XLA Modules:
  0.0 597.4 jit_solution(3109318494111184366)
XLA Ops:
  20.4 15.4 %all-gather.1 = bf16[8,1,2304]{2,1,0:T(2,128)(2,1)S(1)} all-gather(bf16[1,1,2304]{2,1,0:T(2,128)(2,1)S(1)} %reshape.228), channel_id=1, replica_groups=mesh['ctx'=4,'fsdp'=8] {'fsdp'}, dimensions={0}, use_global_device_ids=true | all-gather | bytes 41472 | tf_op jit(solution)/shard_map/all_gather | solution.py:847
  36.0 5.7 all-gather
  47.3 22.3 %collective-permute-done.3.a = bf16[4,2,96,768]{3,2,1,0:T(8,128)(2,1)S(1)} collective-permute-done((bf16[4,2,96,768]{3,2,1,0:T(8,128)(2,1)}, bf16[4,2,96,768]{3,2,1,0:T(8,128)(2,1)S(1)}, u32[]{:S(2)}, u32[]{:S(2)}) %collective-permute-start.3) | collective-permute-done | bytes 1179680 | tf_op jit(solution)/shard_map/ppermute | solution.py:814
  76.1 5.5 collective-permute-start.6
  81.8 19.1 %collective-permute-done.2.h3 = bf16[384,768]{1,0:T(8,128)(2,1)} collective-permute-done((bf16[384,768]{1,0:T(8,128)(2,1)}, bf16[384,768]{1,0:T(8,128)(2,1)}, u32[]{:S(2)}, u32[]{:S(2)}) %collective-permute-start.2) | collective-permute-done | bytes 589856 | tf_op jit(solution)/shard_map/ppermute | solution.py:817
  100.9 8.5 %collective-permute-start.7 = (bf16[4,2,96,768]{3,2,1,0:T(8,128)(2,1)S(1)}, bf16[4,2,96,768]{3,2,1,0:T(8,128)(2,1)}, u32[]{:S(2)}, u32[]{:S(2)}) collective-permute-start(bf16[4,2,96,768]{3,2,1,0:T(8,128)(2,1)S(1)} %collective-permute-done.3.a), channel_id=1, source_target_pairs={{0,1},{1,0},{2,3},{3,2},{4,5},{5,4},{6,7},{7,6},{8,9},{9,8},{10,11... | collective-permute-start | bytes 3538952 | tf_op jit(solution)/shard_map/ppermute | solution.py:820
  114.7 24.0 %attn_fwd.2 = (bf16[4,384,576]{2,1,0:T(8,128)(2,1)}, bf16[4,192,384]{2,1,0:T(8,128)(2,1)}, f32[8,1536]{1,0:T(8,128)}) custom-call(s32[4]{0:T(128)} %and_select_fusion.1.jmap, s32[4]{0:T(128)} %copy-done.37, s32[6]{0:T(128)} %and_select_fusion.jmin, bf16[384,768]{1,0:T(8,128)(2,1)} %bitcast.6.h0, bf16[384,768]{1,0:T(8,128)(2,1)} %collective-permute-done.h1, ...), custom_call_target="tpu_custom_call" | custom-call | flops 5435817984 | bytes 10485760 | tf_op jit(solution)/shard_map/attn_fwd/pallas_call | solution.py:447
  138.7 4.2 all-to-all-start
  151.7 12.1 %mlp_fwd.2 = (bf16[384,768]{1,0:T(8,128)(2,1)}, f32[384,768]{1,0:T(8,128)}, f32[384,1]{1,0:T(8,128)}, bf16[384,768]{1,0:T(8,128)(2,1)}, bf16[384,3072]{1,0:T(8,1...) custom-call(s32[1]{0:T(128)} %bitcast.core_ref, ...), custom_call_target="tpu_custom_call" | custom-call | flops 4076863488 | bytes 20971520 | tf_op jit(solution)/shard_map/mlp_fwd/pallas_call | solution.py:447
  165.3 14.3 %collective-permute-done.10.h1 = bf16[384,768]{1,0:T(8,128)(2,1)S(1)} collective-permute-done((bf16[384,768]{1,0:T(8,128)(2,1)}, bf16[384,768]{1,0:T(8,128)(2,1)S(1)}, u32[]{:S(2)}, u32[]{:S(2)}) %collective-permute-start.10) | collective-permute-done | bytes 589856 | tf_op jit(solution)/shard_map/ppermute | solution.py:814
  184.1 5.9 collective-permute-done.11.h2
  191.0 5.2 collective-permute-done.12.h3
  197.1 23.5 %attn_fwd.3 = (bf16[4,384,576]{2,1,0:T(8,128)(2,1)}, bf16[4,192,384]{2,1,0:T(8,128)(2,1)}, f32[8,1536]{1,0:T(8,128)}) custom-call(s32[4]{0:T(128)} %and_select_fusion.1.jmap, s32[4]{0:T(128)} %copy-done.37, s32[6]{0:T(128)} %and_select_fusion.jmin, bf16[384,768]{1,0:T(8,128)(2,1)} %get-tuple-element.79.h0, bf16[384,768]{1,0:T(8,128)(2,1)} %copy-done.39, ...), custom_call_target="tpu_custom_call" | custom-call | flops 5435817984 | bytes 10485760 | tf_op jit(solution)/shard_map/attn_fwd/pallas_call | solution.py:447
  220.6 4.1 all-to-all-start.1
  233.3 12.1 %mlp_fwd.3 = (bf16[384,768]{1,0:T(8,128)(2,1)}, f32[384,768]{1,0:T(8,128)}, f32[384,1]{1,0:T(8,128)}, bf16[384,768]{1,0:T(8,128)(2,1)}, bf16[384,3072]{1,0:T(8,1...) custom-call(s32[1]{0:T(128)} %bitcast.core_ref, ...), custom_call_target="tpu_custom_call" | custom-call | flops 4076863488 | bytes 20971520 | tf_op jit(solution)/shard_map/mlp_fwd/pallas_call | solution.py:447
  245.4 11.7 %mlp_bwd.2 = (f32[384,768]{1,0:T(8,128)}, bf16[384,768]{1,0:T(8,128)(2,1)}, bf16[384,768]{1,0:T(8,128)(2,1)}, bf16[384,3072]{1,0:T(8,128)(2,1)}, bf16[4,192,384]...) custom-call(s32[1]{0:T(128)} %bitcast.core_ref, s32[4]{0:T(128)} %pad_add_fusion.1.rk, f32[384,768]{1,0:T(8,128)} %bitcast_convert_fusion.gh, ...), custom_call_target="tpu_custom_call" | custom-call | flops 4076863488 | bytes 20971520 | tf_op jit(solution)/shard_map/mlp_bwd/pallas_call | solution.py:447
  257.1 12.1 %all_to_all.20.gctx = bf16[4,192,384]{2,1,0:T(8,128)(2,1)} all-to-all(bf16[4,192,384]{2,1,0:T(8,128)(2,1)} %get-tuple-element.90), channel_id=1, replica_groups=mesh['ctx'=4,'fsdp'=8] {'ctx'}, dimensions={0} | all-to-all | bytes 1179648 | tf_op jit(solution)/shard_map/all_to_all | solution.py:940
  269.2 27.9 %attn_bwd.2 = (f32[384,768]{1,0:T(8,128)}, bf16[384,768]{1,0:T(8,128)(2,1)}, bf16[2,384,768]{2,1,0:T(8,128)(2,1)}, bf16[8,112,576]{2,1,0:T(8,128)(2,1)}) custom-call(s32[4]{0:T(128)} %and_select_fusion.1.jmap, s32[4]{0:T(128)} %copy-done.37, s32[6]{0:T(128)} %and_select_fusion.jmin, bf16[384,768]{1,0:T(8,128)(2,1)} %get-tuple-element.79.h0, ...), custom_call_target="tpu_custom_call" | custom-call | flops 10871635968 | bytes 10485760 | tf_op jit(solution)/shard_map/attn_bwd/pallas_call | solution.py:447
  298.2 14.6 %collective-permute-done.20 = bf16[2,384,768]{2,1,0:T(8,128)(2,1)S(1)} collective-permute-done((bf16[2,384,768]{2,1,0:T(8,128)(2,1)}, bf16[2,384,768]{2,1,0:T(8,128)(2,1)S(1)}, u32[]{:S(2)}, u32[]{:S(2)}) %collective-permute-start.20) | collective-permute-done | bytes 1179680 | tf_op jit(solution)/shard_map/ppermute | solution.py:817
  314.9 17.1 %wgrad.3 = (bf16[2,4,2,96,768]{4,3,2,1,0:T(8,128)(2,1)}, bf16[2,4,2,96,768]{4,3,2,1,0:T(8,128)(2,1)}, bf16[2,4,2,96,768]{4,3,2,1,0:T(8,128)(2,1)}, bf16[2,4,2,96...) custom-call(s32[1]{0:T(128)} %bitcast.core_ref, bf16[384,768]{1,0:T(8,128)(2,1)} %get-tuple-element.121.lown, ...), custom_call_target="tpu_custom_call" | custom-call | flops 4076863488 | bytes 20971520 | tf_op jit(solution)/shard_map/wgrad/pallas_call | solution.py:447
  338.1 11.7 %mlp_bwd.3 = (f32[384,768]{1,0:T(8,128)}, bf16[384,768]{1,0:T(8,128)(2,1)}, bf16[384,768]{1,0:T(8,128)(2,1)}, bf16[384,3072]{1,0:T(8,128)(2,1)}, bf16[4,192,384]...) custom-call(s32[1]{0:T(128)} %bitcast.core_ref, s32[4]{0:T(128)} %pad_add_fusion.1.rk, f32[384,768]{1,0:T(8,128)} %fusion.16.gh, ...), custom_call_target="tpu_custom_call" | custom-call | flops 4076863488 | bytes 20971520 | tf_op jit(solution)/shard_map/mlp_bwd/pallas_call | solution.py:447
  354.7 17.1 %wgrad.2 = (bf16[2,4,2,96,768]{4,3,2,1,0:T(8,128)(2,1)}, bf16[2,4,2,96,768]{4,3,2,1,0:T(8,128)(2,1)}, bf16[2,4,2,96,768]{4,3,2,1,0:T(8,128)(2,1)}, bf16[2,4,2,96...) custom-call(s32[1]{0:T(128)} %bitcast.core_ref, bf16[384,768]{1,0:T(8,128)(2,1)} %get-tuple-element.107.lown, ...), custom_call_target="tpu_custom_call" | custom-call | flops 4076863488 | bytes 20971520 | tf_op jit(solution)/shard_map/wgrad/pallas_call | solution.py:447
  372.6 28.1 %attn_bwd.3 = (f32[384,768]{1,0:T(8,128)}, bf16[384,768]{1,0:T(8,128)(2,1)}, bf16[2,384,768]{2,1,0:T(8,128)(2,1)}, bf16[8,112,576]{2,1,0:T(8,128)(2,1)}) custom-call(s32[4]{0:T(128)} %and_select_fusion.1.jmap, s32[4]{0:T(128)} %copy-done.37, s32[6]{0:T(128)} %and_select_fusion.jmin, bf16[384,768]{1,0:T(8,128)(2,1)} %bitcast.6.h0, ...), custom_call_target="tpu_custom_call" | custom-call | flops 10871635968 | bytes 10485760 | tf_op jit(solution)/shard_map/attn_bwd/pallas_call | solution.py:447
  400.8 3.8 add_convert_fusion
  411.5 21.4 %collective-permute-done.38 = bf16[2,4,2,96,768]{4,3,2,1,0:T(8,128)(2,1)} collective-permute-done((bf16[2,4,2,96,768]{4,3,2,1,0:T(8,128)(2,1)}, bf16[2,4,2,96,768]{4,3,2,1,0:T(8,128)(2,1)}, u32[]{:S(2)}, u32[]{:S(2)}) %collective-permute-start.38) | collective-permute-done | bytes 2359328 | tf_op jit(solution)/shard_map/ppermute | solution.py:817
  443.4 27.8 %collective-permute-done.43.win1 = bf16[112,576]{1,0:T(8,128)(2,1)} collective-permute-done((bf16[112,576]{1,0:T(8,128)(2,1)}, bf16[112,576]{1,0:T(8,128)(2,1)}, u32[]{:S(2)}, u32[]{:S(2)}) %collective-permute-start.43) | collective-permute-done | bytes 129056 | tf_op jit(solution)/shard_map/ppermute | solution.py:814
  480.7 4.1 convert_add_fusion.1
  487.3 6.9 %collective-permute-done.22 = bf16[2,384,768]{2,1,0:T(8,128)(2,1)S(1)} collective-permute-done((bf16[2,384,768]{2,1,0:T(8,128)(2,1)}, bf16[2,384,768]{2,1,0:T(8,128)(2,1)S(1)}, u32[]{:S(2)}, u32[]{:S(2)}) %collective-permute-start.22) | collective-permute-done | bytes 1179680 | tf_op jit(solution)/shard_map/ppermute | solution.py:817
  497.8 10.2 %collective-permute-done.27 = bf16[4,2,96,768]{3,2,1,0:T(8,128)(2,1)S(1)} collective-permute-done((bf16[4,2,96,768]{3,2,1,0:T(8,128)(2,1)S(1)}, bf16[4,2,96,768]{3,2,1,0:T(8,128)(2,1)S(1)}, u32[]{:S(2)}, u32[]{:S(2)}) %collective-permute-start.27) | collective-permute-done | bytes 1179680 | tf_op jit(solution)/shard_map/ppermute | solution.py:814
  534.0 23.5 %reduce-scatter.7.cloned.1.call-done = bf16[1,2,96,768]{3,2,1,0:T(8,128)(2,1)} async-done(((bf16[4,2,96,768]{3,2,1,0:T(8,128)(2,1)}), bf16[1,2,96,768]{3,2,1,0:T(8,128)(2,1)}) %reduce-scatter.7.cloned.1.call-update) | async-done | bytes 294928 | tf_op jit(solution)/shard_map/reduce_scatter | solution.py:983
  572.0 3.9 place.3
  578.3 3.9 place.2
  (340 shorter events, 154.2 us)
Async XLA Ops:
  7.2 37.2 %all-gather.11.cloned.1.call-start = ((), (), s32[]{:S(2)}) async-start(), calls=%async_computation.12 | async-start | bytes 1474560 | tf_op jit(solution)/shard_map/all_gather | solution.py:866
  11.6 70.0 %all-gather.13.cloned.1.call-start = ((), (), s32[]{:S(2)}) async-start(), calls=%async_computation.13 | async-start | bytes 1474560 | tf_op jit(solution)/shard_map/all_gather | solution.py:866
  14.7 95.2 %all-gather.7.cloned.1.call-start = ((), (), s32[]{:S(2)}) async-start(), calls=%async_computation.10 | async-start | bytes 2211840 | tf_op jit(solution)/shard_map/all_gather | solution.py:874
  16.6 128.8 %all-gather.9.cloned.1.call-start = ((), (), s32[]{:S(2)}) async-start(), calls=%async_computation.11 | async-start | bytes 2654208 | tf_op jit(solution)/shard_map/all_gather | solution.py:876
  16.7 65.0 %collective-permute-start.1 = (bf16[384,768]{1,0:T(8,128)(2,1)}, bf16[384,768]{1,0:T(8,128)(2,1)S(1)}, u32[]{:S(2)}, u32[]{:S(2)}) collective-permute-start(bf16[384,768]{1,0:T(8,128)(2,1)} %bitcast.6.h0), channel_id=1, source_target_pairs={{0,16},{1,9},{2,18},{3,11},{4,20},{5,13},{6,22},{7,15},{8,24},{9,1... | collective-permute-start | bytes 1769480 | tf_op jit(solution)/shard_map/ppermute | solution.py:817
  18.8 53.9 %collective-permute-start = (bf16[384,768]{1,0:T(8,128)(2,1)}, bf16[384,768]{1,0:T(8,128)(2,1)}, u32[]{:S(2)}, u32[]{:S(2)}) collective-permute-start(bf16[384,768]{1,0:T(8,128)(2,1)} %bitcast.6.h0), channel_id=1, source_target_pairs={{0,8},{1,17},{2,10},{3,19},{4,12},{5,21},{6,14},{7,23},{8,0},{9,25... | collective-permute-start | bytes 1769480 | tf_op jit(solution)/shard_map/ppermute | solution.py:814
  45.8 63.6 %collective-permute-start.4 = (bf16[4,2,96,768]{3,2,1,0:T(8,128)(2,1)}, bf16[4,2,96,768]{3,2,1,0:T(8,128)(2,1)}, u32[]{:S(2)}, u32[]{:S(2)}) collective-permute-start(bf16[4,2,96,768]{3,2,1,0:T(8,128)(2,1)} %bitcast.158), channel_id=1, source_target_pairs={{0,16},{1,9},{2,18},{3,11},{4,20},{5,13},{6,22},{7,15},{8,24},{9,1... | collective-permute-start | bytes 3538952 | tf_op jit(solution)/shard_map/ppermute | solution.py:817
  69.6 39.9 %collective-permute-start.5 = (bf16[4,2,96,768]{3,2,1,0:T(8,128)(2,1)S(1)}, bf16[4,2,96,768]{3,2,1,0:T(8,128)(2,1)}, u32[]{:S(2)}, u32[]{:S(2)}) collective-permute-start(bf16[4,2,96,768]{3,2,1,0:T(8,128)(2,1)S(1)} %collective-permute-done.3.a), channel_id=1, source_target_pairs={{0,16},{1,9},{2,18},{3,11},{4,20},{5,13},{6,22},{7,15},{8,24},{9,1... | collective-permute-start | bytes 3538952 | tf_op jit(solution)/shard_map/ppermute | solution.py:817
  76.1 72.6 %collective-permute-start.6 = (bf16[4,2,96,768]{3,2,1,0:T(8,128)(2,1)S(1)}, bf16[4,2,96,768]{3,2,1,0:T(8,128)(2,1)}, u32[]{:S(2)}, u32[]{:S(2)}) collective-permute-start(bf16[4,2,96,768]{3,2,1,0:T(8,128)(2,1)S(1)} %bitcast.161), channel_id=1, source_target_pairs={{0,1},{1,0},{2,3},{3,2},{4,5},{5,4},{6,7},{7,6},{8,9},{9,8},{10,11... | collective-permute-start | bytes 3538952 | tf_op jit(solution)/shard_map/ppermute | solution.py:820
  81.7 68.6 %collective-permute-start.13 = (bf16[4,2,96,768]{3,2,1,0:T(8,128)(2,1)}, bf16[4,2,96,768]{3,2,1,0:T(8,128)(2,1)}, u32[]{:S(2)}, u32[]{:S(2)}) collective-permute-start(bf16[4,2,96,768]{3,2,1,0:T(8,128)(2,1)} %bitcast.162), channel_id=1, source_target_pairs={{0,8},{1,17},{2,10},{3,19},{4,12},{5,21},{6,14},{7,23},{8,0},{9,25... | collective-permute-start | bytes 3538952 | tf_op jit(solution)/shard_map/ppermute | solution.py:814
  100.9 50.8 %collective-permute-start.7 = (bf16[4,2,96,768]{3,2,1,0:T(8,128)(2,1)S(1)}, bf16[4,2,96,768]{3,2,1,0:T(8,128)(2,1)}, u32[]{:S(2)}, u32[]{:S(2)}) collective-permute-start(bf16[4,2,96,768]{3,2,1,0:T(8,128)(2,1)S(1)} %collective-permute-done.3.a), channel_id=1, source_target_pairs={{0,1},{1,0},{2,3},{3,2},{4,5},{5,4},{6,7},{7,6},{8,9},{9,8},{10,11... | collective-permute-start | bytes 3538952 | tf_op jit(solution)/shard_map/ppermute | solution.py:820
  109.4 42.3 %collective-permute-start.8 = (bf16[4,2,96,768]{3,2,1,0:T(8,128)(2,1)}, bf16[4,2,96,768]{3,2,1,0:T(8,128)(2,1)}, u32[]{:S(2)}, u32[]{:S(2)}) collective-permute-start(bf16[4,2,96,768]{3,2,1,0:T(8,128)(2,1)} %collective-permute-done.4.b), channel_id=1, source_target_pairs={{0,1},{1,0},{2,3},{3,2},{4,5},{5,4},{6,7},{7,6},{8,9},{9,8},{10,11... | collective-permute-start | bytes 3538952 | tf_op jit(solution)/shard_map/ppermute | solution.py:820
  109.4 42.3 %collective-permute-start.9 = (bf16[4,2,96,768]{3,2,1,0:T(8,128)(2,1)}, bf16[4,2,96,768]{3,2,1,0:T(8,128)(2,1)}, u32[]{:S(2)}, u32[]{:S(2)}) collective-permute-start(bf16[4,2,96,768]{3,2,1,0:T(8,128)(2,1)} %collective-permute-done.5.d), channel_id=1, source_target_pairs={{0,1},{1,0},{2,3},{3,2},{4,5},{5,4},{6,7},{7,6},{8,9},{9,8},{10,11... | collective-permute-start | bytes 3538952 | tf_op jit(solution)/shard_map/ppermute | solution.py:820
  148.8 34.2 %collective-permute-start.14 = (bf16[4,2,96,768]{3,2,1,0:T(8,128)(2,1)S(1)}, bf16[4,2,96,768]{3,2,1,0:T(8,128)(2,1)S(1)}, u32[]{:S(2)}, u32[]{:S(2)}) collective-permute-start(bf16[4,2,96,768]{3,2,1,0:T(8,128)(2,1)S(1)} %bitcast.165), channel_id=1, source_target_pairs={{0,16},{1,9},{2,18},{3,11},{4,20},{5,13},{6,22},{7,15},{8,24},{9,1... | collective-permute-start | bytes 3538952 | tf_op jit(solution)/shard_map/ppermute | solution.py:817
  150.2 33.6 %collective-permute-start.15 = (bf16[4,2,96,768]{3,2,1,0:T(8,128)(2,1)}, bf16[4,2,96,768]{3,2,1,0:T(8,128)(2,1)}, u32[]{:S(2)}, u32[]{:S(2)}) collective-permute-start(bf16[4,2,96,768]{3,2,1,0:T(8,128)(2,1)} %collective-permute-done.13.a), channel_id=1, source_target_pairs={{0,16},{1,9},{2,18},{3,11},{4,20},{5,13},{6,22},{7,15},{8,24},{9,1... | collective-permute-start | bytes 3538952 | tf_op jit(solution)/shard_map/ppermute | solution.py:817
  180.8 50.4 %collective-permute-start.16 = (bf16[4,2,96,768]{3,2,1,0:T(8,128)(2,1)S(1)}, bf16[4,2,96,768]{3,2,1,0:T(8,128)(2,1)S(1)}, u32[]{:S(2)}, u32[]{:S(2)}) collective-permute-start(bf16[4,2,96,768]{3,2,1,0:T(8,128)(2,1)S(1)} %bitcast.166), channel_id=1, source_target_pairs={{0,1},{1,0},{2,3},{3,2},{4,5},{5,4},{6,7},{7,6},{8,9},{9,8},{10,11... | collective-permute-start | bytes 3538952 | tf_op jit(solution)/shard_map/ppermute | solution.py:820
  183.0 48.2 %collective-permute-start.17 = (bf16[4,2,96,768]{3,2,1,0:T(8,128)(2,1)}, bf16[4,2,96,768]{3,2,1,0:T(8,128)(2,1)}, u32[]{:S(2)}, u32[]{:S(2)}) collective-permute-start(bf16[4,2,96,768]{3,2,1,0:T(8,128)(2,1)} %collective-permute-done.13.a), channel_id=1, source_target_pairs={{0,1},{1,0},{2,3},{3,2},{4,5},{5,4},{6,7},{7,6},{8,9},{9,8},{10,11... | collective-permute-start | bytes 3538952 | tf_op jit(solution)/shard_map/ppermute | solution.py:820
  183.8 47.4 %collective-permute-start.18 = (bf16[4,2,96,768]{3,2,1,0:T(8,128)(2,1)S(1)}, bf16[4,2,96,768]{3,2,1,0:T(8,128)(2,1)}, u32[]{:S(2)}, u32[]{:S(2)}) collective-permute-start(bf16[4,2,96,768]{3,2,1,0:T(8,128)(2,1)S(1)} %collective-permute-done.14.b), channel_id=1, source_target_pairs={{0,1},{1,0},{2,3},{3,2},{4,5},{5,4},{6,7},{7,6},{8,9},{9,8},{10,11... | collective-permute-start | bytes 3538952 | tf_op jit(solution)/shard_map/ppermute | solution.py:820
  190.1 41.2 %collective-permute-start.19 = (bf16[4,2,96,768]{3,2,1,0:T(8,128)(2,1)}, bf16[4,2,96,768]{3,2,1,0:T(8,128)(2,1)}, u32[]{:S(2)}, u32[]{:S(2)}) collective-permute-start(bf16[4,2,96,768]{3,2,1,0:T(8,128)(2,1)} %collective-permute-done.15.d), channel_id=1, source_target_pairs={{0,1},{1,0},{2,3},{3,2},{4,5},{5,4},{6,7},{7,6},{8,9},{9,8},{10,11... | collective-permute-start | bytes 3538952 | tf_op jit(solution)/shard_map/ppermute | solution.py:820
  224.8 216.3 %reduce-scatter.15.cloned.1.call-start = ((), (), s32[]{:S(2)}) async-start(), calls=%async_computation.18 | async-start | bytes 1290240 | tf_op jit(solution)/shard_map/reduce_scatter | solution.py:986
  297.2 178.8 %reduce-scatter.17.cloned.1.call-start = ((), (), s32[]{:S(2)}) async-start(), calls=%async_computation.19 | async-start | bytes 1548288 | tf_op jit(solution)/shard_map/reduce_scatter | solution.py:987
  332.0 68.8 %collective-permute-start.37 = (bf16[2,4,2,96,768]{4,3,2,1,0:T(8,128)(2,1)}, bf16[2,4,2,96,768]{4,3,2,1,0:T(8,128)(2,1)}, u32[]{:S(2)}, u32[]{:S(2)}) collective-permute-start(bf16[2,4,2,96,768]{4,3,2,1,0:T(8,128)(2,1)} %get-tuple-element.131), channel_id=1, source_target_pairs={{0,1},{1,0},{2,3},{3,2},{4,5},{5,4},{6,7},{7,6},{8,9},{9,8},{10,11... | collective-permute-start | bytes 7077896 | tf_op jit(solution)/shard_map/ppermute | solution.py:820
  353.4 156.1 %reduce-scatter.9.cloned.1.call-start = ((), (), s32[]{:S(2)}) async-start(), calls=%async_computation.15 | async-start | bytes 1290240 | tf_op jit(solution)/shard_map/reduce_scatter | solution.py:986
  353.4 58.1 %collective-permute-start.36 = (bf16[2,4,2,96,768]{4,3,2,1,0:T(8,128)(2,1)}, bf16[2,4,2,96,768]{4,3,2,1,0:T(8,128)(2,1)}, u32[]{:S(2)}, u32[]{:S(2)}) collective-permute-start(bf16[2,4,2,96,768]{4,3,2,1,0:T(8,128)(2,1)} %get-tuple-element.129), channel_id=1, source_target_pairs={{0,1},{1,0},{2,3},{3,2},{4,5},{5,4},{6,7},{7,6},{8,9},{9,8},{10,11... | collective-permute-start | bytes 7077896 | tf_op jit(solution)/shard_map/ppermute | solution.py:820
  371.8 35.3 %collective-permute-start.25 = (bf16[2,4,2,96,768]{4,3,2,1,0:T(8,128)(2,1)}, bf16[2,4,2,96,768]{4,3,2,1,0:T(8,128)(2,1)}, u32[]{:S(2)}, u32[]{:S(2)}) collective-permute-start(bf16[2,4,2,96,768]{4,3,2,1,0:T(8,128)(2,1)} %get-tuple-element.117), channel_id=1, source_target_pairs={{0,1},{1,0},{2,3},{3,2},{4,5},{5,4},{6,7},{7,6},{8,9},{9,8},{10,11... | collective-permute-start | bytes 7077896 | tf_op jit(solution)/shard_map/ppermute | solution.py:820
  400.7 120.9 %reduce-scatter.11.cloned.1.call-start = ((), (), s32[]{:S(2)}) async-start(), calls=%async_computation.16 | async-start | bytes 1548288 | tf_op jit(solution)/shard_map/reduce_scatter | solution.py:987
  406.1 74.6 %collective-permute-start.24 = (bf16[2,4,2,96,768]{4,3,2,1,0:T(8,128)(2,1)}, bf16[2,4,2,96,768]{4,3,2,1,0:T(8,128)(2,1)}, u32[]{:S(2)}, u32[]{:S(2)}) collective-permute-start(bf16[2,4,2,96,768]{4,3,2,1,0:T(8,128)(2,1)} %get-tuple-element.115), channel_id=1, source_target_pairs={{0,1},{1,0},{2,3},{3,2},{4,5},{5,4},{6,7},{7,6},{8,9},{9,8},{10,11... | collective-permute-start | bytes 7077896 | tf_op jit(solution)/shard_map/ppermute | solution.py:820
  407.0 125.8 %reduce-scatter.13.cloned.1.call-start = ((), (), s32[]{:S(2)}) async-start(), calls=%async_computation.17 | async-start | bytes 1474560 | tf_op jit(solution)/shard_map/reduce_scatter | solution.py:983
  410.3 70.4 %collective-permute-start.26 = (bf16[2,4,2,96,768]{4,3,2,1,0:T(8,128)(2,1)S(1)}, bf16[2,4,2,96,768]{4,3,2,1,0:T(8,128)(2,1)}, u32[]{:S(2)}, u32[]{:S(2)}) collective-permute-start(bf16[2,4,2,96,768]{4,3,2,1,0:T(8,128)(2,1)S(1)} %add_convert_fusion.1), channel_id=1, source_target_pairs={{0,16},{1,9},{2,18},{3,11},{4,20},{5,13},{6,22},{7,15},{8,24},{9,1... | collective-permute-start | bytes 7077896 | tf_op jit(solution)/shard_map/ppermute | solution.py:817
  439.7 36.3 %collective-permute-start.39 = (bf16[4,2,96,768]{3,2,1,0:T(8,128)(2,1)}, bf16[4,2,96,768]{3,2,1,0:T(8,128)(2,1)}, u32[]{:S(2)}, u32[]{:S(2)}) collective-permute-start(bf16[4,2,96,768]{3,2,1,0:T(8,128)(2,1)} %fusion.5), channel_id=1, source_target_pairs={{0,8},{1,17},{2,10},{3,19},{4,12},{5,21},{6,14},{7,23},{8,0},{9,25... | collective-permute-start | bytes 3538952 | tf_op jit(solution)/shard_map/ppermute | solution.py:814
  441.2 32.7 %collective-permute-start.44 = (bf16[112,576]{1,0:T(8,128)(2,1)}, bf16[112,576]{1,0:T(8,128)(2,1)S(1)}, u32[]{:S(2)}, u32[]{:S(2)}) collective-permute-start(bf16[112,576]{1,0:T(8,128)(2,1)} %bitcast.191), channel_id=1, source_target_pairs={{0,16},{1,9},{2,18},{3,11},{4,20},{5,13},{6,22},{7,15},{8,24},{9,1... | collective-permute-start | bytes 387080 | tf_op jit(solution)/shard_map/ppermute | solution.py:817
  480.5 77.1 %reduce-scatter.7.cloned.1.call-start = ((), (), s32[]{:S(2)}) async-start(), calls=%async_computation.14 | async-start | bytes 1474560 | tf_op jit(solution)/shard_map/reduce_scatter | solution.py:983
  (79 other events, 1147.9 us)
Sparse Core Ops, SparseCore 0:
  11.8 32.5 all-gather.10
  46.5 29.4 all-gather.12
  78.2 28.0 all-gather.6
  107.9 31.1 all-gather.8
  297.3 36.2 reduce-scatter.14
  336.3 42.1 reduce-scatter.16
  400.8 47.6 reduce-scatter.8
  450.9 30.3 reduce-scatter.10
  484.2 42.6 reduce-scatter.12
  529.6 27.8 reduce-scatter.6

commit v2 on v1

--- a/solution.py
+++ b/solution.py
@@ -451,7 +451,7 @@
         out_specs=[pl.BlockSpec(memory_space=pltpu.VMEM) for _ in outs],
         scratch_shapes=scratch,
         compiler_params=pltpu.CompilerParams(vmem_limit_bytes=VMEM_LIMIT),
-        cost_estimate=pl.CostEstimate(flops=flops, bytes_accessed=nbytes, transcendentals=0),
+        cost_estimate=pl.CostEstimate(flops=0, bytes_accessed=0, transcendentals=0),
         name=name,
     )(*args)
 
@@ -461,18 +461,181 @@
     return (block if half == 0 else blocks - 1 - block), half
 
 
+CORE, SHARD, RANK, JMAP, INV, JMIN = 0, 1, 2, 6, 10, 14
+SWAPPED = (0, 2, 1, 3)
+VEC_AT = 640
+
+
+def started_copies(sems, *pairs):
+    copies = []
+    for n, (src, dst) in enumerate(pairs):
+        copy = pltpu.make_async_copy(src, dst, sems.at[n])
+        copy.start()
+        copies.append(copy)
+    return copies
+
+
+def prep_kernel(
+    expand, reduce, attend_in, attend_out, expand_bias, v0, v1, v2, v3, v4, v5, v6, v7,
+    t0, d0, t1, d1,
+):
+    rank = lax.axis_index("ctx")
+    cut = expand.shape[1]
+    hw = WIDTH // 4
+    for layer, (t, d) in enumerate(((t0, d0), (t1, d1))):
+        bias = expand_bias[layer : layer + 1, :].astype(F32)
+        rows = [v[layer : layer + 1, :].astype(F32) for v in (v0, v1, v2, v3, v4, v5, v6, v7)]
+        rows += [bias[:, k * cut : (k + 1) * cut] for k in range(4)]
+        rows.append(jnp.zeros((4, cut), F32))
+        d[2 * cut :, :] = attend_out[layer]
+        t[2 * cut :, 3 * hw :] = jnp.zeros((cut, WIDTH - 3 * hw), BF)
+        t[2 * cut : 2 * cut + 16, VEC_AT : VEC_AT + cut] = jnp.concatenate(rows, axis=0).astype(BF)
+        for k in range(4):
+
+            @pl.when(rank == k)
+            def _():
+                for out, at in ((t, k), (d, k ^ 3)):
+                    out[0:cut, :] = jnp.concatenate(
+                        [
+                            expand[layer, :, (2 * z + h) * 4 * cut + at * cut : (2 * z + h) * 4 * cut + (at + 1) * cut]
+                            for h in range(2)
+                            for z in range(4)
+                        ],
+                        axis=1,
+                    )
+                    out[cut : 2 * cut, :] = reduce[layer, at * cut : (at + 1) * cut, :]
+                t[2 * cut :, 0 : 3 * hw] = jnp.concatenate(
+                    [attend_in[layer, :, n * WIDTH + k * hw : n * WIDTH + (k + 1) * hw] for n in range(3)], axis=1
+                )
+
+
+def nothing_kernel(*refs):
+    pass
+
+
+def after(xs, *others):
+    return pl.pallas_call(
+        nothing_kernel,
+        out_shape=[jax.ShapeDtypeStruct(x.shape, x.dtype) for x in xs],
+        in_specs=[pl.BlockSpec(memory_space=pl.ANY)] * (len(xs) + len(others)),
+        out_specs=[pl.BlockSpec(memory_space=pl.ANY)] * len(xs),
+        input_output_aliases={n: n for n in range(len(xs))},
+        name="after",
+    )(*xs, *others)
+
+
+def token_kernel(*refs):
+    refs[-1][...] = jnp.zeros_like(refs[-1])
+
+
+def token(*others):
+    return call(token_kernel, [((8, 128), F32)], others, [pl.ANY] * len(others), [], "token", 0, 0)[0]
+
+
+def pack_kernel(a, b, *rest):
+    out = rest[-1]
+    out[0] = a[...]
+    out[1] = b[...]
+
+
+def pack(a, b, *others):
+    return call(
+        pack_kernel, [((2,) + a.shape, a.dtype)], (a, b) + others, [pltpu.VMEM] * 2 + [pl.ANY] * len(others), [],
+        "pack", 0, 0,
+    )[0]
+
+
+def half_kernel(meta, t, *rest):
+    out, sem = rest[-2:]
+    copy = pltpu.make_async_copy(t.at[:, meta[CORE], 0:2], out, sem)
+    copy.start()
+    copy.wait()
+
+
+def half_of(meta, t, *others):
+    shape = (t.shape[0], 2) + t.shape[3:]
+    return call(
+        half_kernel, [(shape, t.dtype)], (meta, t) + others, [pltpu.SMEM] + [pl.ANY] * (1 + len(others)),
+        [pltpu.SemaphoreType.DMA(())], "half", 0, 0,
+    )[0]
+
+
+def sums_kernel(*refs, layout, count, split):
+    outs = refs[-len(layout) :]
+    at = 0
+    for out, parts in zip(outs, layout):
+        lane = 0
+        for n in parts:
+            total = refs[at][...].astype(F32)
+            for ref in refs[at + 1 : at + n]:
+                total = total + ref[...].astype(F32)
+            at += n
+            if split:
+                for k in range(len(outs)):
+                    outs[k][...] = total[k].astype(BF)
+            else:
+                out[..., lane : lane + total.shape[-1]] = total.astype(BF)
+            lane += total.shape[-1]
+        if split:
+            break
+
+
+def sums(outputs, *others, split=0):
+    args = tuple(x for groups in outputs for group in groups for x in group)
+    layout = tuple(tuple(len(group) for group in groups) for groups in outputs)
+    if split:
+        shapes = [(args[0].shape[1:], BF)] * split
+        layout = layout * split
+    else:
+        shapes = [
+            (groups[0][0].shape[:-1] + (sum(group[0].shape[-1] for group in groups),), BF) for groups in outputs
+        ]
+    return call(
+        functools.partial(sums_kernel, layout=layout, count=len(args), split=split),
+        shapes, args + others, [pltpu.VMEM] * len(args) + [pl.ANY] * len(others), [], "sums", 0, 0,
+    )
+
+
+def merge_kernel(dwo, own, other, *rest):
+    out = rest[-1]
+    out[:, :, 0:WIDTH] = dwo[...]
+    out[:, :, WIDTH:] = (own[...].astype(F32) + other[...].astype(F32)).astype(BF)
+
+
+def vectors_of(shards, order):
+    return jnp.concatenate([shards[f // 2, f % 2, :, 0:96] for f in order], axis=1).astype(F32)
+
+
+NATURAL = tuple(range(8))
+CORE_MAJOR = (0, 2, 4, 6, 1, 3, 5, 7)
+
+
 def attn_fwd_kernel(
-    jmap, inv, jmin, h0, h1, h2, h3, w, bias, qrow, kcol, qkv, ctx, lse, q_s, k_s, vt_s, o_s, *, heads, tokens
+    meta, h0, h1, h2, h3, qrow, kcol, t, *rest, heads, tokens
 ):
+    qkv, c0, c1, c2, c3, lse, q_s, k_s, vt_s, o_s, ctx, w_s, b_s, sems = rest[-14:]
     blocks = tokens // BLK
     hw = heads * HEAD_DIM
+    copies = started_copies(
+        sems, (t.at[:, :, 2, :, 0:VEC_AT], w_s), (t.at[:, :, 2, 0:16, VEC_AT : VEC_AT + 128], b_s)
+    )
+    for copy in copies:
+        copy.wait()
+    w = w_s[...].reshape(WIDTH, VEC_AT)[:, 0 : 3 * hw]
+    vec = vectors_of(b_s, NATURAL)
+    bias = jnp.zeros((1, 3 * hw), F32)
+    for k in range(4):
+        part = jnp.concatenate(
+            [vec[6:7, k * hw : (k + 1) * hw], jnp.zeros((1, hw), F32), vec[7:8, k * hw : (k + 1) * hw]], axis=1
+        )
+        bias = jnp.where(meta[RANK] == k, part, bias)
     for j, piece in enumerate((h0, h1, h2, h3)):
-        qkv[j] = (mm_nn(piece[...], w[...]) + bias[...]).astype(BF)
+        qkv[j] = (mm_nn(piece[...], w) + bias).astype(BF)
     for pair in range(blocks // 2):
         rows = []
         for block in (2 * pair, 2 * pair + 1):
             at, half = block_of(block, blocks)
-            rows.append(qkv[jmap[at], half * BLK : (half + 1) * BLK, :])
+            rows.append(qkv[meta[JMAP + at], half * BLK : (half + 1) * BLK, :])
         both = jnp.concatenate(rows, axis=0)
         lo, hi = 2 * pair * BLK, 2 * (pair + 1) * BLK
         for h in range(heads):
@@ -516,7 +679,7 @@
                 return (new_top, total, out)
 
             if i > 0:
-                top, total, out = lax.fori_loop(jmin[i], i, step, (top, total, out))
+                top, total, out = lax.fori_loop(meta[JMIN + i], i, step, (top, total, out))
             o_s[h * HEAD_DIM : (h + 1) * HEAD_DIM, lo : lo + QB] = out / total
             lse[h : h + 1, lo : lo + QB] = top + jnp.log2(total)
     for pair in range(blocks // 2):
@@ -524,24 +687,30 @@
         both = o_s[:, lo:hi].T.astype(BF)
         for n, block in enumerate((2 * pair, 2 * pair + 1)):
             at, half = block_of(block, blocks)
-            ctx[inv[at], :, half * hw : (half + 1) * hw] = both[n * BLK : (n + 1) * BLK, :]
+            ctx[meta[JMAP + at], :, half * hw : (half + 1) * hw] = both[n * BLK : (n + 1) * BLK, :]
+    for j, out in enumerate((c0, c1, c2, c3)):
+        out[...] = ctx[j]
 
 
 def attn_bwd_kernel(
-    jmap, inv, jmin, h0, h1, h2, h3, w, qrow, kcol, qkv, ctx, gctx, lse,
-    g_own, g_a, g_bd, dw,
-    q_s, k_s, v_s, do_s, kt_s, delta_s, dk_s, dv_s, dqt_s, g_s, *, heads, tokens
+    meta, h0, h1, h2, h3, qrow, kcol, qkv, c0, c1, c2, c3, gctx, lse, t, *rest, heads, tokens
 ):
+    (
+        g_own, g_a, g_b, g_d, dw_own, dw_other, q_s, k_s, v_s, do_s, kt_s, delta_s, dk_s, dv_s, dqt_s, g_s, w_s, ctx, dw, sems,
+    ) = rest[-20:]
     blocks = tokens // BLK
     hw = heads * HEAD_DIM
     scale = HEAD_DIM ** (-0.5)
+    copies = started_copies(sems, (t.at[:, :, 2, :, 0:VEC_AT], w_s))
+    for j, c in enumerate((c0, c1, c2, c3)):
+        ctx[j] = c[...]
     for pair in range(blocks // 2):
         rows, grads, outs = [], [], []
         for block in (2 * pair, 2 * pair + 1):
             at, half = block_of(block, blocks)
-            rows.append(qkv[jmap[at], half * BLK : (half + 1) * BLK, :])
-            grads.append(gctx[inv[at], :, half * hw : (half + 1) * hw])
-            outs.append(ctx[inv[at], :, half * hw : (half + 1) * hw])
+            rows.append(qkv[meta[JMAP + at], half * BLK : (half + 1) * BLK, :])
+            grads.append(gctx[meta[INV + at], :, half * hw : (half + 1) * hw])
+            outs.append(ctx[meta[JMAP + at], :, half * hw : (half + 1) * hw])
         both = jnp.concatenate(rows, axis=0)
         grad = jnp.concatenate(grads, axis=0)
         out = jnp.concatenate(outs, axis=0)
@@ -585,7 +754,7 @@
             dq = block(lo, True)
             if i > 0:
                 dq = lax.fori_loop(
-                    jmin[i], i, lambda jb, acc: acc + block(pl.multiple_of(jb * QB, QB), False), dq
+                    meta[JMIN + i], i, lambda jb, acc: acc + block(pl.multiple_of(jb * QB, QB), False), dq
                 )
             dqt_s[h * HEAD_DIM : (h + 1) * HEAD_DIM, lo : lo + QB] = dq * scale
     for pair in range(blocks // 2):
@@ -596,18 +765,19 @@
         both = jnp.concatenate(parts, axis=1)
         for n, block_at in enumerate((2 * pair, 2 * pair + 1)):
             at, half = block_of(block_at, blocks)
-            g_s[jmap[at], half * BLK : (half + 1) * BLK, :] = both[n * BLK : (n + 1) * BLK, :]
+            g_s[meta[JMAP + at], half * BLK : (half + 1) * BLK, :] = both[n * BLK : (n + 1) * BLK, :]
+    for copy in copies:
+        copy.wait()
+    w = w_s[...].reshape(WIDTH, VEC_AT)[:, 0 : 3 * hw]
     total = None
     sums = None
     for j, piece in enumerate((h0, h1, h2, h3)):
         g = g_s[j]
-        back = mm_nt(g, w[...])
+        back = mm_nt(g, w)
         if j == 0:
             g_own[...] = back
-        elif j == 1:
-            g_a[...] = back.astype(BF)
         else:
-            g_bd[j - 2] = back.astype(BF)
+            (g_a, g_b, g_d)[j - 1][...] = back.astype(BF)
         part = mm_tn(piece[...], g)
         col = jnp.sum(g.astype(F32), axis=0, keepdims=True)
         total = part if total is None else total + part
@@ -615,27 +785,42 @@
     shards, rows_out, cols = dw.shape
     rows = WIDTH // shards
     dw[:, 0:rows, :] = total.reshape(shards, rows, cols).astype(BF)
-    dw[:, rows:rows_out, :] = jnp.broadcast_to(sums[None], (shards, rows_out - rows, cols)).astype(BF)
-
-
-def start_ffn_copies(core, own, other, e_s, r_s, sems):
-    copies = []
-    for p, (mine, theirs) in enumerate(zip(own, (other[0], other[2], other[1], other[3]))):
+    dw[:, rows:, :] = jnp.broadcast_to(sums[None], (shards, rows_out - rows, cols)).astype(BF)
+    for k in range(4):
+        dw_own[k] = dw[2 * k + meta[CORE]]
+        dw_other[k] = dw[2 * k + 1 - meta[CORE]]
+
+
+def start_ffn_copies(core, t, a, b, d, crossed, e_s, r_s, sems):
+    ca, cb = crossed.at[0], crossed.at[1]
+    groups = []
+    for p, parts in enumerate(((t,), (a, cb), (b, ca), (d,))):
+        pairs = []
+        if len(parts) == 1:
+            pairs.append((parts[0].at[:, :, 0], e_s.at[p]))
+            for h in range(2):
+                pairs.append((parts[0].at[:, h, 1], r_s.at[p, h]))
+        else:
+            for src, parity in ((parts[0], core), (parts[1], 1 - core)):
+                pairs.append((src.at[:, 0], e_s.at[p, :, parity]))
+                pairs.append((src.at[:, 1], r_s.at[p, parity]))
         group = []
-        for n, (src, parity) in enumerate(((mine, core), (theirs, 1 - core))):
-            for k, dst in enumerate((e_s, r_s)):
-                copy = pltpu.make_async_copy(src.at[:, k], dst.at[p, :, parity], sems.at[p, 2 * n + k])
-                copy.start()
-                group.append(copy)
-        copies.append(group)
-    return copies
+        for n, (src, dst) in enumerate(pairs):
+            copy = pltpu.make_async_copy(src, dst, sems.at[p, n])
+            copy.start()
+            group.append(copy)
+        groups.append(group)
+    return groups
 
 
 def ffn_scratch():
     return [
         pltpu.VMEM((4, 4, 2, 96, WIDTH), BF),
-        pltpu.VMEM((4, 4, 2, 96, WIDTH), BF),
+        pltpu.VMEM((4, 2, 4, 96, WIDTH), BF),
         pltpu.SemaphoreType.DMA((4, 4)),
+        pltpu.VMEM((4, 2, 96, WIDTH), BF),
+        pltpu.VMEM((4, 2, 16, 128), BF),
+        pltpu.SemaphoreType.DMA((2,)),
     ]
 
 
@@ -646,42 +831,70 @@
     return centre * rstd, rstd
 
 
+def shard_columns(x, parity):
+    return jnp.concatenate([x[:, (2 * z + parity) * 96 : (2 * z + parity + 1) * 96] for z in range(4)], axis=1)
+
+
 def mlp_fwd_kernel(
-    core_ref, rk, cx, hid, wo, vec, eb, t, a, b, d, ct, ca, cb, cd,
-    lowctx, xhat1, rstd1, lown, act, gp, xhat2, rstd2, hnext, hlow,
-    e_s, r_s, sems,
+    meta, c0, c1, c2, c3, hid, t, a, b, d, crossed,
+    xhat1, rstd1, gp, xhat2, rstd2, l_mine, l_other, hlow, *rest,
 ):
-    core = core_ref[0]
-    copies = start_ffn_copies(core, (t, a, b, d), (ct, ca, cb, cd), e_s, r_s, sems)
-    ranks, _, cols = cx.shape
-    hw = cols // 2
-    for s in range(ranks):
+    hnext, (e_s, r_s, sems, wo_s, b_s, wo_sems, ctx, eb) = rest[:-8], rest[-8:]
+    core = meta[CORE]
+    wo_copies = started_copies(
+        wo_sems, (d.at[:, :, 2], wo_s), (t.at[:, :, 2, 0:16, VEC_AT : VEC_AT + 128], b_s)
+    )
+    copies = start_ffn_copies(core, t, a, b, d, crossed, e_s, r_s, sems)
+    half_cols = WIDTH // 2
+    hw = c0.shape[1] // 2
+    for p, piece in enumerate((c0, c1, c2, c3)):
         for half in range(2):
-            lowctx[half * BLK : (half + 1) * BLK, s * hw : (s + 1) * hw] = cx[s, :, half * hw : (half + 1) * hw]
-    first_sum = hid[...] + (mm_nn(lowctx[...], wo[...].reshape(WIDTH, WIDTH)) + vec[0:1, :])
+            ctx[meta[RANK + p], half * BLK : (half + 1) * BLK, :] = piece[:, half * hw : (half + 1) * hw]
+
+    def keep(parts, at):
+        for parity in range(2):
+
+            @pl.when(core == parity)
+            def _():
+                l_mine[:, at : at + half_cols] = parts[parity]
+
+            @pl.when(core != parity)
+            def _():
+                l_other[:, at : at + half_cols] = parts[parity]
+
+    low = jnp.concatenate([ctx[rank] for rank in range(4)], axis=1)
+    keep([shard_columns(low, parity) for parity in range(2)], half_cols)
+    for copy in wo_copies:
+        copy.wait()
+    vec = vectors_of(b_s, NATURAL)
+    eb[...] = vectors_of(b_s, CORE_MAJOR)[8:16, :]
+    wo = wo_s[...].reshape(WIDTH, WIDTH)
+    first_sum = hid[...].astype(F32) + (mm_nn(low, wo) + vec[0:1, :])
     x1, r1 = norm_parts(first_sum)
     xhat1[...] = x1
     rstd1[...] = r1
     normed = x1 * vec[1:2, :] + vec[2:3, :]
-    lown[...] = normed.astype(BF)
+    lown = normed.astype(BF)
+    keep([shard_columns(lown, parity) for parity in range(2)], 0)
     out = normed + vec[3:4, :]
     for p in range(4):
         for copy in copies[p]:
             copy.wait()
-        bias = eb[pl.ds(rk[p], 1), :]
-        u = mm_nn(lown[...], e_s[p].reshape(WIDTH, WIDTH)) + bias
+        bias = eb[pl.ds(meta[RANK + p], 1), :]
+        u = mm_nn(lown, e_s[p].reshape(WIDTH, WIDTH)) + bias
         cdf = 0.5 * (1.0 + lax.erf(u * 0.7071067811865476))
         pdf = jnp.exp(-0.5 * u * u) * 0.3989422804014327
         low = (u * cdf).astype(BF)
-        act[:, p * WIDTH : (p + 1) * WIDTH] = low
         gp[:, p * WIDTH : (p + 1) * WIDTH] = (cdf + u * pdf).astype(BF)
+        keep([low[:, :half_cols], low[:, half_cols:]], WIDTH + p * half_cols)
         out = out + mm_nn(low, r_s[p].reshape(WIDTH, WIDTH))
     x2, r2 = norm_parts(out)
     xhat2[...] = x2
     rstd2[...] = r2
     nxt = x2 * vec[4:5, :] + vec[5:6, :]
-    hnext[...] = nxt
     hlow[...] = nxt.astype(BF)
+    if hnext:
+        hnext[0][...] = nxt
 
 
 def norm_back(gy, gain, xhat, rstd):
@@ -694,17 +907,26 @@
 
 
 def mlp_bwd_kernel(
-    core_ref, rk, gh, xhat1, rstd1, xhat2, rstd2, gp, vec, wo, t, a, b, d, ct, ca, cb, cd,
-    gfs, gb, gat, di, gctx, ext,
-    e_s, r_s, sems, eb_s,
+    meta, xhat1, rstd1, xhat2, rstd2, gp, *rest, parts
 ):
-    core = core_ref[0]
-    copies = start_ffn_copies(core, (t, a, b, d), (ct, ca, cb, cd), e_s, r_s, sems)
-    grad = gh[...]
+    t, a, b, d, crossed = rest[parts : parts + 5]
+    gfs, dgg, gctx, e_s, r_s, sems, wo_s, b_s, wo_sems, eb_s = rest[-10:]
+    rows = gfs.shape[0]
+    core = meta[CORE]
+    copies = start_ffn_copies(core, t, a, b, d, crossed, e_s, r_s, sems)
+    wo_copies = started_copies(
+        wo_sems, (d.at[:, :, 2], wo_s), (t.at[:, :, 2, 0:16, VEC_AT : VEC_AT + 128], b_s)
+    )
+    grad = rest[0][...].astype(F32)
+    for ref in rest[1:parts]:
+        grad = grad + ref[...].astype(F32)
     x2 = xhat2[...]
+    for copy in wo_copies:
+        copy.wait()
+    vec = vectors_of(b_s, NATURAL)
     gss = norm_back(grad, vec[4:5, :], x2, rstd2[...])
     low = gss.astype(BF)
-    gb[...] = low
+    dgg[0:rows, 4 * WIDTH : 5 * WIDTH] = low
     sums = [None] * 8
     sums[4] = rows_sum(grad * x2)
     sums[5] = rows_sum(grad)
@@ -716,8 +938,8 @@
             copy.wait()
         ga = mm_nt(low, r_s[p].reshape(WIDTH, WIDTH))
         dip = (ga * gp[:, p * WIDTH : (p + 1) * WIDTH].astype(F32)).astype(BF)
-        di[:, p * WIDTH : (p + 1) * WIDTH] = dip
-        eb_s[pl.ds(rk[p], 1), :] = rows_sum(dip.astype(F32))
+        dgg[0:rows, p * WIDTH : (p + 1) * WIDTH] = dip
+        eb_s[pl.ds(meta[RANK + p], 1), :] = rows_sum(dip.astype(F32))
         gn = gn + mm_nt(dip, e_s[p].reshape(WIDTH, WIDTH))
     x1 = xhat1[...]
     gf = norm_back(gn, vec[1:2, :], x1, rstd1[...])
@@ -725,77 +947,123 @@
     sums[2] = rows_sum(gn)
     gfs[...] = gf
     lowa = gf.astype(BF)
-    gat[...] = lowa
+    dgg[0:rows, 5 * WIDTH :] = lowa
     sums[0] = rows_sum(lowa.astype(F32))
     sums[6] = jnp.zeros_like(sums[0])
     sums[7] = sums[6]
-    gc = mm_nt(lowa, wo[...].reshape(WIDTH, WIDTH)).astype(BF)
-    ranks, _, cols = gctx.shape
-    hw = cols // 2
-    for s in range(ranks):
+    gc = mm_nt(lowa, wo_s[...].reshape(WIDTH, WIDTH)).astype(BF)
+    hw = gctx.shape[2] // 2
+    for rank in range(4):
         for half in range(2):
-            gctx[s, :, half * hw : (half + 1) * hw] = gc[half * BLK : (half + 1) * BLK, s * hw : (s + 1) * hw]
-    vecs = jnp.concatenate(sums + [eb_s[...]], axis=0)
-    ext[...] = jnp.zeros_like(ext)
-    shards = ext.shape[0]
-    cut = WIDTH // shards
-    for f in range(shards):
-        ext[f, :, 0:cut] = vecs[:, f * cut : (f + 1) * cut].astype(BF)
+            gctx[rank, :, half * hw : (half + 1) * hw] = gc[half * BLK : (half + 1) * BLK, rank * hw : (rank + 1) * hw]
+    vecs = jnp.concatenate(sums, axis=0)
+    ebs = jnp.concatenate([eb_s[:, (4 * (f % 2) + f // 2) * 96 : (4 * (f % 2) + f // 2 + 1) * 96] for f in range(8)], axis=1)
+    dgg[rows:, 0:WIDTH] = jnp.concatenate([vecs, ebs], axis=0).astype(BF)
+    dgg[rows:, WIDTH:] = jnp.zeros((16, 5 * WIDTH), BF)
 
 
 def wgrad_kernel(
-    core_ref, lown, di, act, gb, lowctx, gat, ext, mine_ta, mine_bd, other_ta, other_bd, dwo
+    meta, l_mine, l_other, dgg, dgg_other, *rest, by_z
 ):
-    core = core_ref[0]
-    shards, rows_out, _ = dwo.shape
-    rows = WIDTH // shards
-    dwo[:, 0:rows, :] = mm_tn(lowctx[...], gat[...]).reshape(shards, rows, WIDTH).astype(BF)
-    dwo[:, rows:rows_out, :] = ext[...]
-    mine = ((mine_ta, 0), (mine_ta, 1), (mine_bd, 0), (mine_bd, 1))
-    other = ((other_ta, 0), (other_bd, 0), (other_ta, 1), (other_bd, 1))
-    for p in (2, 3, 1, 0):
-        cut = slice(p * WIDTH, (p + 1) * WIDTH)
-        for k, (left, right) in enumerate(((lown[...], di[:, cut]), (act[:, cut], gb[...]))):
-            x = mm_tn(left, right).reshape(4, 2, 96, WIDTH).astype(BF)
-            for parity in range(2):
-
-                @pl.when(core == parity)
-                def _():
-                    ref, at = mine[p]
-                    ref[at, :, k] = x[:, parity]
-
-                @pl.when(core != parity)
-                def _():
-                    ref, at = other[p]
-                    ref[at, :, k] = x[:, parity]
-
-
-def place_kernel(rk, ffn0, ffn1, ffn2, ffn3, win0, win1, win2, win3, dwo, e_out, r_out, i_out, o_out, e_s, i_s):
-    for p, (ffn, win) in enumerate(((ffn0, win0), (ffn1, win1), (ffn2, win2), (ffn3, win3))):
-        r_out[pl.ds(pl.multiple_of(rk[p] * 96, 96), 96), :] = ffn[1].astype(F32)
-        e_s[rk[p]] = ffn[0].astype(F32)
-        i_s[rk[p]] = win[0:96, :].astype(F32)
+    t, a, b, dwo = rest[-9:-5] if by_z else rest[-5:-1]
+    d = rest[-1]
+    half = WIDTH // 2
+    rows = l_mine.shape[0]
+
+    def grad(at, at_other, right, right_other):
+        return mm_tn(l_mine[:, at : at + half], dgg[0:rows, right : right + WIDTH]) + mm_tn(
+            l_other[:, at_other : at_other + half], dgg_other[0:rows, right_other : right_other + WIDTH]
+        )
+
+    for p, out in ((3, d), (1, a), (2, b), (0, t)):
+        q = SWAPPED[p]
+        out[:, 0] = grad(0, 0, p * WIDTH, q * WIDTH).reshape(4, 96, WIDTH).astype(BF)
+        at, at_other = WIDTH + p * half, WIDTH + q * half
+        out[:, 1] = grad(at, at_other, 4 * WIDTH, 4 * WIDTH).reshape(4, 96, WIDTH).astype(BF)
+    dwo[:, 0:96, :] = grad(half, half, 5 * WIDTH, 5 * WIDTH).reshape(4, 96, WIDTH).astype(BF)
+    vecs = dgg[rows:, 0:WIDTH].astype(F32) + dgg_other[rows:, 0:WIDTH].astype(F32)
+    dwo[:, 96:, :] = jnp.zeros((4, 16, WIDTH), BF)
+    for parity in range(2):
+
+        @pl.when(meta[CORE] == parity)
+        def _():
+            for z in range(4):
+                dwo[z, 96:, 0:96] = vecs[:, (2 * z + parity) * 96 : (2 * z + parity + 1) * 96].astype(BF)
+
+    for k in range(4 if by_z else 0):
+        rest[-5 + k][...] = d[lax.shift_right_logical(meta[SHARD], 1) ^ k]
+
+
+def place_kernel(
+    meta, ffn0, ffn1, ffn2, ffn3, att0, att1, att2, att3, *rest, layer, last
+):
+    if last:
+        small_in, rest = rest[0], rest[5:]
+    else:
+        rest = rest[1:]
+    e_hbm, r_hbm, i_hbm, o_hbm = rest[:4]
+    smalls = rest[4:-10]
+    e_s, i_s, b_s, e_out, r_out, i_out, o_out, small_s, eb_s, sems = rest[-10:]
+    for p, (ffn, att) in enumerate(((ffn0, att0), (ffn1, att1), (ffn2, att2), (ffn3, att3))):
+        rank = meta[RANK + p]
+        r_out[pl.ds(pl.multiple_of(rank * 96, 96), 96), :] = ffn[1].astype(F32)
+        e_s[rank] = ffn[0].astype(F32)
+        i_s[rank] = att[0:96, WIDTH:].astype(F32)
+        b_s[rank] = att[96:112, WIDTH:].astype(F32)
+    copies = []
+
+    def send(n, src, dst):
+        copy = pltpu.make_async_copy(src, dst.at[layer], sems.at[n])
+        copy.start()
+        copies.append(copy)
+
+    send(0, r_out, r_hbm)
     for f in range(8):
-        e_out[:, f * 384 : (f + 1) * 384] = jnp.concatenate(
-            [e_s[c, :, f * 96 : (f + 1) * 96] for c in range(4)], axis=1
-        )
+        at = (4 * (f % 2) + f // 2) * 96
+        e_out[:, f * 384 : (f + 1) * 384] = jnp.concatenate([e_s[c, :, at : at + 96] for c in range(4)], axis=1)
+    send(1, e_out, e_hbm)
     hw = WIDTH // 4
     for k in range(3):
         i_out[:, k * WIDTH : (k + 1) * WIDTH] = jnp.concatenate(
             [i_s[c, :, k * hw : (k + 1) * hw] for c in range(4)], axis=1
         )
-    o_out[...] = dwo[0:96, :].astype(F32)
-
-
-def permutations(ctx, fsdp):
-    first, second, cores = [], [], []
-    for c in range(ctx):
-        for f in range(fsdp):
-            m1, m2 = (1, 2) if f % 2 == 0 else (2, 1)
-            first.append((c * fsdp + f, (c ^ m1) * fsdp + f))
-            second.append((c * fsdp + f, (c ^ m2) * fsdp + f))
-            cores.append((c * fsdp + f, c * fsdp + (f ^ 1)))
-    return first, second, cores
+    send(2, i_out, i_hbm)
+    wo = [att[:, 0:WIDTH].astype(F32) for att in (att0, att1, att2, att3)]
+    total = (wo[0] + wo[1]) + (wo[2] + wo[3])
+    o_out[...] = total[0:96, :]
+    send(3, o_out, o_hbm)
+    bias = b_s[lax.shift_right_logical(meta[SHARD], 1)]
+    low_half = (meta[SHARD] & 1) == 0
+    qb = jnp.where(low_half, bias[:, 0:96], bias[:, 96:192])
+    vb = jnp.where(low_half, bias[:, 2 * hw : 2 * hw + 96], bias[:, 2 * hw + 96 : 3 * hw])
+    rows = jnp.concatenate([total[96:102, 0:96], qb[0:1], vb[0:1], total[104:112, 0:96]], axis=0)
+    if last:
+        for n, ref in enumerate(smalls[:-1]):
+            ref[...] = jnp.concatenate([rows[n : n + 1], small_in[n : n + 1, 0:96]], axis=0)
+        smalls[-1][...] = jnp.concatenate(
+            [
+                jnp.concatenate([x[8 + c : 9 + c, 0:96] for c in range(4)], axis=1)
+                for x in (rows, small_in[...])
+            ],
+            axis=0,
+        )
+    else:
+        smalls[0][...] = rows
+    for copy in copies:
+        copy.wait()
+
+
+def permutation(ctx, fsdp, move):
+    return [
+        (c * fsdp + f, move(c, f)[0] * fsdp + move(c, f)[1]) for c in range(ctx) for f in range(fsdp)
+    ]
+
+
+def add(*parts):
+    total = parts[0].astype(F32)
+    for part in parts[1:]:
+        total = total + part.astype(F32)
+    return total
 
 
 def on_device_fast(
@@ -804,20 +1072,32 @@
     expand_proj, expand_bias, reduce_proj, reduce_bias, second_gain, second_shift,
     *, ctx, fsdp,
 ):
-    S = pltpu.SMEM
-    V = pltpu.VMEM
-    A = pl.ANY
-    first, second, cores = permutations(ctx, fsdp)
-    both_axes = ("ctx", "fsdp")
-
-    def via_first(x):
-        return lax.ppermute(x, both_axes, first)
-
-    def via_second(x):
-        return lax.ppermute(x, both_axes, second)
-
-    def via_core(x):
-        return lax.ppermute(x, both_axes, cores)
+    S = [pltpu.SMEM]
+    V = [pltpu.VMEM]
+    A = [pl.ANY]
+    axes = ("ctx", "fsdp")
+
+    def via(move):
+        perm = permutation(ctx, fsdp, move)
+        return lambda x: lax.ppermute(x, axes, perm)
+
+    via_first = via(lambda c, f: (c ^ (1 + f % 2), f))
+    via_second = via(lambda c, f: (c ^ (2 - f % 2), f))
+    via_diagonal = via(lambda c, f: (c ^ 3, f))
+    via_core = via(lambda c, f: (c, f ^ 1))
+    via_z = [None] + [via(lambda c, f, k=k: (c, f ^ (2 * k))) for k in range(1, 4)]
+
+    def exchange_ctx(own, a, b, d):
+        return (own, via_first(a), via_second(b), via_diagonal(d))
+
+    def spread_ctx(x):
+        return (x, via_first(x), via_second(x), via_diagonal(x))
+
+    def reduce_z(x):
+        return lax.psum_scatter(x, "fsdp", scatter_dimension=0, tiled=True, axis_index_groups=zgroups)
+
+    def exchange_z(own, *others):
+        return (own,) + tuple(via_z[k + 1](x) for k, x in enumerate(others))
 
     def gather_ctx(x):
         a, b = via_first(x), via_second(x)
@@ -827,193 +1107,245 @@
     hw = heads * HEAD_DIM
     rows = activations.shape[1]
     tokens = rows * ctx
+    cut = WIDTH // fsdp
     c = lax.axis_index("ctx").astype(jnp.int32)
-    core = (lax.axis_index("fsdp") % 2).astype(jnp.int32)
-    core1 = core.reshape(1)
-    m1 = 1 + core
-    rk = jnp.stack([c, c ^ m1, c ^ (3 - m1), c ^ 3])
-    inv = jnp.sum(
-        jnp.where(deal[None, :] == jnp.arange(ctx)[:, None], jnp.arange(ctx)[None, :], 0), axis=1
-    ).astype(jnp.int32)
-    mask = inv ^ c
-    jmap = jnp.where((core == 1) & (mask > 0) & (mask < 3), 3 - mask, mask).astype(jnp.int32)
-
+    shard = lax.axis_index("fsdp").astype(jnp.int32)
+    core = shard % 2
     zgroups = [[2 * z + k for z in range(fsdp // 2)] for k in range(2)]
-    hidden = activations[0].astype(F32)
-    hlow = activations[0]
-
-    small = [attend_bias, first_gain, first_shift, reduce_bias, second_gain, second_shift, query_bias, value_bias]
-    packed = jnp.concatenate([jnp.stack(small, axis=1).reshape(LAYERS, -1), expand_bias], axis=1)
-    packed = lax.all_gather(packed.reshape(1, -1), "fsdp", axis=0, tiled=True).reshape(fsdp, LAYERS, -1)
-    cut = WIDTH // fsdp
-    vec = packed[:, :, : 8 * cut].reshape(fsdp, LAYERS, 8, cut).transpose(1, 2, 0, 3).reshape(LAYERS, 8, WIDTH)
-    vec = vec.astype(F32)
-    ebias = packed[:, :, 8 * cut :].reshape(fsdp, LAYERS, ctx, cut).transpose(1, 2, 0, 3)
-    ebias = ebias.reshape(LAYERS, ctx, WIDTH).astype(F32)
-
-    starts = lax.all_gather(doc_start[0], "ctx", axis=0, tiled=True).reshape(ctx, 2, BLK)
-    chosen = inv[:, None, None, None] == jnp.arange(ctx, dtype=jnp.int32)[None, :, None, None]
-    starts = jnp.sum(jnp.where(chosen, starts[None], 0), axis=1)
-    logical = jnp.concatenate([starts[:, 0], starts[::-1, 1]], axis=0).reshape(-1)
+
+    hidden = activations[0]
+    gathered = gather_ctx(hidden)
+    small = (attend_bias, first_gain, first_shift, reduce_bias, second_gain, second_shift, query_bias, value_bias)
+    sent = call(
+        prep_kernel,
+        [((3 * cut, WIDTH), BF)] * 4,
+        (expand_proj, reduce_proj, attend_in, attend_out, expand_bias) + small,
+        V * 13,
+        [],
+        "prep",
+        0,
+        8 * 1024 * 1024,
+    )
+
+    def gather_ffn(x):
+        x = lax.all_gather(x, "fsdp", axis=0, tiled=True)
+        return x.reshape(fsdp // 2, 2, 3, cut, WIDTH)
+
+    ranks = jnp.arange(ctx, dtype=jnp.int32)
+    inv = jnp.sum(jnp.where(deal[None, :] == ranks[:, None], ranks[None, :], 0), axis=1).astype(jnp.int32)
+    starts = lax.all_gather(doc_start[0], "ctx", axis=0, tiled=True)
+    by_rank = starts.reshape(ctx, 2, BLK)
+    chosen = inv[:, None, None, None] == ranks[None, :, None, None]
+    by_block = jnp.sum(jnp.where(chosen, by_rank[None], 0), axis=1)
+    logical = jnp.concatenate([by_block[:, 0], by_block[::-1, 1]], axis=0).reshape(-1)
     qrow = jnp.broadcast_to(logical[None, :], (8, tokens))
     kcol = jnp.broadcast_to(logical[:, None], (tokens, 128))
     jmin = jnp.min(logical.reshape(tokens // QB, QB), axis=1) // QB
 
-    def ffn_piece(layer):
-        e = expand_proj[layer].reshape(cut, fsdp, ctx, cut)
-        e = lax.dynamic_index_in_dim(e, c, axis=2, keepdims=False).reshape(cut, WIDTH)
-        r = lax.dynamic_slice_in_dim(reduce_proj[layer], c * cut, cut, axis=0)
-        x = lax.all_gather(
-            jnp.concatenate([e, r], axis=0), "fsdp", axis=0, tiled=True, axis_index_groups=zgroups
-        ).reshape(fsdp // 2, 2, cut, WIDTH)
-        own = gather_ctx(x)
-        return own + tuple(via_core(piece) for piece in own)
-
-    win = attend_in.reshape(LAYERS, cut, 3, WIDTH)
-    win = lax.dynamic_slice_in_dim(win, c * hw, hw, axis=3).reshape(LAYERS * cut, 3 * hw)
-    win = lax.all_gather(win, "fsdp", axis=0, tiled=True).reshape(fsdp, LAYERS, cut, 3 * hw)
-    win = [win[:, layer].reshape(WIDTH, 3 * hw) for layer in range(LAYERS)]
-    wout = lax.all_gather(attend_out.reshape(LAYERS * cut, WIDTH), "fsdp", axis=0, tiled=True)
-    wout = wout.reshape(fsdp, LAYERS, cut, WIDTH)
-    wout = [wout[:, layer] for layer in range(LAYERS)]
-    pieces = [ffn_piece(layer) for layer in range(LAYERS)]
-    qkv_bias = []
+    m1 = 1 + core
+    mask = inv ^ c
+    jmap = jnp.where((core == 1) & (mask > 0) & (mask < 3), 3 - mask, mask)
+    meta = jnp.concatenate(
+        [jnp.stack([core, shard, c, c ^ m1, c ^ (3 - m1), c ^ 3]), jmap, inv, jmin]
+    ).astype(jnp.int32)
+
+    kept = []
+    earlier = ()
+    wide = [gather_ffn(sent[0]), gather_ffn(sent[1]), None, None]
+    wide[0] = after((wide[0],), starts, *gathered[1:])[0]
+    wide[2] = gather_ffn(*after(sent[2:3], wide[0]))
+    pieces = []
     for layer in range(LAYERS):
-        qb = lax.dynamic_slice_in_dim(vec[layer, 6], c * hw, hw)
-        vb = lax.dynamic_slice_in_dim(vec[layer, 7], c * hw, hw)
-        qkv_bias.append(jnp.concatenate([qb, jnp.zeros_like(qb), vb])[None, :])
-
-    mac = 2
-    kept = []
-    for layer in range(LAYERS):
-        gathered = gather_ctx(hlow)
-        qkv, ctx_own, lse = call(
+        t, d = wide[2 * layer : 2 * layer + 2]
+        mine = half_of(meta, t, *gathered[1:])
+        a, b = via_first(mine), via_second(mine)
+        qkv, *ctx_own, lse = call(
             functools.partial(attn_fwd_kernel, heads=heads, tokens=tokens),
-            [((ctx, rows, 3 * hw), BF), ((ctx, BLK, 2 * hw), BF), ((8, tokens), F32)],
-            (jmap, inv, jmin) + gathered + (win[layer], qkv_bias[layer], qrow, kcol),
-            [S] * 3 + [V] * 8,
+            [((ctx, rows, 3 * hw), BF)] + [((BLK, 2 * hw), BF)] * 4 + [((8, tokens), F32)],
+            (meta,) + gathered + (qrow, kcol, t, mine) + earlier,
+            S + V * 6 + A * (2 + len(earlier)),
             [
                 pltpu.VMEM((heads, tokens, HEAD_DIM), BF),
                 pltpu.VMEM((heads, tokens, HEAD_DIM), BF),
                 pltpu.VMEM((hw, tokens), BF),
                 pltpu.VMEM((hw, tokens), F32),
+                pltpu.VMEM((ctx, BLK, 2 * hw), BF),
+                pltpu.VMEM((fsdp // 2, 2, cut, VEC_AT), BF),
+                pltpu.VMEM((fsdp // 2, 2, 16, 128), BF),
+                pltpu.SemaphoreType.DMA((2,)),
             ],
             "attn_fwd",
-            mac * tokens * WIDTH * 3 * hw * 4,
+            2 * tokens * WIDTH * 3 * hw * 4,
             10 * 1024 * 1024,
         )
-        cx = lax.all_to_all(ctx_own, "ctx", 0, 0, tiled=True)
-        lowctx, xhat1, rstd1, lown, act, gp, xhat2, rstd2, hidden, hlow = call(
+        cx = exchange_ctx(*ctx_own)
+        if layer + 1 < LAYERS:
+            wide[3] = gather_ffn(*after(sent[3:4], *cx[1:]))
+        pieces.append((t, a, b, d, via_core(pack(a, b, lse))))
+        outs = [
+            ((rows, WIDTH), F32), ((rows, 1), F32), ((rows, 4 * WIDTH), BF), ((rows, WIDTH), F32), ((rows, 1), F32),
+            ((rows, 3 * WIDTH), BF), ((rows, 3 * WIDTH), BF), ((rows, WIDTH), BF),
+        ]
+        if layer + 1 < LAYERS:
+            outs.append(((rows, WIDTH), F32))
+        xhat1, rstd1, gp, xhat2, rstd2, l_mine, l_other, hlow, *more = call(
             mlp_fwd_kernel,
-            [
-                ((rows, WIDTH), BF), ((rows, WIDTH), F32), ((rows, 1), F32), ((rows, WIDTH), BF),
-                ((rows, 4 * WIDTH), BF), ((rows, 4 * WIDTH), BF), ((rows, WIDTH), F32), ((rows, 1), F32),
-                ((rows, WIDTH), F32), ((rows, WIDTH), BF),
-            ],
-            (core1, rk, cx, hidden, wout[layer], vec[layer], ebias[layer]) + pieces[layer],
-            [S] * 2 + [V] * 5 + [A] * 8,
-            ffn_scratch(),
+            outs,
+            (meta,) + cx + (hidden,) + pieces[layer],
+            S + V * 5 + A * 5,
+            ffn_scratch() + [pltpu.VMEM((ctx, rows, hw), BF), pltpu.VMEM((8, WIDTH), F32)],
             "mlp_fwd",
-            mac * rows * WIDTH * WIDTH * 9,
+            2 * rows * WIDTH * WIDTH * 9,
             20 * 1024 * 1024,
         )
-        kept.append((gathered, qkv, ctx_own, lse, lowctx, xhat1, rstd1, lown, act, gp, xhat2, rstd2))
+        l_other = via_core(l_other)
+        earlier = (l_other,)
+        kept.append((gathered, qkv, ctx_own, lse, xhat1, rstd1, gp, xhat2, rstd2, l_mine, l_other))
+        if more:
+            hidden = more[0]
+            gathered = gather_ctx(hlow)
     out_act = hlow[None]
 
-    grad = cotangent[0].astype(F32)
-    results = [None] * LAYERS
+    grads = (cotangent[0],)
+    order = ()
     for layer in reversed(range(LAYERS)):
-        gathered, qkv, ctx_own, lse, lowctx, xhat1, rstd1, lown, act, gp, xhat2, rstd2 = kept[layer]
-        gfs, gb, gat, di, gctx, ext = call(
-            mlp_bwd_kernel,
+        gathered, qkv, ctx_own, lse, xhat1, rstd1, gp, xhat2, rstd2, l_mine, l_other = kept[layer]
+        gfs, dgg, gctx = call(
+            functools.partial(mlp_bwd_kernel, parts=len(grads)),
             [
-                ((rows, WIDTH), F32), ((rows, WIDTH), BF), ((rows, WIDTH), BF), ((rows, 4 * WIDTH), BF),
-                ((ctx, BLK, 2 * hw), BF), ((fsdp, 16, WIDTH), BF),
+                ((rows, WIDTH), F32), ((rows + 16, 6 * WIDTH), BF), ((ctx, BLK, 2 * hw), BF),
             ],
-            (core1, rk, grad, xhat1, rstd1, xhat2, rstd2, gp, vec[layer], wout[layer]) + pieces[layer],
-            [S] * 2 + [V] * 8 + [A] * 8,
+            (meta, xhat1, rstd1, xhat2, rstd2, gp) + grads + pieces[layer] + order,
+            S + V * (5 + len(grads)) + A * (5 + len(order)),
             ffn_scratch() + [pltpu.VMEM((8, WIDTH), F32)],
             "mlp_bwd",
-            mac * rows * WIDTH * WIDTH * 9,
+            2 * rows * WIDTH * WIDTH * 9,
             20 * 1024 * 1024,
         )
         gcx = lax.all_to_all(gctx, "ctx", 0, 0, tiled=True)
-        pair = ((2, 4, 2, cut, WIDTH), BF)
-        mine_ta, mine_bd, other_ta, other_bd, dwo = call(
-            wgrad_kernel,
-            [pair, pair, pair, pair, ((fsdp, cut + 16, WIDTH), BF)],
-            (core1, lown, di, act, gb, lowctx, gat, ext),
-            [S] + [V] * 7,
-            [],
-            "wgrad",
-            mac * rows * WIDTH * WIDTH * 9,
-            20 * 1024 * 1024,
-        )
-        g_own, g_a, g_bd, dw = call(
-            functools.partial(attn_bwd_kernel, heads=heads, tokens=tokens),
-            [
-                ((rows, WIDTH), F32), ((rows, WIDTH), BF), ((2, rows, WIDTH), BF),
-                ((fsdp, cut + 16, 3 * hw), BF),
+        piece = ((4, 2, cut, WIDTH), BF)
+
+        def weight_grads(by_z, *before):
+            outs = [piece] * 3 + [((4, cut + 16, WIDTH), BF)]
+            return call(
+                functools.partial(wgrad_kernel, by_z=by_z),
+                outs + ([((2, cut, WIDTH), BF)] * 4 if by_z else [piece]),
+                (meta, l_mine, l_other, dgg, via_core(dgg)) + before,
+                S + V * 4 + A * len(before),
+                [pltpu.VMEM(*piece)] if by_z else [],
+                "wgrad",
+                2 * rows * WIDTH * WIDTH * 9,
+                20 * 1024 * 1024,
+            )
+
+        def attention_grads(*before):
+            return call(
+                functools.partial(attn_bwd_kernel, heads=heads, tokens=tokens),
+                [
+                    ((rows, WIDTH), F32), ((rows, WIDTH), BF), ((rows, WIDTH), BF), ((rows, WIDTH), BF),
+                    ((4, cut + 16, 3 * hw), BF), ((4, cut + 16, 3 * hw), BF),
+                ],
+                (meta,) + gathered + (qrow, kcol, qkv) + tuple(ctx_own) + (gcx, lse, wide[2 * layer]) + before,
+                S + V * 13 + A * (1 + len(before)),
+                [pltpu.VMEM((heads, tokens, HEAD_DIM), BF)] * 4
+                + [
+                    pltpu.VMEM((hw, tokens), BF),
+                    pltpu.VMEM((8, tokens), F32),
+                    pltpu.VMEM((heads, tokens, HEAD_DIM), F32),
+                    pltpu.VMEM((heads, tokens, HEAD_DIM), F32),
+                    pltpu.VMEM((hw, tokens), F32),
+                    pltpu.VMEM((ctx, rows, 3 * hw), BF),
+                    pltpu.VMEM((fsdp // 2, 2, cut, VEC_AT), BF),
+                    pltpu.VMEM((ctx, BLK, 2 * hw), BF),
+                    pltpu.VMEM((fsdp, cut + 16, 3 * hw), BF),
+                    pltpu.SemaphoreType.DMA((1,)),
+                ],
+                "attn_bwd",
+                2 * tokens * WIDTH * 3 * hw * 8,
+                10 * 1024 * 1024,
+            )
+
+        def attention_shards(dwo, dw, crossed, *others):
+            shape = (4, cut + 16, WIDTH + 3 * hw)
+            (merged,) = call(
+                merge_kernel, [(shape, BF)], (dwo, dw, crossed) + others, V * 3 + A * len(others), [], "merge", 0, 0
+            )
+            return merged, reduce_z(merged).reshape(shape[1:])
+
+        if layer > 0:
+            g_own, g_a, g_b, g_d, dw, dw_other = attention_grads(l_other)
+            t, a, b, dwo, d = weight_grads(False, g_d)
+            d1 = reduce_z(d)
+            over = via_first(sums([[(g_a, via_second(g_d))]])[0])
+            merged, att1 = attention_shards(dwo, dw, via_core(dw_other))
+            grads = (gfs, g_own, via_second(g_b), over)
+            (t1,) = sums([[(t, via_first(a), via_second(b))]])
+            order = (t1, merged)
+            t1 = reduce_z(t1)
+        else:
+            t, a, b, dwo, d = weight_grads(False, gcx)
+            a, b = via_first(a), via_second(b)
+            d0 = reduce_z(d)
+            g_own, g_a, g_b, g_d, dw, dw_other = attention_grads(t)
+
+    def shards(x):
+        return x.reshape(2, cut, WIDTH)
+
+    (t0,) = sums([[(t, a, b)]], g_d)
+    merged, att0 = attention_shards(dwo, dw, via_core(dw_other), t0)
+    t0 = reduce_z(t0)
+    back = via_second(g_d), via_second(g_b)
+    (ffn1,) = sums([[(shards(t1), shards(via_diagonal(d1)))]], merged)
+    ffn1 = spread_ctx(ffn1)
+    att1 = spread_ctx(att1)
+    (over,) = sums([[(g_a, back[0])]], ffn1[0])
+    over = via_first(over)
+
+    finals = [None, (ffn1, att1)]
+    small_out = None
+    placed = []
+    for layer in reversed(range(LAYERS)):
+        if layer == 0:
+            (ffn0,) = sums([[(shards(t0), shards(via_diagonal(d0)))]], small_out)
+            finals[0] = (spread_ctx(ffn0), spread_ctx(att0))
+        ffn, att = finals[layer]
+        waits = (over,) if layer > 0 else ()
+        last = layer == 0
+        big = [
+            ((LAYERS, cut, 4 * WIDTH), F32), ((LAYERS, 4 * cut, WIDTH), F32),
+            ((LAYERS, cut, 3 * WIDTH), F32), ((LAYERS, cut, WIDTH), F32),
+        ]
+        if last:
+            smalls = [((LAYERS, cut), F32)] * 8 + [((LAYERS, 4 * cut), F32)]
+        else:
+            smalls = [((16, cut), F32)]
+        args = (meta,) + ffn + att + ((small_out,) + tuple(placed) if last else waits)
+        spaces = S + V * 8 + (V + A * 4 if last else A)
+        outs = pl.pallas_call(
+            functools.partial(place_kernel, layer=layer, last=last),
+            out_shape=[jax.ShapeDtypeStruct(shape, dtype) for shape, dtype in big + smalls],
+            in_specs=[pl.BlockSpec(memory_space=space) for space in spaces],
+            out_specs=[pl.BlockSpec(memory_space=space) for space in A * 4 + V * len(smalls)],
+            scratch_shapes=[
+                pltpu.VMEM((ctx, cut, WIDTH), F32), pltpu.VMEM((ctx, cut, 3 * hw), F32),
+                pltpu.VMEM((ctx, 16, 3 * hw), F32),
+                pltpu.VMEM((cut, 4 * WIDTH), F32), pltpu.VMEM((4 * cut, WIDTH), F32),
+                pltpu.VMEM((cut, 3 * WIDTH), F32), pltpu.VMEM((cut, WIDTH), F32),
+                pltpu.VMEM((16, 128), F32), pltpu.VMEM((8, 128), F32),
+                pltpu.SemaphoreType.DMA((4,)),
             ],
-            (jmap, inv, jmin) + gathered + (win[layer], qrow, kcol, qkv, ctx_own, gcx, lse),
-            [S] * 3 + [V] * 11,
-            [
-                pltpu.VMEM((heads, tokens, HEAD_DIM), BF),
-                pltpu.VMEM((heads, tokens, HEAD_DIM), BF),
-                pltpu.VMEM((heads, tokens, HEAD_DIM), BF),
-                pltpu.VMEM((heads, tokens, HEAD_DIM), BF),
-                pltpu.VMEM((hw, tokens), BF),
-                pltpu.VMEM((8, tokens), F32),
-                pltpu.VMEM((heads, tokens, HEAD_DIM), F32),
-                pltpu.VMEM((heads, tokens, HEAD_DIM), F32),
-                pltpu.VMEM((hw, tokens), F32),
-                pltpu.VMEM((ctx, rows, 3 * hw), BF),
-            ],
-            "attn_bwd",
-            mac * tokens * WIDTH * 3 * hw * 8,
-            10 * 1024 * 1024,
-        )
-        back = via_second(g_bd).astype(F32)
-        over = via_first((g_a.astype(F32) + back[1]).astype(BF)).astype(F32)
-        grad = gfs + (g_own + (back[0] + over))
-        sum_bd = (mine_bd.astype(F32) + via_core(other_bd).astype(F32)).astype(BF)
-        back = via_second(sum_bd).astype(F32)
-        sum_ta = mine_ta.astype(F32) + via_core(other_ta).astype(F32) + back
-        over = via_first(sum_ta[1].astype(BF)).astype(F32)
-        ffn = lax.psum_scatter(
-            (sum_ta[0] + over).astype(BF), "fsdp", scatter_dimension=0, tiled=True, axis_index_groups=zgroups
-        ).reshape(2, cut, WIDTH)
-        dw = lax.psum_scatter(dw, "fsdp", scatter_dimension=0, tiled=True).reshape(cut + 16, 3 * hw)
-        dwo = lax.psum_scatter(dwo, "fsdp", scatter_dimension=0, tiled=True).reshape(cut + 16, WIDTH)
-        dwo = (dwo.astype(F32) + via_first(dwo).astype(F32)).astype(BF)
-        dwo = dwo.astype(F32) + via_second(dwo).astype(F32)
-        ffn_all = gather_ctx(ffn)
-        dw_all = gather_ctx(dw)
-        e_out, r_out, i_out, o_out = call(
-            place_kernel,
-            [((cut, 4 * WIDTH), F32), ((4 * cut, WIDTH), F32), ((cut, 3 * WIDTH), F32), ((cut, WIDTH), F32)],
-            (rk,) + ffn_all + dw_all + (dwo,),
-            [S] + [V] * 9,
-            [pltpu.VMEM((ctx, cut, WIDTH), F32), pltpu.VMEM((ctx, cut, 3 * hw), F32)],
-            "place",
-            0,
-            10 * 1024 * 1024,
-        )
-        shard = lax.axis_index("fsdp").astype(jnp.int32)
-        bias_rows = jnp.stack([piece[cut : cut + 1] for piece in dw_all])
-        owner = (shard * cut) // hw
-        holder = owner ^ c
-        holder = jnp.where((core == 1) & (holder > 0) & (holder < 3), 3 - holder, holder)
-        row = lax.dynamic_index_in_dim(bias_rows, holder, axis=0, keepdims=False)[0]
-        offset = shard * cut - owner * hw
-        qb = lax.dynamic_slice_in_dim(row, offset, cut).astype(F32)
-        vb = lax.dynamic_slice_in_dim(row, 2 * hw + offset, cut).astype(F32)
-        v = dwo[cut:, :cut]
-        results[layer] = (
-            i_out, qb, vb, o_out, v[0], v[1], v[2], e_out, v[8 : 8 + ctx].reshape(-1), r_out, v[3], v[4], v[5]
-        )
-    stacked = [jnp.stack([results[layer][n] for layer in range(LAYERS)]) for n in range(13)]
-    return (out_act, grad[None]) + tuple(stacked)
+            input_output_aliases={10 + n: n for n in range(4)} if last else {},
+            compiler_params=pltpu.CompilerParams(vmem_limit_bytes=VMEM_LIMIT),
+            cost_estimate=pl.CostEstimate(flops=0, bytes_accessed=10 * 1024 * 1024, transcendentals=0),
+            name="place",
+        )(*args)
+        placed = outs[:4]
+        small_out = outs[4]
+        vectors = outs[4:]
+    in_grad = add(gfs, g_own, back[1], over)[None]
+    e_out, r_out, i_out, o_out = placed
+    ab, fg, fs, rb, sg, ss, qb, vb, xb = vectors
+    return (out_act, in_grad, i_out, qb, vb, o_out, ab, fg, fs, e_out, xb, r_out, rb, sg, ss)
 
 
 def on_device(*args, ctx, fsdp):

time: 607 us -> 533 us (0.88)
  Pallas kernels: 193 us -> 251 us
  other arithmetic: 49 us -> 3.37 us
  waiting for transfers between devices: 198 us -> 153 us
  starting transfers between devices: 72.6 us -> 42.7 us
  local copies, waits for them, and re-layouts: 35.8 us -> 23.3 us
    pallas_call x12 -> x23, Pallas kernels: 193 us -> 241 us  [call(): pl.pallas_call(kernel, out_shape=[jax.ShapeDtypeStruct(shape, dtype) for...]
    ppermute x48, waiting for transfers between devices: 169 us -> 136 us  [via(): return lambda x: lax.ppermute(x, axes, perm)]
    reduce_scatter x6, waiting for transfers between devices: 23.6 us -> 0.03 us  [reduce_z(): lax.psum_scatter(x, 'fsdp', scatter_dimension=0, tiled=True, axis_index_g...]
    convert_element_type x14 -> x0, other arithmetic: 20.1 us -> none  [the longest x2 6.99 us: on_device_fast(): sum_bd = (mine_bd.astype(F32) + via_core(other_bd).astype(F32)).astype(BF)]
    ppermute x48, starting transfers between devices: 60.2 us -> 41.9 us  [via(): return lambda x: lax.ppermute(x, axes, perm)]
    all_gather x4, waiting for transfers between devices: 2.17 us -> 15.7 us  [gather_ffn(): x = lax.all_gather(x, 'fsdp', axis=0, tiled=True)]
    unnamed x108 -> x120, local copies, waits for them, and re-layouts: 7.67 us -> 20.6 us
    all_to_all x1 -> x2, blocking collectives: 12.1 us -> 24.8 us  [on_device_fast(): gcx = lax.all_to_all(gctx, 'ctx', 0, 0, tiled=True)]
  transfers between devices with their start and end apart: 61 -> 58, of which waited for: 26 -> 22; matrix products, arithmetic and copies ran while one was open for 11% -> 1% of each run, Pallas kernels for 23% -> 38%
where the time goes in v2:
time: 533 us; the launch traced here: 523 us
  Pallas kernels  251 us (47%)
  waiting for transfers between devices  153 us (29%)
  starting transfers between devices  42.7 us (8%)
  blocking collectives  35.3 us (7%)
  local copies, waits for them, and re-layouts  23.3 us (4%)
  between operations  15.2 us (3%)
    pallas_call x23, Pallas kernels, call(): pl.pallas_call(kernel, out_shape=[jax.ShapeDtypeStruct(shape, dtype) for...  241 us
    ppermute x48, waiting for transfers between devices, via(): return lambda x: lax.ppermute(x, axes, perm)  136 us
    ppermute x48, starting transfers between devices, via(): return lambda x: lax.ppermute(x, axes, perm)  41.9 us
    all_to_all x2, blocking collectives, on_device_fast(): gcx = lax.all_to_all(gctx, 'ctx', 0, 0, tiled=True)  24.8 us
    unnamed x120, local copies, waits for them, and re-layouts  20.6 us
    all_gather x4, waiting for transfers between devices, gather_ffn(): x = lax.all_gather(x, 'fsdp', axis=0, tiled=True)  15.7 us
  transfers between devices with their start and end apart: 58, of which 22 were waited for; matrix products, arithmetic and copies ran while one was open for 1% of the time, Pallas kernels for 38%

profile of v2, /device:TPU:1, one launch (start us, length us, event | category | flops | bytes accessed | tf_op | source)
XLA Modules:
  0.0 523.1 jit_solution(4402517095726880487)
XLA Ops:
  7.3 3.8 prep.1
  15.3 10.0 %collective-permute-done.refs_2_.rest_0_.h1 = bf16[384,768]{1,0:T(8,128)(2,1)S(1)} collective-permute-done((bf16[384,768]{1,0:T(8,128)(2,1)S(1)}, bf16[384,768]{1,0:T(8,128)(2,1)S(1)}, u32[]{:S(2)}, u32[]{:S(2)}) %collective-permute-start) | collective-permute-done | bytes 589856 | tf_op jit(solution)/shard_map/ppermute | solution.py:1082
  28.4 10.5 %all-gather = s32[1,1536]{1,0:T(1,128)S(1)} all-gather(s32[1,384]{1,0:T(1,128)S(1)} %copy-done.54), channel_id=2, replica_groups=mesh['ctx'=4,'fsdp'=8] {'ctx'}, dimensions={1}, use_global_device_ids=true | all-gather | bytes 7680 | tf_op jit(solution)/shard_map/all_gather | solution.py:1136
  39.5 15.7 %all-gather.6.cloned.1.call-done = bf16[2304,768]{1,0:T(8,128)(2,1)} async-done(((bf16[288,768]{1,0:T(8,128)(2,1)}), bf16[2304,768]{1,0:T(8,128)(2,1)}) %all-gather.6.cloned.1.call-update) | async-done | bytes 3538960 | tf_op jit(solution)/shard_map/all_gather | solution.py:1131
  64.6 28.0 %attn_fwd.2 = (bf16[4,384,576]{2,1,0:T(8,128)(2,1)}, bf16[192,384]{1,0:T(8,128)(2,1)}, bf16[192,384]{1,0:T(8,128)(2,1)}, bf16[192,384]{1,0:T(8,128)(2,1)}, bf16[192,384]{1,0:T(8,128)(2,1)}, /*index=5*/f32[8,1536]{1,0:T(8,128)}) custom-call(s32[20]{0:T(128)} %concatenate.7.meta, bf16[384,768]{1,0:T(8,128)(2,1)} %bitcast.35, bf16[384,768]{1,0:T(8,128)(2,1)} %copy-done.4, ...), custom_call_target="tpu_custom_call" | custom-call | tf_op jit(solution)/shard_map/attn_fwd/pallas_call | solution.py:447
  103.3 4.1 collective-permute-done.5.c3.refs_3_
  109.6 14.4 %mlp_fwd.2 = (f32[384,768]{1,0:T(8,128)}, f32[384,1]{1,0:T(8,128)}, bf16[384,3072]{1,0:T(8,128)(2,1)}, f32[384,768]{1,0:T(8,128)}, f32[384,1]{1,0:T(8,128)}, /*i...) custom-call(s32[20]{0:T(128)} %concatenate.7.meta, ...), custom_call_target="tpu_custom_call" | custom-call | tf_op jit(solution)/shard_map/mlp_fwd/pallas_call | solution.py:447
  124.6 13.4 %collective-permute-done.9.rest_0_.h1 = bf16[384,768]{1,0:T(8,128)(2,1)S(1)} collective-permute-done((bf16[384,768]{1,0:T(8,128)(2,1)}, bf16[384,768]{1,0:T(8,128)(2,1)S(1)}, u32[]{:S(2)}, u32[]{:S(2)}) %collective-permute-start.9) | collective-permute-done | bytes 589856 | tf_op jit(solution)/shard_map/ppermute | solution.py:1082
  138.1 3.7 collective-permute-start.12
  141.8 5.3 %collective-permute-done.11.rest_2_.h3 = bf16[384,768]{1,0:T(8,128)(2,1)S(1)} collective-permute-done((bf16[384,768]{1,0:T(8,128)(2,1)S(1)}, bf16[384,768]{1,0:T(8,128)(2,1)S(1)}, u32[]{:S(2)}, u32[]{:S(2)}) %collective-permute-start.11) | collective-permute-done | bytes 589856 | tf_op jit(solution)/shard_map/ppermute | solution.py:1082
  151.7 28.2 %attn_fwd.3 = (bf16[4,384,576]{2,1,0:T(8,128)(2,1)}, bf16[192,384]{1,0:T(8,128)(2,1)}, bf16[192,384]{1,0:T(8,128)(2,1)}, bf16[192,384]{1,0:T(8,128)(2,1)}, bf16[192,384]{1,0:T(8,128)(2,1)}, /*index=5*/f32[8,1536]{1,0:T(8,128)}) custom-call(s32[20]{0:T(128)} %concatenate.7.meta, bf16[384,768]{1,0:T(8,128)(2,1)} %get-tuple-element.101.h0, ...), custom_call_target="tpu_custom_call" | custom-call | tf_op jit(solution)/shard_map/attn_fwd/pallas_call | solution.py:447
  191.4 3.6 collective-permute-done.15.c3
  196.4 14.4 %mlp_fwd.3 = (f32[384,768]{1,0:T(8,128)}, f32[384,1]{1,0:T(8,128)}, bf16[384,3072]{1,0:T(8,128)(2,1)}, f32[384,768]{1,0:T(8,128)}, f32[384,1]{1,0:T(8,128)}, /*i...) custom-call(s32[20]{0:T(128)} %concatenate.7.meta, ...), custom_call_target="tpu_custom_call" | custom-call | tf_op jit(solution)/shard_map/mlp_fwd/pallas_call | solution.py:447
  210.9 15.8 %mlp_bwd.2 = (f32[384,768]{1,0:T(8,128)}, bf16[400,4608]{1,0:T(8,128)(2,1)}, bf16[4,192,384]{2,1,0:T(8,128)(2,1)}) custom-call(s32[20]{0:T(128)} %concatenate.7.meta, f32[384,768]{1,0:T(8,128)} %get-tuple-element.117.xhat1, f32[384,1]{1,0:T(8,128)} %get-tuple-element.118.rstd1, f32[384,768]{1,0:T(8,128)} %get-tuple-element.119.xhat2, ...), custom_call_target="tpu_custom_call" | custom-call | tf_op jit(solution)/shard_map/mlp_bwd/pallas_call | solution.py:447
  227.3 13.3 %all_to_all.10.gctx = bf16[4,192,384]{2,1,0:T(8,128)(2,1)} all-to-all(bf16[4,192,384]{2,1,0:T(8,128)(2,1)} %get-tuple-element.124), channel_id=1, replica_groups=mesh['ctx'=4,'fsdp'=8] {'ctx'}, dimensions={0} | all-to-all | bytes 1179648 | tf_op jit(solution)/shard_map/all_to_all | solution.py:1225
  241.9 31.1 %attn_bwd.2 = (f32[384,768]{1,0:T(8,128)}, bf16[384,768]{1,0:T(8,128)(2,1)}, bf16[384,768]{1,0:T(8,128)(2,1)}, bf16[384,768]{1,0:T(8,128)(2,1)}, bf16[4,112,576]...) custom-call(s32[20]{0:T(128)} %concatenate.7.meta, bf16[384,768]{1,0:T(8,128)(2,1)} %get-tuple-element.101.h0, ...), custom_call_target="tpu_custom_call" | custom-call | tf_op jit(solution)/shard_map/attn_bwd/pallas_call | solution.py:447
  273.1 12.3 %wgrad.2 = (bf16[4,2,96,768]{3,2,1,0:T(8,128)(2,1)}, bf16[4,2,96,768]{3,2,1,0:T(8,128)(2,1)}, bf16[4,2,96,768]{3,2,1,0:T(8,128)(2,1)}, bf16[4,112,768]{2,1,0:T(8,128)(2,1)}, bf16[4,2,96,768]{3,2,1,0:T(8,128)(2,1)}) custom-call(s32[20]{0:T(128)} %concatenate.7.meta, bf16[384,2304]{1,0:T(8,128)(2,1)} %get-tuple-element.130.l_mine, ...), custom_call_target="tpu_custom_call" | custom-call | tf_op jit(solution)/shard_map/wgrad/pallas_call | solution.py:447
  292.8 28.9 %collective-permute-done.21.refs_1_ = bf16[384,768]{1,0:T(8,128)(2,1)} collective-permute-done((bf16[384,768]{1,0:T(8,128)(2,1)S(1)}, bf16[384,768]{1,0:T(8,128)(2,1)}, u32[]{:S(2)}, u32[]{:S(2)}) %collective-permute-start.21) | collective-permute-done | bytes 589856 | tf_op jit(solution)/shard_map/ppermute | solution.py:1082
  326.1 3.4 sums.7.rest_9_
  329.5 4.2 collective-permute-done.22.rest_3_
  334.5 16.5 %mlp_bwd.3 = (f32[384,768]{1,0:T(8,128)}, bf16[400,4608]{1,0:T(8,128)(2,1)}, bf16[4,192,384]{2,1,0:T(8,128)(2,1)}) custom-call(s32[20]{0:T(128)} %concatenate.7.meta, f32[384,768]{1,0:T(8,128)} %get-tuple-element.112.xhat1, f32[384,1]{1,0:T(8,128)} %get-tuple-element.113.rstd1, f32[384,768]{1,0:T(8,128)} %get-tuple-element.114.xhat2, ...), custom_call_target="tpu_custom_call" | custom-call | tf_op jit(solution)/shard_map/mlp_bwd/pallas_call | solution.py:447
  352.1 11.5 %all_to_all.11.rest_0_.gctx = bf16[4,192,384]{2,1,0:T(8,128)(2,1)} all-to-all(bf16[4,192,384]{2,1,0:T(8,128)(2,1)S(1)} %copy-done.26), channel_id=1, replica_groups=mesh['ctx'=4,'fsdp'=8] {'ctx'}, dimensions={0} | all-to-all | bytes 1179648 | tf_op jit(solution)/shard_map/all_to_all | solution.py:1225
  363.5 12.4 %wgrad.3 = (bf16[4,2,96,768]{3,2,1,0:T(8,128)(2,1)}, bf16[4,2,96,768]{3,2,1,0:T(8,128)(2,1)}, bf16[4,2,96,768]{3,2,1,0:T(8,128)(2,1)}, bf16[4,112,768]{2,1,0:T(8,128)(2,1)}, bf16[4,2,96,768]{3,2,1,0:T(8,128)(2,1)}) custom-call(s32[20]{0:T(128)} %concatenate.7.meta, bf16[384,2304]{1,0:T(8,128)(2,1)} %get-tuple-element.141.l_mine, ...), custom_call_target="tpu_custom_call" | custom-call | tf_op jit(solution)/shard_map/wgrad/pallas_call | solution.py:447
  377.9 31.0 %attn_bwd.3 = (f32[384,768]{1,0:T(8,128)}, bf16[384,768]{1,0:T(8,128)(2,1)}, bf16[384,768]{1,0:T(8,128)(2,1)}, bf16[384,768]{1,0:T(8,128)(2,1)}, bf16[4,112,576]...) custom-call(s32[20]{0:T(128)} %concatenate.7.meta, bf16[384,768]{1,0:T(8,128)(2,1)} %bitcast.37, bf16[384,768]{1,0:T(8,128)(2,1)} %copy-done.4, ...), custom_call_target="tpu_custom_call" | custom-call | tf_op jit(solution)/shard_map/attn_bwd/pallas_call | solution.py:447
  410.3 3.4 sums.8.rest_0_
  425.9 15.0 %collective-permute-done.30 = bf16[1,2,96,768]{3,2,1,0:T(8,128)(2,1)S(1)} collective-permute-done((bf16[1,2,96,768]{3,2,1,0:T(8,128)(2,1)}, bf16[1,2,96,768]{3,2,1,0:T(8,128)(2,1)S(1)}, u32[]{:S(2)}, u32[]{:S(2)}) %collective-permute-start.30) | collective-permute-done | bytes 294944 | tf_op jit(solution)/shard_map/ppermute | solution.py:1082
  455.3 4.0 collective-permute-done.37.ffn2
  459.3 12.9 %collective-permute-done.36.ffn1 = bf16[2,96,768]{2,1,0:T(8,128)(2,1)S(1)} collective-permute-done((bf16[2,96,768]{2,1,0:T(8,128)(2,1)S(1)}, bf16[2,96,768]{2,1,0:T(8,128)(2,1)S(1)}, u32[]{:S(2)}, u32[]{:S(2)}) %collective-permute-start.36) | collective-permute-done | bytes 294944 | tf_op jit(solution)/shard_map/ppermute | solution.py:1082
  473.7 5.0 place.2
  490.5 10.3 %collective-permute-done.42.ffn1 = bf16[2,96,768]{2,1,0:T(8,128)(2,1)} collective-permute-done((bf16[2,96,768]{2,1,0:T(8,128)(2,1)}, bf16[2,96,768]{2,1,0:T(8,128)(2,1)}, u32[]{:S(2)}, u32[]{:S(2)}) %collective-permute-start.42) | collective-permute-done | bytes 294944 | tf_op jit(solution)/shard_map/ppermute | solution.py:1082
  502.9 8.0 %collective-permute-done.45.att1 = bf16[112,1344]{1,0:T(8,128)(2,1)} collective-permute-done((bf16[112,1344]{1,0:T(8,128)(2,1)}, bf16[112,1344]{1,0:T(8,128)(2,1)}, u32[]{:S(2)}, u32[]{:S(2)}) %collective-permute-start.45) | collective-permute-done | bytes 301088 | tf_op jit(solution)/shard_map/ppermute | solution.py:1082
  510.9 4.9 place.3
  (264 shorter events, 109.0 us)
Async XLA Ops:
  7.2 48.1 %all-gather.6.cloned.1.call-start = ((), (), s32[]{:S(2)}) async-start(), calls=%async_computation.8 | async-start | bytes 3981312 | tf_op jit(solution)/shard_map/all_gather | solution.py:1131
  11.1 97.1 %all-gather.8.cloned.1.call-start = ((), (), s32[]{:S(2)}) async-start(), calls=%async_computation.9 | async-start | bytes 3981312 | tf_op jit(solution)/shard_map/all_gather | solution.py:1131
  11.8 135.2 %all-gather.10.cloned.1.call-start = ((), (), s32[]{:S(2)}) async-start(), calls=%async_computation.10 | async-start | bytes 3981312 | tf_op jit(solution)/shard_map/all_gather | solution.py:1131
  14.2 25.3 %collective-permute-start.1 = (bf16[384,768]{1,0:T(8,128)(2,1)S(1)}, bf16[384,768]{1,0:T(8,128)(2,1)S(1)}, u32[]{:S(2)}, u32[]{:S(2)}) collective-permute-start(bf16[384,768]{1,0:T(8,128)(2,1)S(1)} %bitcast.39), channel_id=1, source_target_pairs={{0,16},{1,9},{2,18},{3,11},{4,20},{5,13},{6,22},{7,15},{8,24},{9,1... | collective-permute-start | bytes 1769480 | tf_op jit(solution)/shard_map/ppermute | solution.py:1082
  55.3 132.2 %all-gather.12.cloned.1.call-start = ((), (), s32[]{:S(2)}) async-start(), calls=%async_computation.11 | async-start | bytes 3981312 | tf_op jit(solution)/shard_map/all_gather | solution.py:1131
  60.2 32.3 %collective-permute-start.7 = (bf16[4,2,96,768]{3,2,1,0:T(8,128)(2,1)}, bf16[4,2,96,768]{3,2,1,0:T(8,128)(2,1)S(1)}, u32[]{:S(2)}, u32[]{:S(2)}) collective-permute-start(bf16[4,2,96,768]{3,2,1,0:T(8,128)(2,1)} %half.2.rest_0_), channel_id=1, source_target_pairs={{0,16},{1,9},{2,18},{3,11},{4,20},{5,13},{6,22},{7,15},{8,24},{9,1... | collective-permute-start | bytes 3538952 | tf_op jit(solution)/shard_map/ppermute | solution.py:1082
  61.5 31.1 %collective-permute-start.6 = (bf16[4,2,96,768]{3,2,1,0:T(8,128)(2,1)}, bf16[4,2,96,768]{3,2,1,0:T(8,128)(2,1)S(1)}, u32[]{:S(2)}, u32[]{:S(2)}) collective-permute-start(bf16[4,2,96,768]{3,2,1,0:T(8,128)(2,1)} %half.2.rest_0_), channel_id=1, source_target_pairs={{0,8},{1,17},{2,10},{3,19},{4,12},{5,21},{6,14},{7,23},{8,0},{9,25... | collective-permute-start | bytes 3538952 | tf_op jit(solution)/shard_map/ppermute | solution.py:1082
  108.1 314.3 %reduce-scatter.9.cloned.1.call-start = ((), (), s32[]{:S(2)}) async-start(), calls=%async_computation.13 | async-start | bytes 1474560 | tf_op jit(solution)/shard_map/reduce_scatter | solution.py:1097
  150.9 29.1 %collective-permute-start.17 = (bf16[4,2,96,768]{3,2,1,0:T(8,128)(2,1)}, bf16[4,2,96,768]{3,2,1,0:T(8,128)(2,1)S(1)}, u32[]{:S(2)}, u32[]{:S(2)}) collective-permute-start(bf16[4,2,96,768]{3,2,1,0:T(8,128)(2,1)} %half.3.rest_0_), channel_id=1, source_target_pairs={{0,16},{1,9},{2,18},{3,11},{4,20},{5,13},{6,22},{7,15},{8,24},{9,1... | collective-permute-start | bytes 3538952 | tf_op jit(solution)/shard_map/ppermute | solution.py:1082
  150.9 29.1 %collective-permute-start.16 = (bf16[4,2,96,768]{3,2,1,0:T(8,128)(2,1)}, bf16[4,2,96,768]{3,2,1,0:T(8,128)(2,1)S(1)}, u32[]{:S(2)}, u32[]{:S(2)}) collective-permute-start(bf16[4,2,96,768]{3,2,1,0:T(8,128)(2,1)} %half.3.rest_0_), channel_id=1, source_target_pairs={{0,8},{1,17},{2,10},{3,19},{4,12},{5,21},{6,14},{7,23},{8,0},{9,25... | collective-permute-start | bytes 3538952 | tf_op jit(solution)/shard_map/ppermute | solution.py:1082
  226.6 46.4 %collective-permute-start.23 = (bf16[400,4608]{1,0:T(8,128)(2,1)}, bf16[400,4608]{1,0:T(8,128)(2,1)}, u32[]{:S(2)}, u32[]{:S(2)}) collective-permute-start(bf16[400,4608]{1,0:T(8,128)(2,1)} %get-tuple-element.131.dgg), channel_id=1, source_target_pairs={{0,1},{1,0},{2,3},{3,2},{4,5},{5,4},{6,7},{7,6},{8,9},{9,8},{10,11... | collective-permute-start | bytes 11059208 | tf_op jit(solution)/shard_map/ppermute | solution.py:1082
  285.4 137.9 %reduce-scatter.15.cloned.1.call-start = ((), (), s32[]{:S(2)}) async-start(), calls=%async_computation.16 | async-start | bytes 1576960 | tf_op jit(solution)/shard_map/reduce_scatter | solution.py:1097
  286.4 38.2 %collective-permute-start.24 = (bf16[4,2,96,768]{3,2,1,0:T(8,128)(2,1)}, bf16[4,2,96,768]{3,2,1,0:T(8,128)(2,1)S(1)}, u32[]{:S(2)}, u32[]{:S(2)}) collective-permute-start(bf16[4,2,96,768]{3,2,1,0:T(8,128)(2,1)} %get-tuple-element.133), channel_id=1, source_target_pairs={{0,8},{1,17},{2,10},{3,19},{4,12},{5,21},{6,14},{7,23},{8,0},{9,25... | collective-permute-start | bytes 3538952 | tf_op jit(solution)/shard_map/ppermute | solution.py:1082
  287.1 37.6 %collective-permute-start.25 = (bf16[4,2,96,768]{3,2,1,0:T(8,128)(2,1)}, bf16[4,2,96,768]{3,2,1,0:T(8,128)(2,1)S(1)}, u32[]{:S(2)}, u32[]{:S(2)}) collective-permute-start(bf16[4,2,96,768]{3,2,1,0:T(8,128)(2,1)} %get-tuple-element.134), channel_id=1, source_target_pairs={{0,16},{1,9},{2,18},{3,11},{4,20},{5,13},{6,22},{7,15},{8,24},{9,1... | collective-permute-start | bytes 3538952 | tf_op jit(solution)/shard_map/ppermute | solution.py:1082
  287.4 34.3 %collective-permute-start.21 = (bf16[384,768]{1,0:T(8,128)(2,1)S(1)}, bf16[384,768]{1,0:T(8,128)(2,1)}, u32[]{:S(2)}, u32[]{:S(2)}) collective-permute-start(bf16[384,768]{1,0:T(8,128)(2,1)S(1)} %copy-done.23), channel_id=1, source_target_pairs={{0,16},{1,9},{2,18},{3,11},{4,20},{5,13},{6,22},{7,15},{8,24},{9,1... | collective-permute-start | bytes 1769480 | tf_op jit(solution)/shard_map/ppermute | solution.py:1082
  292.1 148.8 %reduce-scatter.7.cloned.1.call-start = ((), (), s32[]{:S(2)}) async-start(), calls=%async_computation.12 | async-start | bytes 1474560 | tf_op jit(solution)/shard_map/reduce_scatter | solution.py:1097
  292.3 37.2 %collective-permute-start.20 = (bf16[384,768]{1,0:T(8,128)(2,1)}, bf16[384,768]{1,0:T(8,128)(2,1)S(1)}, u32[]{:S(2)}, u32[]{:S(2)}) collective-permute-start(bf16[384,768]{1,0:T(8,128)(2,1)} %get-tuple-element.127), channel_id=1, source_target_pairs={{0,16},{1,9},{2,18},{3,11},{4,20},{5,13},{6,22},{7,15},{8,24},{9,1... | collective-permute-start | bytes 1769480 | tf_op jit(solution)/shard_map/ppermute | solution.py:1082
  352.0 99.0 %reduce-scatter.13.cloned.1.call-start = ((), (), s32[]{:S(2)}) async-start(), calls=%async_computation.15 | async-start | bytes 1474560 | tf_op jit(solution)/shard_map/reduce_scatter | solution.py:1097
  376.0 102.8 %reduce-scatter.11.cloned.1.call-start = ((), (), s32[]{:S(2)}) async-start(), calls=%async_computation.14 | async-start | bytes 1474560 | tf_op jit(solution)/shard_map/reduce_scatter | solution.py:1097
  376.3 32.7 %collective-permute-start.32 = (bf16[4,2,96,768]{3,2,1,0:T(8,128)(2,1)}, bf16[4,2,96,768]{3,2,1,0:T(8,128)(2,1)S(1)}, u32[]{:S(2)}, u32[]{:S(2)}) collective-permute-start(bf16[4,2,96,768]{3,2,1,0:T(8,128)(2,1)} %get-tuple-element.152), channel_id=1, source_target_pairs={{0,8},{1,17},{2,10},{3,19},{4,12},{5,21},{6,14},{7,23},{8,0},{9,25... | collective-permute-start | bytes 3538952 | tf_op jit(solution)/shard_map/ppermute | solution.py:1082
  377.3 31.7 %collective-permute-start.33 = (bf16[4,2,96,768]{3,2,1,0:T(8,128)(2,1)S(1)}, bf16[4,2,96,768]{3,2,1,0:T(8,128)(2,1)S(1)}, u32[]{:S(2)}, u32[]{:S(2)}) collective-permute-start(bf16[4,2,96,768]{3,2,1,0:T(8,128)(2,1)S(1)} %copy-done.56), channel_id=1, source_target_pairs={{0,16},{1,9},{2,18},{3,11},{4,20},{5,13},{6,22},{7,15},{8,24},{9,1... | collective-permute-start | bytes 3538952 | tf_op jit(solution)/shard_map/ppermute | solution.py:1082
  413.8 69.6 %reduce-scatter.17.cloned.1.call-start = ((), (), s32[]{:S(2)}) async-start(), calls=%async_computation.17 | async-start | bytes 1576960 | tf_op jit(solution)/shard_map/reduce_scatter | solution.py:1097
  421.4 22.1 %collective-permute-start.29 = (bf16[384,768]{1,0:T(8,128)(2,1)S(1)}, bf16[384,768]{1,0:T(8,128)(2,1)S(1)}, u32[]{:S(2)}, u32[]{:S(2)}) collective-permute-start(bf16[384,768]{1,0:T(8,128)(2,1)S(1)} %copy-done.27), channel_id=1, source_target_pairs={{0,16},{1,9},{2,18},{3,11},{4,20},{5,13},{6,22},{7,15},{8,24},{9,1... | collective-permute-start | bytes 1769480 | tf_op jit(solution)/shard_map/ppermute | solution.py:1082
  422.3 18.6 %collective-permute-start.30 = (bf16[1,2,96,768]{3,2,1,0:T(8,128)(2,1)}, bf16[1,2,96,768]{3,2,1,0:T(8,128)(2,1)S(1)}, u32[]{:S(2)}, u32[]{:S(2)}) collective-permute-start(bf16[1,2,96,768]{3,2,1,0:T(8,128)(2,1)} %reduce-scatter.9.cloned.1.call-done), channel_id=1, source_target_pairs={{0,24},{1,25},{2,26},{3,27},{4,28},{5,29},{6,30},{7,31},{8,16},{9,... | collective-permute-start | bytes 884744 | tf_op jit(solution)/shard_map/ppermute | solution.py:1082
  423.3 25.3 %collective-permute-start.41 = (bf16[112,1344]{1,0:T(8,128)(2,1)}, bf16[112,1344]{1,0:T(8,128)(2,1)S(1)}, u32[]{:S(2)}, u32[]{:S(2)}) collective-permute-start(bf16[112,1344]{1,0:T(8,128)(2,1)} %bitcast.45), channel_id=1, source_target_pairs={{0,24},{1,25},{2,26},{3,27},{4,28},{5,29},{6,30},{7,31},{8,16},{9,... | collective-permute-start | bytes 903176 | tf_op jit(solution)/shard_map/ppermute | solution.py:1082
  424.7 25.7 %collective-permute-start.40 = (bf16[112,1344]{1,0:T(8,128)(2,1)}, bf16[112,1344]{1,0:T(8,128)(2,1)S(1)}, u32[]{:S(2)}, u32[]{:S(2)}) collective-permute-start(bf16[112,1344]{1,0:T(8,128)(2,1)} %bitcast.46), channel_id=1, source_target_pairs={{0,16},{1,9},{2,18},{3,11},{4,20},{5,13},{6,22},{7,15},{8,24},{9,1... | collective-permute-start | bytes 903176 | tf_op jit(solution)/shard_map/ppermute | solution.py:1082
  425.2 25.8 %collective-permute-start.39 = (bf16[112,1344]{1,0:T(8,128)(2,1)}, bf16[112,1344]{1,0:T(8,128)(2,1)S(1)}, u32[]{:S(2)}, u32[]{:S(2)}) collective-permute-start(bf16[112,1344]{1,0:T(8,128)(2,1)} %bitcast.47), channel_id=1, source_target_pairs={{0,8},{1,17},{2,10},{3,19},{4,12},{5,21},{6,14},{7,23},{8,0},{9,25... | collective-permute-start | bytes 903176 | tf_op jit(solution)/shard_map/ppermute | solution.py:1082
  446.5 26.4 %collective-permute-start.34 = (bf16[384,768]{1,0:T(8,128)(2,1)}, bf16[384,768]{1,0:T(8,128)(2,1)S(1)}, u32[]{:S(2)}, u32[]{:S(2)}) collective-permute-start(bf16[384,768]{1,0:T(8,128)(2,1)} %sums.10), channel_id=1, source_target_pairs={{0,8},{1,17},{2,10},{3,19},{4,12},{5,21},{6,14},{7,23},{8,0},{9,25... | collective-permute-start | bytes 1769480 | tf_op jit(solution)/shard_map/ppermute | solution.py:1082
  450.4 21.8 %collective-permute-start.36 = (bf16[2,96,768]{2,1,0:T(8,128)(2,1)S(1)}, bf16[2,96,768]{2,1,0:T(8,128)(2,1)S(1)}, u32[]{:S(2)}, u32[]{:S(2)}) collective-permute-start(bf16[2,96,768]{2,1,0:T(8,128)(2,1)S(1)} %copy-done.14), channel_id=1, source_target_pairs={{0,8},{1,17},{2,10},{3,19},{4,12},{5,21},{6,14},{7,23},{8,0},{9,25... | collective-permute-start | bytes 884744 | tf_op jit(solution)/shard_map/ppermute | solution.py:1082
  451.0 27.7 %collective-permute-start.35 = (bf16[1,2,96,768]{3,2,1,0:T(8,128)(2,1)}, bf16[1,2,96,768]{3,2,1,0:T(8,128)(2,1)}, u32[]{:S(2)}, u32[]{:S(2)}) collective-permute-start(bf16[1,2,96,768]{3,2,1,0:T(8,128)(2,1)} %reduce-scatter.13.cloned.1.call-done), channel_id=1, source_target_pairs={{0,24},{1,25},{2,26},{3,27},{4,28},{5,29},{6,30},{7,31},{8,16},{9,... | collective-permute-start | bytes 884744 | tf_op jit(solution)/shard_map/ppermute | solution.py:1082
  454.1 30.5 %collective-permute-start.28 = (bf16[384,768]{1,0:T(8,128)(2,1)}, bf16[384,768]{1,0:T(8,128)(2,1)}, u32[]{:S(2)}, u32[]{:S(2)}) collective-permute-start(bf16[384,768]{1,0:T(8,128)(2,1)} %get-tuple-element.145), channel_id=1, source_target_pairs={{0,16},{1,9},{2,18},{3,11},{4,20},{5,13},{6,22},{7,15},{8,24},{9,1... | collective-permute-start | bytes 1769480 | tf_op jit(solution)/shard_map/ppermute | solution.py:1082
  487.5 23.4 %collective-permute-start.45 = (bf16[112,1344]{1,0:T(8,128)(2,1)}, bf16[112,1344]{1,0:T(8,128)(2,1)}, u32[]{:S(2)}, u32[]{:S(2)}) collective-permute-start(bf16[112,1344]{1,0:T(8,128)(2,1)} %bitcast.43), channel_id=1, source_target_pairs={{0,8},{1,17},{2,10},{3,19},{4,12},{5,21},{6,14},{7,23},{8,0},{9,25... | collective-permute-start | bytes 903176 | tf_op jit(solution)/shard_map/ppermute | solution.py:1082
  (86 other events, 637.7 us)
Sparse Core Ops, SparseCore 0:
  11.2 44.0 all-gather.5
  57.5 40.3 all-gather.7
  99.6 42.7 all-gather.9
  143.9 41.4 all-gather.11
  285.5 25.8 reduce-scatter.8
  313.6 29.3 reduce-scatter.14
  352.1 26.0 reduce-scatter.6
  380.6 27.8 reduce-scatter.12
  413.9 26.3 reduce-scatter.10
  442.6 29.2 reduce-scatter.16
